TPU v7x, 128 devices: a whole 4x4x4 slice. The times are simulated.
128 devices in a mesh: morton: 32 (over x_hi, z, y), oct: 4 (over x_lo, core).
Axes of the slice: x: 4 (x_hi: 2, x_lo: 2; x = x_hi * 2 + x_lo), y: 4, z: 4, core: 2. Of those that a mesh axis runs over, the one named last changes fastest.
Arguments:
- state: float32 [5, 512, 128, 128], P(None, 'morton', 'oct'), may hold values from -25 to 200
- fine_pairs: int32 [64, 16, 16, 32], P('morton', 'oct'), may hold values from 0 to 124, as said below
- fine_count: int32 [64, 16, 16], P('morton', 'oct'), may hold values from 1 to 32, as said below
- coarse_pairs: int32 [32, 8, 8, 32], P('morton', 'oct'), may hold values from 0 to 2047, as said below
Outputs:
- new_state: float32 [5, 512, 128, 128], P(None, 'morton', 'oct')
- gravity: float32 [3, 512, 128, 128], P(None, 'morton', 'oct')
Inputs may be any that keep to these rules, and one draw needn't show every extreme that they name: `fine_pairs`: each entry codes an offset (ox, oy, oz), each of -2 to 2, as (ox + 2) * 25 + (oy + 2) * 5 + oz + 2, and the largest of |ox|, |oy|, |oz| is 2. Entries of a row of fine_pairs at or past fine_count are not used. `coarse_pairs`: each entry is a parent's index (px * 8 + py) * 8 + pz; its pz differs from that of the row's own parent by 2 or more.
All inputs are finite; a program needn't handle non-finite values.
Results may differ from a plain program's by a relative error of at most 0.0001.
Values sent between devices are 32-bit elements; how exact they have to be, the bound alone decides.
No kernel may reach another device: no remote copies, remote signals or barrier semaphores. Data moves between devices by JAX's collectives and lax.ppermute only.
A program may use at most 64 MiB of HBM per device.

v0:
```python
import jax
import jax.numpy as jnp
from jax import lax
from jax.sharding import PartitionSpec as P

ADIABATIC = 5.0 / 3.0
COURANT = 0.2
GRAVITY = 1.0


def with_halo(array, sides, width):
    for axis, dim in sides:
        devices, length = (lax.axis_size(axis), array.shape[dim])
        up = [(i, (i + 1) % devices) for i in range(devices - 1)]
        down = [(j, i) for i, j in up]
        last = lax.slice_in_dim(array, length - width, length, axis=dim)
        initial = lax.slice_in_dim(array, 0, width, axis=dim)
        before = lax.ppermute(last, axis, up)
        after = lax.ppermute(initial, axis, down)
        array = jnp.concatenate([before, array, after], axis=dim)
    return array


def window(values, offset, extent, dimension):
    return lax.slice_in_dim(values, offset, offset + extent, axis=dimension)


def pressure_of(fields):
    kinetic = (
        0.5 * (fields[1] * fields[1] + fields[2] * fields[2] + fields[3] * fields[3]) / fields[0]
    )
    return (ADIABATIC - 1.0) * (fields[4] - kinetic)


def wave_speed(fields, direction):
    sound_speed = jnp.sqrt(ADIABATIC * pressure_of(fields) / fields[0])
    return jnp.abs(fields[1 + direction] / fields[0]) + sound_speed


def euler_flux(fields, direction):
    velocity = fields[1 + direction] / fields[0]
    pressure = pressure_of(fields)
    momenta = []
    for component in range(3):
        carried = fields[1 + component] * velocity
        if component == direction:
            carried = carried + pressure
        momenta.append(carried)
    return jnp.stack([fields[1 + direction]] + momenta + [(fields[4] + pressure) * velocity])


def flux_difference(padded, speeds, direction):
    dimension = direction + 1
    length = padded.shape[dimension] - 6
    left_far = window(padded, 0, length + 3, dimension)
    left_near = window(padded, 1, length + 3, dimension)
    right_near = window(padded, 2, length + 3, dimension)
    right_far = window(padded, 3, length + 3, dimension)
    face_value = 7.0 / 12.0 * (left_near + right_near) - 1.0 / 12.0 * (left_far + right_far)
    face_value = jnp.minimum(
        jnp.maximum(face_value, jnp.minimum(left_near, right_near)),
        jnp.maximum(left_near, right_near),
    )
    centre = window(padded, 2, length + 2, dimension)
    upper_jump = window(face_value, 1, length + 2, dimension) - centre
    lower_jump = window(face_value, 0, length + 2, dimension) - centre
    upper_state = centre + jnp.minimum(
        jnp.maximum(upper_jump, -2.0 * jnp.abs(lower_jump)), 2.0 * jnp.abs(lower_jump)
    )
    lower_state = centre + jnp.minimum(
        jnp.maximum(lower_jump, -2.0 * jnp.abs(upper_jump)), 2.0 * jnp.abs(upper_jump)
    )
    from_left = window(upper_state, 0, length + 1, dimension)
    from_right = window(lower_state, 1, length + 1, dimension)
    face_speed = jnp.maximum(
        window(speeds, 2, length + 1, direction), window(speeds, 3, length + 1, direction)
    )
    flux = 0.5 * (
        euler_flux(from_left, direction) + euler_flux(from_right, direction)
    ) - 0.5 * face_speed * (from_right - from_left)
    return window(flux, 1, length, dimension) - window(flux, 0, length, dimension)


def cell_offsets(count_cells, factor):
    return (jnp.arange(count_cells, dtype=jnp.int32) % factor).astype(jnp.float32) - 0.5 * (
        factor - 1
    )


def subgrid_moments(density):
    count_x, count_y, count_z = density.shape
    weighted = jnp.stack(
        [
            density,
            density * cell_offsets(count_x, 8)[:, None, None],
            density * cell_offsets(count_y, 8)[None, :, None],
            density * cell_offsets(count_z, 8)[None, None, :],
        ]
    )
    folded = weighted.reshape(4, count_x // 8, 8, count_y, count_z).sum(axis=2)
    folded = folded.reshape(4, count_x // 8, count_y // 8, 8, count_z).sum(axis=3)
    selector = (
        jnp.arange(count_z, dtype=jnp.int32)[:, None] // 8
        == jnp.arange(count_z // 8, dtype=jnp.int32)[None, :]
    ).astype(jnp.float32)
    return jnp.dot(folded, selector, precision=lax.Precision.HIGHEST)


def parent_moments(moments):
    groups_x = moments.shape[1] // 2
    groups_y = moments.shape[2] // 2
    groups_z = moments.shape[3] // 2
    grouped = moments.reshape(4, groups_x, 2, groups_y, 2, groups_z, 2)
    child_side = jnp.array([-4.0, 4.0], jnp.float32)
    source_mass = grouped[0]
    pieces = [
        source_mass,
        grouped[1] + source_mass * child_side.reshape(1, 2, 1, 1, 1, 1),
        grouped[2] + source_mass * child_side.reshape(1, 1, 1, 2, 1, 1),
        grouped[3] + source_mass * child_side.reshape(1, 1, 1, 1, 1, 2),
    ]
    return jnp.stack([piece_sum.sum(axis=(1, 3, 5)) for piece_sum in pieces])


def far_field(sources, separation, weight):
    distance_sq = (
        separation[0] * separation[0]
        + separation[1] * separation[1]
        + separation[2] * separation[2]
    )
    inverse_cube = 1.0 / (distance_sq * jnp.sqrt(distance_sq))
    inverse_fifth = inverse_cube / distance_sq
    source_mass = sources[0] * weight
    acceleration = []
    tidal_terms = []
    for row_index in range(3):
        summed = source_mass * separation[row_index] * inverse_cube
        for col_index in range(3):
            jacobian = 3.0 * separation[row_index] * separation[col_index] * inverse_fifth
            if row_index == col_index:
                jacobian = jacobian - inverse_cube
            summed = summed - jacobian * (sources[1 + col_index] * weight)
            tidal_terms.append(jnp.sum(source_mass * jacobian, axis=-1))
        acceleration.append(jnp.sum(summed, axis=-1))
    return (GRAVITY * jnp.stack(acceleration), GRAVITY * jnp.stack(tidal_terms))


def spread(values, factor):
    return jnp.repeat(
        jnp.repeat(jnp.repeat(values, factor, axis=1), factor, axis=2), factor, axis=3
    )


def level_field(acceleration, tidal_terms, factor):
    full_accel = spread(acceleration, factor)
    full_tidal = spread(tidal_terms, factor)
    count_x, count_y, count_z = full_accel.shape[1:]
    offsets = [
        cell_offsets(count_x, factor)[:, None, None],
        cell_offsets(count_y, factor)[None, :, None],
        cell_offsets(count_z, factor)[None, None, :],
    ]
    components = []
    for row_index in range(3):
        summed = full_accel[row_index]
        for col_index in range(3):
            summed = summed + full_tidal[3 * row_index + col_index] * offsets[col_index]
        components.append(summed)
    return jnp.stack(components)


def advance(fields, divergence, gravity, time_step):
    updated = fields - time_step * divergence
    momentum_gain = time_step * fields[0] * gravity
    energy_gain = time_step * (
        fields[1] * gravity[0] + fields[2] * gravity[1] + fields[3] * gravity[2]
    )
    return jnp.concatenate(
        [updated[0:1], updated[1:4] + momentum_gain, (updated[4] + energy_gain)[None]]
    )


def outflow(extended, interior, dimension, position, devices):
    length = interior.shape[dimension]
    lower_rim = window(extended, 0, 3, dimension)
    middle = window(extended, 3, length, dimension)
    upper_rim = window(extended, length + 3, 3, dimension)
    lower_rim = jnp.where(
        position == 0, jnp.repeat(window(interior, 0, 1, dimension), 3, axis=dimension), lower_rim
    )
    upper_rim = jnp.where(
        position == devices - 1,
        jnp.repeat(window(interior, length - 1, 1, dimension), 3, axis=dimension),
        upper_rim,
    )
    return jnp.concatenate([lower_rim, middle, upper_rim], axis=dimension)


def local(state, fine_pairs, fine_count, coarse_pairs):
    morton_place = lax.axis_index("morton")
    oct_place = lax.axis_index("oct")
    morton_devices = lax.axis_size("morton")
    oct_devices = lax.axis_size("oct")
    extended = with_halo(state, (("morton", 1), ("oct", 2)), 3)
    rows_x = outflow(extended[:, :, 3:-3, :], state, 1, morton_place, morton_devices)
    rows_y = outflow(extended[:, 3:-3, :, :], state, 2, oct_place, oct_devices)
    rows_z = jnp.pad(state, ((0, 0), (0, 0), (0, 0), (3, 3)), mode="edge")
    fastest = jnp.maximum(
        jnp.maximum(wave_speed(state, 0), wave_speed(state, 1)), wave_speed(state, 2)
    )
    time_step = COURANT / lax.pmax(jnp.max(fastest), ("morton", "oct"))
    moments = subgrid_moments(state[0])
    near_moments = with_halo(moments, (("morton", 1), ("oct", 2)), 2)
    near_moments = jnp.pad(near_moments, ((0, 0), (0, 0), (0, 0), (2, 2)))
    local_x, local_y, local_z = moments.shape[1:]
    offset_x = fine_pairs // 25 - 2
    offset_y = fine_pairs // 5 % 5 - 2
    offset_z = fine_pairs % 5 - 2
    index_x = jnp.arange(local_x, dtype=jnp.int32)[:, None, None, None] + 2 + offset_x
    index_y = jnp.arange(local_y, dtype=jnp.int32)[None, :, None, None] + 2 + offset_y
    index_z = jnp.arange(local_z, dtype=jnp.int32)[None, None, :, None] + 2 + offset_z
    sources = near_moments[:, index_x, index_y, index_z]
    pair_slots = fine_pairs.shape[3]
    in_use = (
        jnp.arange(pair_slots, dtype=jnp.int32)[None, None, None, :] < fine_count[:, :, :, None]
    ).astype(jnp.float32)
    separation = 8.0 * jnp.stack([offset_x, offset_y, offset_z]).astype(jnp.float32)
    fine_accel, fine_tidal = far_field(sources, separation, in_use)
    parents = parent_moments(moments)
    parent_x, parent_y, parent_z = parents.shape[1:]
    per_device = parent_x * parent_y * parent_z
    flat_local = parents.reshape(4, per_device)
    total_y = parent_y * oct_devices
    source_x = coarse_pairs // (total_y * parent_z)
    source_y = coarse_pairs // parent_z % total_y
    source_z = coarse_pairs % parent_z
    holder = source_x // parent_x * oct_devices + source_y // parent_y
    location = (
        holder * per_device
        + (source_x % parent_x * parent_y + source_y % parent_y) * parent_z
        + source_z
    )
    everything = lax.all_gather(flat_local, ("morton", "oct"), axis=1, tiled=True)
    far_sources = everything[:, location]
    target_x = morton_place * parent_x + jnp.arange(parent_x, dtype=jnp.int32)[:, None, None, None]
    target_y = oct_place * parent_y + jnp.arange(parent_y, dtype=jnp.int32)[None, :, None, None]
    target_z = jnp.arange(parent_z, dtype=jnp.int32)[None, None, :, None]
    far_separation = 16.0 * jnp.stack(
        [source_x - target_x, source_y - target_y, source_z - target_z]
    ).astype(jnp.float32)
    coarse_accel, coarse_tidal = far_field(far_sources, far_separation, 1.0)
    divergence = flux_difference(rows_x, wave_speed(rows_x, 0), 0)
    divergence = divergence + flux_difference(rows_y, wave_speed(rows_y, 1), 1)
    divergence = divergence + flux_difference(rows_z, wave_speed(rows_z, 2), 2)
    gravity = level_field(fine_accel, fine_tidal, 8)
    gravity = gravity + level_field(coarse_accel, coarse_tidal, 16)
    return (advance(state, divergence, gravity, time_step), gravity)


def solution(mesh):
    in_specs = (
        P(None, "morton", "oct", None),
        P("morton", "oct", None, None),
        P("morton", "oct", None),
        P("morton", "oct", None, None),
    )
    out_specs = (P(None, "morton", "oct", None), P(None, "morton", "oct", None))
    return jax.shard_map(local, mesh=mesh, in_specs=in_specs, out_specs=out_specs, check_vma=False)
```

profile of v0, /device:TPU:1, one launch (start us, length us, event | category | flops | bytes accessed | tf_op | source)
XLA Modules:
  0.0 435.7 jit_solution(4193316628449988545)
XLA Ops:
  0.7 2.1 fusion.70
  2.8 68.7 %pmax.7 = f32[]{:T(128)} all-reduce(f32[]{:T(128)} %fusion.70), channel_id=1, replica_groups=mesh['morton'=32,'oct'=4] {'morton','oct'}, use_global_device_ids=true, to_apply=%region_1.2 | all-reduce | flops 1 | bytes 8 | tf_op jit(solution)/shard_map/pmax | solution.py:211
  72.2 1.7 fusion.161
  74.6 1.3 copy.402
  76.0 1.3 copy.401
  77.3 3.0 maximum_reduce_fusion
  80.3 1.2 copy.405
  81.7 1.3 collective-permute-start.5
  83.0 4.6 %collective-permute-start.4 = (f32[4,2,4,16]{3,2,1,0:T(4,128)S(1)}, f32[4,2,4,16]{3,2,1,0:T(4,128)}, u32[]{:S(2)}, u32[]{:S(2)}) collective-permute-start(f32[4,2,4,16]{3,2,1,0:T(4,128)S(1)} %fusion.132), channel_id=1, source_target_pairs={{0,4},{4,8},{8,12},{12,16},{16,20},{20,24},{24,28},{28,32},{32,36}... | collective-permute-start | bytes 6152 | tf_op jit(solution)/shard_map/ppermute | solution.py:18
  87.6 0.8 fusion.163
  88.4 1.3 collective-permute-start.1
  89.7 4.7 %collective-permute-start = (f32[5,3,32,128]{3,2,1,0:T(8,128)}, f32[5,3,32,128]{3,2,1,0:T(8,128)}, u32[]{:S(2)}, u32[]{:S(2)}) collective-permute-start(f32[5,3,32,128]{3,2,1,0:T(8,128)} %get-tuple-element.88), channel_id=1, source_target_pairs={{0,4},{4,8},{8,12},{12,16},{16,20},{20,24},{24,28},{28,32},{32,36}... | collective-permute-start | bytes 737288 | tf_op jit(solution)/shard_map/ppermute | solution.py:18
  94.4 1.5 fusion.164
  95.9 1.8 copy.464
  99.1 1.2 pad_maximum_fusion
  100.3 2.1 fusion.5
  107.4 1.6 minimum_add_fusion
  110.5 0.7 add_dynamic-update-slice_fusion
  111.4 1.3 copy-done.5
  112.8 1.1 add_dynamic-update-slice_fusion.1
  114.0 1.6 copy-done.6
  117.2 181.3 %all-gather = f32[128,16,4]{1,2,0:T(4,128)} all-gather(f32[1,16,4]{1,2,0:T(4,128)S(1)} %maximum_bitcast_fusion), channel_id=1, replica_groups=mesh['morton'=32,'oct'=4] {'morton','oct'}, dimensions={0}, use_global_device_ids=true | all-gather | bytes 33024 | tf_op jit(solution)/shard_map/all_gather | solution.py:243
  298.5 2.7 copy.432
  301.4 2.9 gather_fusion.1
  304.3 1.1 copy.433
  305.4 1.2 multiply_reduce_fusion.17
  308.8 0.7 copy.438
  311.7 0.7 copy.436
  314.5 1.4 multiply_reduce_fusion.14
  316.6 0.7 copy.446
  317.5 0.8 copy.444
  318.5 0.8 copy.442
  324.2 0.7 copy.454
  329.8 0.8 copy.450
  332.7 2.8 multiply_dynamic-update-slice_fusion
  335.6 6.3 %fusion.1 = f32[5,16,32,129]{3,2,1,0:T(8,128)} fusion(f32[5,16,32,130]{3,2,1,0:T(8,128)} %copy-done.3, f32[5,16,32,130]{3,2,1,0:T(8,128)S(1)} %copy-done.2, f32[5,16,32,129]{3,2,1,0:T(8,128)} %get-tuple-element.120, f32[5,16,32,129]{3,2,1,0:T(8,128)} %get-tuple-element.119, f32[16,32,129]{2,1,0:T(8,128)S(1)} %fusion.22), kind=kLoop, calls=%fused_computation.5 | loop fusion | flops 1651200 | bytes 6868992 | tf_op jit(solution)/shard_map/sub | solution.py:78
  342.0 1.1 multiply_add_fusion.2
  343.3 0.8 pad_maximum_fusion.5
  344.1 2.1 collective-permute-start.7
  346.2 3.5 collective-permute-start.6
  349.8 0.8 collective-permute-done.6
  350.6 0.8 pad_maximum_fusion.4
  351.8 43.0 %gather_fusion = f32[4096,4]{1,0:T(8,128)} fusion(f32[4,6,8,20]{0,2,3,1:T(8,128)S(1)} %pad.4.clone, s32[4096]{0:T(1024)S(1)} %reshape.1652), kind=kCustom, calls=%fused_computation | custom fusion | bytes 180224 | tf_op jit(solution)/shard_map/gather | solution.py:222
  394.7 2.6 copy.407
  397.3 0.8 subtract_reduce_fusion.2
  398.2 0.9 multiply_reduce_fusion.7
  401.7 1.0 copy.423
  403.7 1.0 copy.421
  405.6 1.0 copy.419
  407.6 1.0 copy.418
  408.9 1.0 copy.431
  410.2 1.0 copy.429
  411.5 1.0 copy.427
  412.8 1.0 copy.426
  413.8 1.9 multiply_add_fusion.5
  415.8 1.0 broadcast_select_fusion.1
  416.9 1.0 broadcast_select_fusion
  419.0 1.9 collective-permute-start.3
  420.9 4.5 %collective-permute-start.2 = (f32[5,22,3,128]{3,1,2,0:T(8,128)S(1)}, f32[5,22,3,128]{3,1,2,0:T(8,128)S(1)}, u32[]{:S(2)}, u32[]{:S(2)}) collective-permute-start(f32[5,22,3,128]{3,1,2,0:T(8,128)S(1)} %copy.459), channel_id=1, source_target_pairs={{0,1},{1,2},{2,3},{4,5},{5,6},{6,7},{8,9},{9,10},{10,11},{12,13},{... | collective-permute-start | bytes 506888 | tf_op jit(solution)/shard_map/ppermute | solution.py:18
  426.9 0.7 fusion.17
  428.1 0.8 fusion.11
  429.2 1.0 minimum_add_fusion.2
  431.6 1.2 copy-done.4
  434.5 1.2 pad_maximum_fusion.3
  (283 shorter events, 43.5 us)
Async XLA Ops:
  0.6 73.6 %copy-start.27 = (f32[16]{0:T(128)}, f32[16]{0:T(128)S(1)}, u32[]{:S(2)}) copy-start(f32[16]{0:T(128)S(1)} %fusion.144) | copy-start | bytes 196
  0.7 73.6 %copy-start.29 = (f32[32]{0:T(128)}, f32[32]{0:T(128)S(1)}, u32[]{:S(2)}) copy-start(f32[32]{0:T(128)S(1)} %fusion.146) | copy-start | bytes 388
  0.7 73.6 %copy-start.31 = (f32[128]{0:T(128)}, f32[128]{0:T(128)S(1)}, u32[]{:S(2)}) copy-start(f32[128]{0:T(128)S(1)} %fusion.148) | copy-start | bytes 1540
  77.3 10.3 %copy-start = (f32[5,16,32,128]{3,2,1,0:T(8,128)S(1)}, f32[5,16,32,128]{3,2,1,0:T(8,128)}, u32[]{:S(2)}) copy-start(f32[5,16,32,128]{3,2,1,0:T(8,128)} %param.5) | copy-start | bytes 3932164
  81.7 261.6 %collective-permute-start.5 = (f32[4,2,4,16]{3,2,1,0:T(4,128)S(1)}, f32[4,2,4,16]{3,2,1,0:T(4,128)}, u32[]{:S(2)}, u32[]{:S(2)}) collective-permute-start(f32[4,2,4,16]{3,2,1,0:T(4,128)S(1)} %fusion.132), channel_id=1, source_target_pairs={{4,0},{8,4},{12,8},{16,12},{20,16},{24,20},{28,24},{32,28},{36,32}... | collective-permute-start | bytes 6152 | tf_op jit(solution)/shard_map/ppermute | solution.py:19
  83.0 260.3 %collective-permute-start.4 = (f32[4,2,4,16]{3,2,1,0:T(4,128)S(1)}, f32[4,2,4,16]{3,2,1,0:T(4,128)}, u32[]{:S(2)}, u32[]{:S(2)}) collective-permute-start(f32[4,2,4,16]{3,2,1,0:T(4,128)S(1)} %fusion.132), channel_id=1, source_target_pairs={{0,4},{4,8},{8,12},{12,16},{16,20},{20,24},{24,28},{28,32},{32,36}... | collective-permute-start | bytes 6152 | tf_op jit(solution)/shard_map/ppermute | solution.py:18
  88.4 328.5 %collective-permute-start.1 = (f32[5,3,32,128]{3,2,1,0:T(8,128)}, f32[5,3,32,128]{3,2,1,0:T(8,128)}, u32[]{:S(2)}, u32[]{:S(2)}) collective-permute-start(f32[5,3,32,128]{3,2,1,0:T(8,128)} %get-tuple-element.87), channel_id=1, source_target_pairs={{4,0},{8,4},{12,8},{16,12},{20,16},{24,20},{28,24},{32,28},{36,32}... | collective-permute-start | bytes 737288 | tf_op jit(solution)/shard_map/ppermute | solution.py:19
  89.7 326.1 %collective-permute-start = (f32[5,3,32,128]{3,2,1,0:T(8,128)}, f32[5,3,32,128]{3,2,1,0:T(8,128)}, u32[]{:S(2)}, u32[]{:S(2)}) collective-permute-start(f32[5,3,32,128]{3,2,1,0:T(8,128)} %get-tuple-element.88), channel_id=1, source_target_pairs={{0,4},{4,8},{8,12},{12,16},{16,20},{20,24},{24,28},{28,32},{32,36}... | collective-permute-start | bytes 737288 | tf_op jit(solution)/shard_map/ppermute | solution.py:18
  109.0 1.5 copy-start.1
  109.0 3.8 copy-start.3
  111.2 1.5 copy-start.5
  112.8 3.0 copy-start.33
  114.0 1.6 copy-start.6
  115.5 185.7 %copy-start.26 = (s32[1,2,8,32]{3,2,1,0:T(8,128)S(1)}, s32[1,2,8,32]{3,2,1,0:T(8,128)}, u32[]{:S(2)}) copy-start(s32[1,2,8,32]{3,2,1,0:T(8,128)} %param.8) | copy-start | bytes 6148
  332.7 2.8 copy-start.2
  335.4 6.4 %copy-start.16 = (f32[32,128]{1,0:T(8,128)S(1)}, f32[32,128]{1,0:T(8,128)}, u32[]{:S(2)}) copy-start(f32[32,128]{1,0:T(8,128)} %copy.441) | copy-start | bytes 49156
  335.4 6.4 %copy-start.17 = (f32[32,128]{1,0:T(8,128)S(1)}, f32[32,128]{1,0:T(8,128)}, u32[]{:S(2)}) copy-start(f32[32,128]{1,0:T(8,128)} %copy.439) | copy-start | bytes 49156
  335.4 6.4 %copy-start.18 = (f32[32,128]{1,0:T(8,128)S(1)}, f32[32,128]{1,0:T(8,128)}, u32[]{:S(2)}) copy-start(f32[32,128]{1,0:T(8,128)} %copy.437) | copy-start | bytes 49156
  335.5 6.4 %copy-start.19 = (f32[32,128]{1,0:T(8,128)S(1)}, f32[32,128]{1,0:T(8,128)}, u32[]{:S(2)}) copy-start(f32[32,128]{1,0:T(8,128)} %copy.443) | copy-start | bytes 49156
  335.5 6.4 %copy-start.20 = (f32[32,128]{1,0:T(8,128)S(1)}, f32[32,128]{1,0:T(8,128)}, u32[]{:S(2)}) copy-start(f32[32,128]{1,0:T(8,128)} %copy.457) | copy-start | bytes 49156
  335.5 6.4 %copy-start.21 = (f32[32,128]{1,0:T(8,128)S(1)}, f32[32,128]{1,0:T(8,128)}, u32[]{:S(2)}) copy-start(f32[32,128]{1,0:T(8,128)} %copy.455) | copy-start | bytes 49156
  335.5 6.4 %copy-start.22 = (f32[32,128]{1,0:T(8,128)S(1)}, f32[32,128]{1,0:T(8,128)}, u32[]{:S(2)}) copy-start(f32[32,128]{1,0:T(8,128)} %copy.453) | copy-start | bytes 49156
  335.5 6.4 %copy-start.23 = (f32[32,128]{1,0:T(8,128)S(1)}, f32[32,128]{1,0:T(8,128)}, u32[]{:S(2)}) copy-start(f32[32,128]{1,0:T(8,128)} %copy.451) | copy-start | bytes 49156
  335.5 6.4 %copy-start.37 = (f32[128]{0:T(128)S(1)}, f32[128]{0:T(128)}, u32[]{:S(2)}) copy-start(f32[128]{0:T(128)} %fusion.154) | copy-start | bytes 1540
  335.5 6.4 %copy-start.38 = (f32[32]{0:T(128)S(1)}, f32[32]{0:T(128)}, u32[]{:S(2)}) copy-start(f32[32]{0:T(128)} %fusion.152) | copy-start | bytes 388
  335.5 6.4 %copy-start.39 = (f32[16]{0:T(128)S(1)}, f32[16]{0:T(128)}, u32[]{:S(2)}) copy-start(f32[16]{0:T(128)} %fusion.150) | copy-start | bytes 196
  335.5 7.5 %copy-start.24 = (s32[2,4,16,32]{3,2,1,0:T(8,128)S(1)}, s32[2,4,16,32]{3,2,1,0:T(8,128)}, u32[]{:S(2)}) copy-start(s32[2,4,16,32]{3,2,1,0:T(8,128)} %param.6) | copy-start | bytes 49156
  335.5 7.5 %copy-start.34 = (s32[16]{0:T(128)S(1)}, s32[16]{0:T(128)}, u32[]{:S(2)}) copy-start(s32[16]{0:T(128)} %iota_add_fusion.1) | copy-start | bytes 196
  335.6 7.5 %copy-start.35 = (s32[4]{0:T(128)S(1)}, s32[4]{0:T(128)}, u32[]{:S(2)}) copy-start(s32[4]{0:T(128)} %iota_add_fusion.2) | copy-start | bytes 52
  335.6 7.5 %copy-start.36 = (s32[2]{0:T(128)S(1)}, s32[2]{0:T(128)}, u32[]{:S(2)}) copy-start(s32[2]{0:T(128)} %iota_add_fusion.3) | copy-start | bytes 28
  344.1 5.7 %collective-permute-start.7 = (f32[4,6,2,16]{3,2,1,0:T(2,128)S(1)}, f32[4,6,2,16]{3,2,1,0:T(2,128)S(1)}, u32[]{:S(2)}, u32[]{:S(2)}) collective-permute-start(f32[4,6,2,16]{3,2,1,0:T(2,128)S(1)} %get-tuple-element.108), channel_id=1, source_target_pairs={{1,0},{2,1},{3,2},{5,4},{6,5},{7,6},{9,8},{10,9},{11,10},{13,12},{... | collective-permute-start | bytes 9224 | tf_op jit(solution)/shard_map/ppermute | solution.py:19
  346.2 4.4 %collective-permute-start.6 = (f32[4,6,2,16]{3,2,1,0:T(2,128)S(1)}, f32[4,6,2,16]{3,2,1,0:T(2,128)S(1)}, u32[]{:S(2)}, u32[]{:S(2)}) collective-permute-start(f32[4,6,2,16]{3,2,1,0:T(2,128)S(1)} %get-tuple-element.107), channel_id=1, source_target_pairs={{0,1},{1,2},{2,3},{4,5},{5,6},{6,7},{8,9},{9,10},{10,11},{12,13},{... | collective-permute-start | bytes 9224 | tf_op jit(solution)/shard_map/ppermute | solution.py:18
  394.7 2.6 copy-start.25
  412.5 1.3 copy-start.28
  412.5 1.3 copy-start.30
  412.5 1.3 copy-start.32
  413.8 2.0 copy-start.13
  415.8 1.1 copy-start.12
  419.0 8.6 %collective-permute-start.3 = (f32[5,22,3,128]{3,1,2,0:T(8,128)S(1)}, f32[5,22,3,128]{3,1,2,0:T(8,128)S(1)}, u32[]{:S(2)}, u32[]{:S(2)}) collective-permute-start(f32[5,22,3,128]{3,1,2,0:T(8,128)S(1)} %copy.461), channel_id=1, source_target_pairs={{1,0},{2,1},{3,2},{5,4},{6,5},{7,6},{9,8},{10,9},{11,10},{13,12},{... | collective-permute-start | bytes 506888 | tf_op jit(solution)/shard_map/ppermute | solution.py:19
  420.9 6.8 %collective-permute-start.2 = (f32[5,22,3,128]{3,1,2,0:T(8,128)S(1)}, f32[5,22,3,128]{3,1,2,0:T(8,128)S(1)}, u32[]{:S(2)}, u32[]{:S(2)}) collective-permute-start(f32[5,22,3,128]{3,1,2,0:T(8,128)S(1)} %copy.459), channel_id=1, source_target_pairs={{0,1},{1,2},{2,3},{4,5},{5,6},{6,7},{8,9},{9,10},{10,11},{12,13},{... | collective-permute-start | bytes 506888 | tf_op jit(solution)/shard_map/ppermute | solution.py:18
  426.9 0.8 copy-start.15
  426.9 0.9 copy-start.14
  431.1 1.7 copy-start.4
  432.8 0.9 copy-start.8
  432.8 1.0 copy-start.9
  432.8 1.1 copy-start.10
  432.8 1.2 copy-start.11
  434.3 1.4 copy-start.7
where the time goes:
time: 437 us; the launch traced here: 436 us
  blocking collectives  250 us (57%)
  local copies, waits for them, and re-layouts  110 us (25%)
  other arithmetic  48.3 us (11%)
  starting transfers between devices  23.8 us (5%)
    all_gather x1, blocking collectives, local(): lax.all_gather(flat_local, ('morton', 'oct'), axis=1, tiled=True)  181 us
    pmax x1, blocking collectives, local(): time_step = COURANT / lax.pmax(jnp.max(fastest), ('morton', 'oct'))  68.7 us
    gather x2, local copies, waits for them, and re-layouts, local(): sources = near_moments[:, index_x, index_y, index_z]  45.5 us
    broadcast_in_dim x48, local copies, waits for them, and re-layouts, spread(): jnp.repeat(jnp.repeat(jnp.repeat(values, factor, axis=1), factor, axis=2)...  21.8 us
    ppermute x4, starting transfers between devices, with_halo(): before = lax.ppermute(last, axis, up)  17.2 us
  transfers between devices with their start and end apart: 8, of which 1 were waited for; matrix products, arithmetic and copies ran while one was open for 31% of the time, Pallas kernels for 0%

commit v1 on v0

v1 whole, which is shorter than its diff:
```python
import functools

import jax
import jax.numpy as jnp
from jax import lax
from jax.experimental import pallas as pl
from jax.experimental.pallas import tpu as pltpu
from jax.sharding import PartitionSpec as P

ADIABATIC = 5.0 / 3.0
COURANT = 0.2
GRAVITY = 1.0
AXES = ("morton", "oct")
F32 = jnp.float32
HIGH = lax.Precision.HIGHEST

NX, NY, NZ = 16, 32, 128
ROWS = NX * NY
SENT = 5
SYM = ((0, 0), (0, 1), (0, 2), (1, 1), (1, 2), (2, 2))


def iota(shape, dim):
    return lax.broadcasted_iota(jnp.int32, shape, dim)


def sym(i, j):
    return SYM.index((min(i, j), max(i, j)))


def reciprocal(x):
    guess = pl.reciprocal(x, approx=True)
    return guess * (2.0 - x * guess)


def sound_of(q, inverse):
    kinetic = (q[1] * q[1] + q[2] * q[2] + q[3] * q[3]) * inverse
    pressure = (2.0 / 3.0) * q[4] - (1.0 / 3.0) * kinetic
    return jnp.sqrt(ADIABATIC * pressure * inverse)


def fold_rows(values, group):
    keep = iota(values.shape, 1) // group == iota(values.shape, 0)
    return jnp.sum(jnp.where(keep, values, 0.0), axis=0, keepdims=True)


def prepare_kernel(place, state, sent, x_one, x_two, y_one, y_two):
    morton_odd = place[0] % 2
    oct_odd = place[1] % 2
    x_starts = (jnp.where(morton_odd == 0, NX - 3, 0), jnp.where(morton_odd == 0, 0, NX - 3))
    y_starts = (jnp.where(oct_odd == 0, NY - 3, 0), jnp.where(oct_odd == 0, 0, NY - 3))
    for field in range(5):
        for out, start in ((x_one, x_starts[0]), (x_two, x_starts[1])):
            out[field * 96 : field * 96 + 96, :] = state[
                pl.ds(pl.multiple_of(field * ROWS + start * NY, 32), 96), :
            ]
        for out, start in ((y_one, y_starts[0]), (y_two, y_starts[1])):
            for layer in range(3):
                row = (field * 3 + layer) * 16
                out[row : row + 16, :] = state[pl.ds(field * ROWS + start + layer, 16, stride=NY), :]

    offset_y = iota((8, 128), 0).astype(F32) - 3.5
    fastest = jnp.zeros((8, 128), F32)
    sums, sums_x, sums_y = [], [], []
    for tx in range(2):
        for ty in range(4):
            total = total_x = None
            for x in range(8):
                row = (tx * 8 + x) * NY + ty * 8
                q = [state[f * ROWS + row : f * ROWS + row + 8, :] for f in range(5)]
                inverse = reciprocal(q[0])
                largest = jnp.maximum(jnp.maximum(jnp.abs(q[1]), jnp.abs(q[2])), jnp.abs(q[3]))
                fastest = jnp.maximum(fastest, largest * inverse + sound_of(q, inverse))
                weighted = q[0] * (x - 3.5)
                total = q[0] if total is None else total + q[0]
                total_x = weighted if total_x is None else total_x + weighted
            sums.append(jnp.sum(total, axis=0, keepdims=True))
            sums_x.append(jnp.sum(total_x, axis=0, keepdims=True))
            sums_y.append(jnp.sum(total * offset_y, axis=0, keepdims=True))
    rows = jnp.concatenate(sums + sums_x + sums_y, axis=0)
    z = iota((128, 128), 0)
    pick = (z // 8 == iota((128, 128), 1) % 16).astype(F32)
    by_z = pick * ((z % 8).astype(F32) - 3.5)
    folded = jnp.dot(rows, pick, precision=HIGH, preferred_element_type=F32)
    folded_z = jnp.dot(rows[0:8], by_z, precision=HIGH, preferred_element_type=F32)
    mass = fold_rows(folded[0:8], 16)
    dipole = [fold_rows(folded[8:16], 16), fold_rows(folded[16:24], 16), fold_rows(folded_z, 16)]

    lane = iota((1, 128), 1)
    odd = [lane // 64, lane // 16 % 2, lane % 2]
    shifted = [d + 4.0 * (2 * o - 1).astype(F32) * mass for d, o in zip(dipole, odd, strict=True)]
    t = iota((128, 128), 0)
    parent = t // 32 % 2 * 8 + t % 16 // 2
    pick = (parent == iota((128, 128), 1) % 16).astype(F32)
    families = jnp.concatenate([mass] + shifted + [jnp.zeros((4, 128), F32)], axis=0)
    families = jnp.dot(families, pick, precision=HIGH, preferred_element_type=F32)
    last = jnp.where(lane < 64, fold_rows(families, 16), jnp.max(fastest))
    five = jnp.concatenate([mass] + dipole + [last], axis=0)
    many = jnp.concatenate([five] * 8, axis=0)
    for copy in range(16):
        sent[copy * 40 : copy * 40 + 40, :] = many


def faces(far_left, left, right, far_right):
    value = (7.0 / 12.0) * (left + right) - (1.0 / 12.0) * (far_left + far_right)
    return jnp.minimum(jnp.maximum(value, jnp.minimum(left, right)), jnp.maximum(left, right))


def upper_and_lower(centre, above, below):
    up, down = above - centre, below - centre
    most_up, most_down = 2.0 * jnp.abs(down), 2.0 * jnp.abs(up)
    upper = centre + jnp.minimum(jnp.maximum(up, -most_up), most_up)
    lower = centre + jnp.minimum(jnp.maximum(down, -most_down), most_down)
    return upper, lower


def flux_of(q, k):
    inverse = reciprocal(q[0])
    velocity = q[1 + k] * inverse
    kinetic = (q[1] * q[1] + q[2] * q[2] + q[3] * q[3]) * inverse
    pressure = (2.0 / 3.0) * q[4] - (1.0 / 3.0) * kinetic
    out = [q[1 + k]] + [q[1 + c] * velocity for c in range(3)] + [(q[4] + pressure) * velocity]
    out[1 + k] = out[1 + k] + pressure
    return out


def twice_flux(left, right, speed, k):
    from_left, from_right = flux_of(left, k), flux_of(right, k)
    return [
        (a + b) - speed * (r - l) for a, b, l, r in zip(from_left, from_right, left, right, strict=True)
    ]


def sweep(load, speed_at, store, length, k):
    window = [[load(f, i) for f in range(5)] for i in (-3, -2, -1)]
    above_old = upper_old = speed_old = flux_old = None
    for i in range(-2, length + 1):
        window.append([load(f, i + 2) for f in range(5)])
        far_left, left, right, far_right = window[-4:]
        above = [faces(*each) for each in zip(far_left, left, right, far_right, strict=True)]
        if above_old is not None:
            pairs = [upper_and_lower(*each) for each in zip(left, above, above_old, strict=True)]
            upper, lower = [p[0] for p in pairs], [p[1] for p in pairs]
            speed = speed_at(i, left)
            if upper_old is not None:
                flux = twice_flux(upper_old, lower, jnp.maximum(speed_old, speed), k)
                if flux_old is not None:
                    store(i - 1, [a - b for a, b in zip(flux, flux_old, strict=True)])
                flux_old = flux
            upper_old, speed_old = upper, speed
        above_old = above


def shift_up(values, lane):
    return jnp.where(lane == NZ - 1, values, pltpu.roll(values, NZ - 1, 1))


def shift_down(values, lane):
    return jnp.where(lane == 0, values, pltpu.roll(values, 1, 1))


def divergence_kernel(
    place, state, x_one, x_two, y_one, y_two, fine_pairs, fine_count, coarse_pairs,
    out, fine_uses, coarse_uses, inverse_of, sound, x_low, x_high, y_low, y_high,
):
    morton, octant = place[0], place[1]
    morton_last, oct_last = place[2] - 1, place[3] - 1
    lane = iota((8, 128), 1)

    for field in range(5):
        edges = [state[field * ROWS : field * ROWS + NY, :], state[field * ROWS + ROWS - NY : field * ROWS + ROWS, :]]
        for layer in range(3):
            row = (field * 3 + layer) * NY
            one, two = x_one[row : row + NY, :], x_two[row : row + NY, :]
            even = morton % 2 == 0
            x_low[row : row + NY, :] = jnp.where(morton == 0, edges[0], jnp.where(even, two, one))
            x_high[row : row + NY, :] = jnp.where(morton == morton_last, edges[1], jnp.where(even, one, two))
        edges = [state[pl.ds(field * ROWS + y, NX, stride=NY), :] for y in (0, NY - 1)]
        for layer in range(3):
            row = (field * 3 + layer) * NX
            one, two = y_one[row : row + NX, :], y_two[row : row + NX, :]
            even = octant % 2 == 0
            y_low[row : row + NX, :] = jnp.where(octant == 0, edges[0], jnp.where(even, two, one))
            y_high[row : row + NX, :] = jnp.where(octant == oct_last, edges[1], jnp.where(even, one, two))

    def along_z(step, _):
        row = pl.multiple_of(step * 8, 8)
        q = [state[pl.ds(pl.multiple_of(f * ROWS + row, 8), 8), :] for f in range(5)]
        inverse = reciprocal(q[0])
        speed_of_sound = sound_of(q, inverse)
        inverse_of[pl.ds(row, 8), :] = inverse
        sound[pl.ds(row, 8), :] = speed_of_sound
        speed = jnp.abs(q[3]) * inverse + speed_of_sound
        speed = jnp.maximum(speed, shift_up(speed, lane))
        upper, lower = [], []
        for values in q:
            right = shift_up(values, lane)
            above = faces(shift_down(values, lane), values, right, shift_up(right, lane))
            below = jnp.where(lane == 0, values, pltpu.roll(above, 1, 1))
            u, l = upper_and_lower(values, above, below)
            upper.append(u)
            lower.append(jnp.where(lane == NZ - 1, values, pltpu.roll(l, NZ - 1, 1)))
        flux = twice_flux(upper, lower, speed, 2)
        first = [2.0 * each for each in flux_of(q, 2)]
        for f in range(5):
            below = jnp.where(lane == 0, first[f], pltpu.roll(flux[f], 1, 1))
            out[pl.ds(pl.multiple_of(f * ROWS + row, 8), 8), :] = flux[f] - below
        return 0

    lax.fori_loop(0, ROWS // 8, along_z, 0, unroll=2)

    def along_x(step, _):
        column = pl.multiple_of(step * 8, 8)

        def rows(f, i):
            return pl.ds(pl.multiple_of(f * ROWS + i * NY + column, 8), 8)

        def load(f, i):
            if i < 0:
                return x_low[pl.ds(pl.multiple_of((f * 3 + i + 3) * NY + column, 8), 8), :]
            if i >= NX:
                return x_high[pl.ds(pl.multiple_of((f * 3 + i - NX) * NY + column, 8), 8), :]
            return state[rows(f, i), :]

        def speed_at(i, q):
            if 0 <= i < NX:
                inverse, own = inverse_of[rows(0, i), :], sound[rows(0, i), :]
            else:
                inverse = reciprocal(q[0])
                own = sound_of(q, inverse)
            return jnp.abs(q[1]) * inverse + own

        def store(i, values):
            for f in range(5):
                out[rows(f, i), :] = out[rows(f, i), :] + values[f]

        sweep(load, speed_at, store, NX, 0)
        return 0

    lax.fori_loop(0, NY // 8, along_x, 0)

    def along_y(step, _):
        start = pl.multiple_of(step * 8, 8)

        def rows(f, i):
            return pl.ds(f * ROWS + start * NY + i, 8, stride=NY)

        def load(f, i):
            if i < 0:
                return y_low[pl.ds(pl.multiple_of((f * 3 + i + 3) * NX + start, 8), 8), :]
            if i >= NY:
                return y_high[pl.ds(pl.multiple_of((f * 3 + i - NY) * NX + start, 8), 8), :]
            return state[rows(f, i), :]

        def speed_at(i, q):
            if 0 <= i < NY:
                inverse, own = inverse_of[rows(0, i), :], sound[rows(0, i), :]
            else:
                inverse = reciprocal(q[0])
                own = sound_of(q, inverse)
            return jnp.abs(q[2]) * inverse + own

        def store(i, values):
            for f in range(5):
                out[rows(f, i), :] = out[rows(f, i), :] + values[f]

        sweep(load, speed_at, store, NY, 1)
        return 0

    lax.fori_loop(0, NX // 8, along_y, 0)

    codes = jnp.concatenate([fine_pairs[...].astype(F32)] * 4, axis=1).T[0:32]
    spread = (iota((16, 128), 1) % 16 == iota((16, 128), 0)).astype(F32)
    used = fold_rows(
        jnp.dot(fine_count[...].astype(F32), spread, precision=HIGH, preferred_element_type=F32), 16
    )
    codes = jnp.where(iota((32, 128), 0).astype(F32) < used, codes, -1000.0)
    down = 25.0 * iota((8, 128), 0).astype(F32)
    codes = [jnp.broadcast_to(codes[j : j + 1], (8, 128)) - down for j in range(32)]
    for plane in range(25):
        count = jnp.zeros((8, 128), F32)
        for each in codes:
            count = count + jnp.where(each == plane, 1.0, 0.0)
        fine_uses[plane * 8 : plane * 8 + 8, :] = count

    for half in range(2):
        named = coarse_pairs[half * 8 : half * 8 + 8, :]
        named = [jnp.broadcast_to(named[:, j : j + 1], (8, 128)) - 16 * lane for j in range(32)]
        for lp in range(16):
            count = jnp.zeros((8, 128), F32)
            for each in named:
                count = count + jnp.where(each == lp, 1.0, 0.0)
            row = (lp * 2 + half) * 8
            coarse_uses[row : row + 8, :] = count


def tensors(r, square):
    square = jnp.maximum(square, 1.0)
    cube = 1.0 / (square * jnp.sqrt(square))
    three = 3.0 * cube / square
    scaled = [three * each for each in r]
    pull = [each * cube for each in r]
    tide = [scaled[i] * r[j] - cube if i == j else scaled[i] * r[j] for i, j in SYM]
    return pull, tide


def add_terms(totals, uses, r, square, mass, dipole):
    pull, tide = tensors(r, square)
    mass = uses * mass
    dipole = [uses * d for d in dipole]
    for i in range(3):
        term = mass * pull[i]
        for j in range(3):
            term = term - tide[sym(i, j)] * dipole[j]
        totals[i] = totals[i] + term
    for e in range(6):
        totals[3 + e] = totals[3 + e] + mass * tide[e]


def far_fields(place, uses_fine, uses_coarse, got, around):
    morton, octant = place[0], place[1]
    mortons, octs = place[2], place[3]
    lane = iota((8, 128), 1)
    lane_row = iota((1, 128), 1)

    rows = jnp.concatenate([got[pl.ds(g * 8 * SENT + 4, 8, stride=SENT), :] for g in range(16)], axis=0)
    time_step = COURANT / jnp.max(rows[:, 64:128])
    moments = rows.T
    target_z = iota((8, 128), 0)
    rx = 16.0 * (lane // 4 - morton).astype(F32)
    coarse = []
    for half in range(2):
        totals = [jnp.zeros((8, 128), F32) for _ in range(9)]
        for lp in range(16):
            ry = 16.0 * (lane % 4 * 2 + lp // 8 - (2 * octant + half)).astype(F32)
            rz = 16.0 * (lp % 8 - target_z).astype(F32)
            own = [jnp.broadcast_to(moments[m * 16 + lp : m * 16 + lp + 1], (8, 128)) for m in range(4)]
            row = (lp * 2 + half) * 8
            add_terms(totals, uses_coarse[row : row + 8, :], (rx, ry, rz), rx * rx + ry * ry + rz * rz, own[0], own[1:])
        coarse.append([jnp.sum(each, axis=1, keepdims=True) for each in totals])
    result = []
    for e in range(9):
        column = jnp.where(lane // 32 % 2 == 0, coarse[0][e], coarse[1][e])
        column = jnp.where(lane % 16 // 2 == iota((8, 128), 0), column, 0.0)
        result.append(jnp.sum(column, axis=0, keepdims=True))
    side = [4.0 * (2 * s - 1).astype(F32) for s in (lane_row // 64, lane_row // 16 % 2, lane_row % 2)]
    for i in range(3):
        for j in range(3):
            result[i] = result[i] + result[3 + sym(i, j)] * side[j]

    blocks = []
    for dy in (-1, 0, 1):
        block = []
        for dx in (-1, 0, 1):
            at_x, at_y = morton + dx, octant + dy
            inside = (at_x >= 0) & (at_x < mortons) & (at_y >= 0) & (at_y < octs)
            device = jnp.clip(at_x, 0, mortons - 1) * octs + jnp.clip(at_y, 0, octs - 1)
            for m in range(4):
                block.append(jnp.where(inside, got[pl.ds(device * SENT + m, 1), :], 0.0))
        blocks.append(jnp.concatenate(block + [jnp.zeros((4, 128), F32)], axis=0))
    wide = iota((16, 128), 1)
    around[...] = jnp.zeros(around.shape, F32)
    for oy in range(-2, 3):
        if oy == 0:
            moved = blocks[1]
        else:
            moved = pltpu.roll(blocks[1], (-16 * oy) % 128, 1)
            if oy > 0:
                moved = jnp.where(wide // 16 % 4 + oy > 3, pltpu.roll(blocks[2], (64 - 16 * oy) % 128, 1), moved)
            else:
                moved = jnp.where(wide // 16 % 4 + oy < 0, pltpu.roll(blocks[0], (-64 - 16 * oy) % 128, 1), moved)
        swapped = pltpu.roll(moved, 64, 1)
        for m in range(4):
            low, own, high = [(moved[d * 4 + m : d * 4 + m + 1], swapped[d * 4 + m : d * 4 + m + 1]) for d in range(3)]
            first = lane_row < 64
            lines = [
                low[0], jnp.where(first, low[1], own[1]), own[0], jnp.where(first, own[1], high[1]), high[0],
            ]
            row = (m * 5 + oy + 2) * 8
            around[row : row + 5, :] = jnp.concatenate(lines, axis=0)
    totals = [jnp.zeros((8, 128), F32) for _ in range(9)]
    rx = 8.0 * (iota((8, 128), 0) - 2).astype(F32)
    square_x = rx * rx
    for oy in range(-2, 3):
        base = [around[(m * 5 + oy + 2) * 8 : (m * 5 + oy + 2) * 8 + 8, :] for m in range(4)]
        for oz in range(-2, 3):
            moved = base
            if oz:
                ok = (lane % 16 + oz >= 0) & (lane % 16 + oz < 16)
                moved = [jnp.where(ok, pltpu.roll(each, (-oz) % 128, 1), 0.0) for each in base]
            plane = ((oy + 2) * 5 + oz + 2) * 8
            add_terms(
                totals, uses_fine[plane : plane + 8, :], (rx, 8.0 * oy, 8.0 * oz),
                square_x + (64.0 * oy * oy + 64.0 * oz * oz), moved[0], moved[1:],
            )
    for e in range(9):
        result[e] = GRAVITY * (result[e] + jnp.sum(totals[e], axis=0, keepdims=True))
    return result, time_step


def update_kernel(place, state, twice, uses_fine, uses_coarse, got, new, gravity, around, field, step_size):
    slab = pl.program_id(0)
    layers = state.shape[1] // NY

    @pl.when(slab == 0)
    def _():
        result, time_step = far_fields(place, uses_fine, uses_coarse, got, around)
        step_size[0] = time_step
        keep = iota((8, 128), 1) // 16 == iota((8, 128), 0)
        spread = (iota((128, 128), 0) % 16 == iota((128, 128), 1) // 8).astype(F32)
        rows = jnp.concatenate([jnp.where(keep, each, 0.0) for each in result], axis=0)
        rows = jnp.dot(rows, spread, precision=HIGH, preferred_element_type=F32)
        rows = [rows[e * 8 : e * 8 + 8] for e in range(9)]
        offset_z = (iota((8, 128), 1) % 8).astype(F32) - 3.5
        for i in range(3):
            field[i * 8 : i * 8 + 8, :] = rows[i] + rows[3 + sym(i, 2)] * offset_z
            field[(3 + i) * 8 : (3 + i) * 8 + 8, :] = rows[3 + sym(i, 0)]
            field[(6 + i) * 8 : (6 + i) * 8 + 8, :] = rows[3 + sym(i, 1)]

    time_step = step_size[0]
    half = 0.5 * time_step
    offset_y = iota((8, 128), 0).astype(F32) - 3.5
    for ty in range(4):
        tx = slab * layers // 8
        at = tx * 4 + ty
        base = [
            field[pl.ds(i * 8 + at, 1), :] + field[pl.ds((6 + i) * 8 + at, 1), :] * offset_y for i in range(3)
        ]
        slope = [field[pl.ds((3 + i) * 8 + at, 1), :] for i in range(3)]
        for layer in range(layers):
            offset_x = ((slab * layers + layer) % 8).astype(F32) - 3.5
            row = layer * NY + ty * 8
            q = [state[f, row : row + 8, :] for f in range(5)]
            pull = [base[i] + slope[i] * offset_x for i in range(3)]
            for i in range(3):
                gravity[i, row : row + 8, :] = pull[i]
            moved = [q[f] - half * twice[f, row : row + 8, :] for f in range(5)]
            new[0, row : row + 8, :] = moved[0]
            weight = time_step * q[0]
            for i in range(3):
                new[1 + i, row : row + 8, :] = moved[1 + i] + weight * pull[i]
            gain = q[1] * pull[0] + q[2] * pull[1] + q[3] * pull[2]
            new[4, row : row + 8, :] = moved[4] + time_step * gain


def whole(count):
    return [pl.BlockSpec(memory_space=pltpu.SMEM)] + [pl.BlockSpec(memory_space=pltpu.VMEM)] * count


LIMIT = pltpu.CompilerParams(vmem_limit_bytes=48 * 1024 * 1024)


def shaped(*shape):
    return jax.ShapeDtypeStruct(shape, F32)


def prepare(place, rows):
    return pl.pallas_call(
        prepare_kernel,
        out_shape=[shaped(128 * SENT, 128), shaped(480, 128), shaped(480, 128), shaped(240, 128), shaped(240, 128)],
        in_specs=whole(1),
        out_specs=[pl.BlockSpec(memory_space=pltpu.VMEM)] * 5,
        compiler_params=LIMIT,
    )(place, rows)


def diverge(place, rows, halos, fine_pairs, fine_count, coarse_pairs):
    return pl.pallas_call(
        divergence_kernel,
        out_shape=[shaped(5 * ROWS, 128), shaped(200, 128), shaped(256, 128)],
        in_specs=whole(8),
        out_specs=[pl.BlockSpec(memory_space=pltpu.VMEM)] * 3,
        scratch_shapes=[pltpu.VMEM((ROWS, 128), F32)] * 2
        + [pltpu.VMEM((480, 128), F32)] * 2
        + [pltpu.VMEM((240, 128), F32)] * 2,
        compiler_params=LIMIT,
    )(place, rows, *halos, fine_pairs, fine_count, coarse_pairs)


def update(place, rows, twice, uses_fine, uses_coarse, got):
    slabs = 4
    part = ROWS // slabs
    at_slab = lambda i: (0, i, 0)
    at_start = lambda i: (0, 0)
    return pl.pallas_call(
        update_kernel,
        grid=(slabs,),
        out_shape=[shaped(5, ROWS, 128), shaped(3, ROWS, 128)],
        in_specs=[
            pl.BlockSpec(memory_space=pltpu.SMEM),
            pl.BlockSpec((5, part, 128), at_slab),
            pl.BlockSpec((5, part, 128), at_slab),
            pl.BlockSpec((200, 128), at_start),
            pl.BlockSpec((256, 128), at_start),
            pl.BlockSpec((128 * SENT, 128), at_start),
        ],
        out_specs=[pl.BlockSpec((5, part, 128), at_slab), pl.BlockSpec((3, part, 128), at_slab)],
        scratch_shapes=[pltpu.VMEM((160, 128), F32), pltpu.VMEM((72, 128), F32), pltpu.SMEM((1,), F32)],
        compiler_params=LIMIT,
    )(place, rows.reshape(5, ROWS, 128), twice.reshape(5, ROWS, 128), uses_fine, uses_coarse, got)


def local(state, fine_pairs, fine_count, coarse_pairs):
    mortons, octs = lax.axis_size("morton"), lax.axis_size("oct")
    place = jnp.stack([lax.axis_index("morton"), lax.axis_index("oct"), mortons, octs]).astype(jnp.int32)
    rows = state.reshape(5 * ROWS, 128)
    sent, x_one, x_two, y_one, y_two = prepare(place, rows)

    def swap(values, axis, devices, first):
        pairs = [(i, i + 1) for i in range(first, devices - 1, 2)]
        return lax.ppermute(values, axis, pairs + [(j, i) for i, j in pairs])

    halos = [
        swap(x_one, "morton", mortons, 0),
        swap(x_two, "morton", mortons, 1),
        swap(y_one, "oct", octs, 0),
        swap(y_two, "oct", octs, 1),
    ]
    got = lax.all_to_all(sent.reshape(mortons * octs, 1, SENT * 128), AXES, 0, 0, tiled=True)
    twice, uses_fine, uses_coarse = diverge(
        place, rows, halos, fine_pairs.reshape(128, 32), fine_count.reshape(8, 16), coarse_pairs.reshape(16, 32)
    )
    new, gravity = update(place, rows, twice, uses_fine, uses_coarse, got.reshape(mortons * octs * SENT, 128))
    return new.reshape(state.shape), gravity.reshape(3, NX, NY, NZ)


def solution(mesh):
    in_specs = (
        P(None, "morton", "oct", None),
        P("morton", "oct", None, None),
        P("morton", "oct", None),
        P("morton", "oct", None, None),
    )
    out_specs = (P(None, "morton", "oct", None), P(None, "morton", "oct", None))
    return jax.shard_map(local, mesh=mesh, in_specs=in_specs, out_specs=out_specs, check_vma=False)
```

time: 437 us -> 55.5 us (0.13)
  the two profiles are of different devices: /device:TPU:1 before, /device:TPU:4 now
where the time goes in v1:
time: 55.5 us; the launch traced here: 55.3 us
  Pallas kernels  24.7 us (45%)
  starting transfers between devices  19.7 us (35%)
  waiting for transfers between devices  8.8 us (16%)
  local copies, waits for them, and re-layouts  1.33 us (2%)
  between operations  0.72 us (1%)
    pallas_call x1, Pallas kernels, diverge(): pl.pallas_call(divergence_kernel, out_shape=[shaped(5 * ROWS, 128), shape...  19 us
    all_to_all x1, starting transfers between devices, local(): lax.all_to_all(sent.reshape(mortons * octs, 1, SENT * 128), AXES, 0, 0, t...  10.5 us
    ppermute x4, starting transfers between devices, swap(): return lax.ppermute(values, axis, pairs + [(j, i) for i, j in pairs])  9.16 us
    ppermute x4, waiting for transfers between devices, swap(): return lax.ppermute(values, axis, pairs + [(j, i) for i, j in pairs])  8.8 us
    pallas_call x1, Pallas kernels, update(): pl.pallas_call(update_kernel, grid=(slabs,), out_shape=[shaped(5, ROWS, 1...  3.56 us
    pallas_call x1, Pallas kernels, prepare(): pl.pallas_call(prepare_kernel, out_shape=[shaped(128 * SENT, 128), shaped...  2.09 us
    unnamed x10, local copies, waits for them, and re-layouts  1.33 us
  transfers between devices with their start and end apart: 5, of which 3 were waited for; matrix products, arithmetic and copies ran while one was open for 0% of the time, Pallas kernels for 34%

profile of v1, /device:TPU:4, one launch (start us, length us, event | category | flops | bytes accessed | tf_op | source)
XLA Modules:
  0.0 55.3 jit_solution(3406389808769327872)
XLA Ops:
  0.6 0.0 copy-start.3
  0.6 0.0 copy-start.4
  0.7 0.1 pad_add_fusion.place
  0.7 0.0 copy-start
  0.7 1.3 %copy-done = f32[5,16,32,128]{3,2,1,0:T(8,128)S(1)} copy-done((f32[5,16,32,128]{3,2,1,0:T(8,128)S(1)}, f32[5,16,32,128]{3,2,1,0:T(8,128)}, u32[]{:S(2)}) %copy-start) | copy-done | bytes 1310744
  2.1 0.0 copy-start.1
  2.1 0.0 copy-start.2
  2.1 2.1 %shard_map.59 = (f32[640,128]{1,0:T(8,128)}, f32[480,128]{1,0:T(8,128)S(1)}, f32[480,128]{1,0:T(8,128)S(1)}, f32[240,128]{1,0:T(8,128)S(1)}, f32[240,128]{1,0:T(8,128)S(1)}) custom-call(s32[4]{0:T(128)S(1)} %pad_add_fusion.place, f32[2560,128]{1,0:T(8,128)S(1)} %bitcast.12), custom_call_target="tpu_custom_call" | custom-call | tf_op jit(solution)/shard_map/pallas_call | solution.py:458
  4.1 10.5 %all-to-all-start = ((f32[128,1,640]{2,1,0:T(1,128)}), f32[128,1,640]{2,1,0:T(1,128)S(1)}, u32[]{:S(2)}, u32[]{:S(2)}) async-start(f32[128,1,640]{2,1,0:T(1,128)} %bitcast.8), calls=%async_computation | async-start | bytes 655360 | tf_op jit(solution)/shard_map/all_to_all | solution.py:519
  14.7 1.5 %collective-permute-start = (f32[480,128]{1,0:T(8,128)S(1)}, f32[480,128]{1,0:T(8,128)S(1)}, u32[]{:S(2)}, u32[]{:S(2)}) collective-permute-start(f32[480,128]{1,0:T(8,128)S(1)} %get-tuple-element.12), channel_id=1, source_target_pairs={{0,4},{8,12},{16,20},{24,28},{32,36},{40,44},{48,52},{56,60},{64,6... | collective-permute-start | bytes 737288 | tf_op jit(solution)/shard_map/ppermute | solution.py:511
  16.2 6.9 %collective-permute-start.1 = (f32[480,128]{1,0:T(8,128)S(1)}, f32[480,128]{1,0:T(8,128)S(1)}, u32[]{:S(2)}, u32[]{:S(2)}) collective-permute-start(f32[480,128]{1,0:T(8,128)S(1)} %get-tuple-element.13), channel_id=1, source_target_pairs={{4,8},{12,16},{20,24},{28,32},{36,40},{44,48},{52,56},{60,64},{68,... | collective-permute-start | bytes 737288 | tf_op jit(solution)/shard_map/ppermute | solution.py:511
  23.1 0.1 collective-permute-start.2
  23.2 0.7 %collective-permute-start.3 = (f32[240,128]{1,0:T(8,128)S(1)}, f32[240,128]{1,0:T(8,128)S(1)}, u32[]{:S(2)}, u32[]{:S(2)}) collective-permute-start(f32[240,128]{1,0:T(8,128)S(1)} %get-tuple-element.15), channel_id=1, source_target_pairs={{1,2},{2,1},{5,6},{6,5},{9,10},{10,9},{13,14},{14,13},{17,18},{18,... | collective-permute-start | bytes 368648 | tf_op jit(solution)/shard_map/ppermute | solution.py:511
  23.8 0.6 %collective-permute-done.2.y_one = f32[240,128]{1,0:T(8,128)S(1)} collective-permute-done((f32[240,128]{1,0:T(8,128)S(1)}, f32[240,128]{1,0:T(8,128)S(1)}, u32[]{:S(2)}, u32[]{:S(2)}) %collective-permute-start.2) | collective-permute-done | bytes 122912 | tf_op jit(solution)/shard_map/ppermute | solution.py:511
  24.5 0.0 collective-permute-done.3.y_two
  24.5 0.7 %collective-permute-done.x_one = f32[480,128]{1,0:T(8,128)S(1)} collective-permute-done((f32[480,128]{1,0:T(8,128)S(1)}, f32[480,128]{1,0:T(8,128)S(1)}, u32[]{:S(2)}, u32[]{:S(2)}) %collective-permute-start) | collective-permute-done | bytes 245792 | tf_op jit(solution)/shard_map/ppermute | solution.py:511
  25.2 7.4 %collective-permute-done.1.x_two = f32[480,128]{1,0:T(8,128)S(1)} collective-permute-done((f32[480,128]{1,0:T(8,128)S(1)}, f32[480,128]{1,0:T(8,128)S(1)}, u32[]{:S(2)}, u32[]{:S(2)}) %collective-permute-start.1) | collective-permute-done | bytes 245792 | tf_op jit(solution)/shard_map/ppermute | solution.py:511
  32.6 0.0 copy-done.3
  32.6 0.0 copy-done.4
  32.6 0.0 copy-done.1
  32.7 0.0 copy-done.2
  32.7 19.0 %shard_map.60 = (f32[2560,128]{1,0:T(8,128)S(1)}, f32[200,128]{1,0:T(8,128)S(1)}, f32[256,128]{1,0:T(8,128)S(1)}) custom-call(s32[4]{0:T(128)S(1)} %pad_add_fusion.place, f32[2560,128]{1,0:T(8,128)S(1)} %bitcast.13, f32[480,128]{1,0:T(8,128)S(1)} %collective-permute-done.x_one, f32[480,128]{1,0:T(8,128)S(1)} %collective-permute-done.1.x_two, ...), custom_call_target="tpu_custom_call" | custom-call | tf_op jit(solution)/shard_map/pallas_call | solution.py:468
  51.7 0.0 all-to-all-done
  51.7 3.6 %shard_map.61 = (f32[5,512,128]{2,1,0:T(8,128)}, f32[3,512,128]{2,1,0:T(8,128)}) custom-call(s32[4]{0:T(128)S(1)} %pad_add_fusion.place, f32[5,512,128]{2,1,0:T(8,128)S(1)} %bitcast.14, f32[5,512,128]{2,1,0:T(8,128)S(1)} %bitcast.15, f32[200,128]{1,0:T(8,128)S(1)} %get-tuple-element.17.uses_fine, f32[256,128]{1,0:T(8,128)S(1)} %get-tuple-element.18.uses_coarse, ...), custom_call_target="tpu_custom_call" | custom-call | tf_op jit(solution)/shard_map/pallas_call | solution.py:485
Async XLA Ops:
  0.6 32.0 %copy-start.3 = (s32[1,2,8,32]{3,2,1,0:T(8,128)S(1)}, s32[1,2,8,32]{3,2,1,0:T(8,128)}, u32[]{:S(2)}) copy-start(s32[1,2,8,32]{3,2,1,0:T(8,128)} %param.7) | copy-start | bytes 6148
  0.6 32.0 %copy-start.4 = (s32[2,4,16]{2,1,0:T(4,128)S(1)}, s32[2,4,16]{2,1,0:T(4,128)}, u32[]{:S(2)}) copy-start(s32[2,4,16]{2,1,0:T(4,128)} %param.6) | copy-start | bytes 1540
  0.7 1.3 %copy-start = (f32[5,16,32,128]{3,2,1,0:T(8,128)S(1)}, f32[5,16,32,128]{3,2,1,0:T(8,128)}, u32[]{:S(2)}) copy-start(f32[5,16,32,128]{3,2,1,0:T(8,128)} %param.4) | copy-start | bytes 3932164
  2.1 30.6 %copy-start.1 = (f32[5,16,32,128]{3,2,1,0:T(8,128)S(1)}, f32[5,16,32,128]{3,2,1,0:T(8,128)}, u32[]{:S(2)}) copy-start(f32[5,16,32,128]{3,2,1,0:T(8,128)} %param.4) | copy-start | bytes 3932164
  2.1 30.6 %copy-start.2 = (s32[2,4,16,32]{3,2,1,0:T(8,128)S(1)}, s32[2,4,16,32]{3,2,1,0:T(8,128)}, u32[]{:S(2)}) copy-start(s32[2,4,16,32]{3,2,1,0:T(8,128)} %param.5) | copy-start | bytes 49156
  4.1 47.6 %all-to-all-start = ((f32[128,1,640]{2,1,0:T(1,128)}), f32[128,1,640]{2,1,0:T(1,128)S(1)}, u32[]{:S(2)}, u32[]{:S(2)}) async-start(f32[128,1,640]{2,1,0:T(1,128)} %bitcast.8), calls=%async_computation | async-start | bytes 655360 | tf_op jit(solution)/shard_map/all_to_all | solution.py:519
  14.7 10.6 %collective-permute-start = (f32[480,128]{1,0:T(8,128)S(1)}, f32[480,128]{1,0:T(8,128)S(1)}, u32[]{:S(2)}, u32[]{:S(2)}) collective-permute-start(f32[480,128]{1,0:T(8,128)S(1)} %get-tuple-element.12), channel_id=1, source_target_pairs={{0,4},{8,12},{16,20},{24,28},{32,36},{40,44},{48,52},{56,60},{64,6... | collective-permute-start | bytes 737288 | tf_op jit(solution)/shard_map/ppermute | solution.py:511
  16.2 16.4 %collective-permute-start.1 = (f32[480,128]{1,0:T(8,128)S(1)}, f32[480,128]{1,0:T(8,128)S(1)}, u32[]{:S(2)}, u32[]{:S(2)}) collective-permute-start(f32[480,128]{1,0:T(8,128)S(1)} %get-tuple-element.13), channel_id=1, source_target_pairs={{4,8},{12,16},{20,24},{28,32},{36,40},{44,48},{52,56},{60,64},{68,... | collective-permute-start | bytes 737288 | tf_op jit(solution)/shard_map/ppermute | solution.py:511
  23.1 1.4 %collective-permute-start.2 = (f32[240,128]{1,0:T(8,128)S(1)}, f32[240,128]{1,0:T(8,128)S(1)}, u32[]{:S(2)}, u32[]{:S(2)}) collective-permute-start(f32[240,128]{1,0:T(8,128)S(1)} %get-tuple-element.14), channel_id=1, source_target_pairs={{0,1},{2,3},{1,0},{3,2},{4,5},{6,7},{5,4},{7,6},{8,9},{10,11},{9,8... | collective-permute-start | bytes 368648 | tf_op jit(solution)/shard_map/ppermute | solution.py:511
  23.2 1.3 %collective-permute-start.3 = (f32[240,128]{1,0:T(8,128)S(1)}, f32[240,128]{1,0:T(8,128)S(1)}, u32[]{:S(2)}, u32[]{:S(2)}) collective-permute-start(f32[240,128]{1,0:T(8,128)S(1)} %get-tuple-element.15), channel_id=1, source_target_pairs={{1,2},{2,1},{5,6},{6,5},{9,10},{10,9},{13,14},{14,13},{17,18},{18,... | collective-permute-start | bytes 368648 | tf_op jit(solution)/shard_map/ppermute | solution.py:511

commit v2 on v1

--- a/solution.py
+++ b/solution.py
@@ -16,6 +16,8 @@
 
 NX, NY, NZ = 16, 32, 128
 ROWS = NX * NY
+PITCH = 33
+TALL = 144
 SENT = 5
 SYM = ((0, 0), (0, 1), (0, 2), (1, 1), (1, 2), (2, 2))
 
@@ -44,45 +46,43 @@
     return jnp.sum(jnp.where(keep, values, 0.0), axis=0, keepdims=True)
 
 
-def prepare_kernel(place, state, sent, x_one, x_two, y_one, y_two):
-    morton_odd = place[0] % 2
-    oct_odd = place[1] % 2
-    x_starts = (jnp.where(morton_odd == 0, NX - 3, 0), jnp.where(morton_odd == 0, 0, NX - 3))
-    y_starts = (jnp.where(oct_odd == 0, NY - 3, 0), jnp.where(oct_odd == 0, 0, NY - 3))
-    for field in range(5):
-        for out, start in ((x_one, x_starts[0]), (x_two, x_starts[1])):
-            out[field * 96 : field * 96 + 96, :] = state[
-                pl.ds(pl.multiple_of(field * ROWS + start * NY, 32), 96), :
-            ]
-        for out, start in ((y_one, y_starts[0]), (y_two, y_starts[1])):
-            for layer in range(3):
-                row = (field * 3 + layer) * 16
-                out[row : row + 16, :] = state[pl.ds(field * ROWS + start + layer, 16, stride=NY), :]
-
+def moments_kernel(state, sent, rows, arrived):
+    part = ROWS // 4
+    copies = [
+        pltpu.make_async_copy(
+            state.at[:, pl.ds(c * part, part), :], rows.at[:, pl.ds(c * part, part), :], arrived.at[c]
+        )
+        for c in range(4)
+    ]
+    for copy in copies:
+        copy.start()
     offset_y = iota((8, 128), 0).astype(F32) - 3.5
     fastest = jnp.zeros((8, 128), F32)
     sums, sums_x, sums_y = [], [], []
     for tx in range(2):
+        totals, totals_x = [jnp.zeros((8, 128), F32)] * 4, [jnp.zeros((8, 128), F32)] * 4
+        for half in range(2):
+            copies[tx * 2 + half].wait()
+            for x in range(half * 4, half * 4 + 4):
+                for ty in range(4):
+                    row = (tx * 8 + x) * NY + ty * 8
+                    q = [rows[f, row : row + 8, :] for f in range(5)]
+                    inverse = reciprocal(q[0])
+                    speed_of_sound = sound_of(q, inverse)
+                    largest = jnp.maximum(jnp.maximum(jnp.abs(q[1]), jnp.abs(q[2])), jnp.abs(q[3]))
+                    fastest = jnp.maximum(fastest, largest * inverse + speed_of_sound)
+                    totals[ty] = totals[ty] + q[0]
+                    totals_x[ty] = totals_x[ty] + q[0] * (x - 3.5)
         for ty in range(4):
-            total = total_x = None
-            for x in range(8):
-                row = (tx * 8 + x) * NY + ty * 8
-                q = [state[f * ROWS + row : f * ROWS + row + 8, :] for f in range(5)]
-                inverse = reciprocal(q[0])
-                largest = jnp.maximum(jnp.maximum(jnp.abs(q[1]), jnp.abs(q[2])), jnp.abs(q[3]))
-                fastest = jnp.maximum(fastest, largest * inverse + sound_of(q, inverse))
-                weighted = q[0] * (x - 3.5)
-                total = q[0] if total is None else total + q[0]
-                total_x = weighted if total_x is None else total_x + weighted
-            sums.append(jnp.sum(total, axis=0, keepdims=True))
-            sums_x.append(jnp.sum(total_x, axis=0, keepdims=True))
-            sums_y.append(jnp.sum(total * offset_y, axis=0, keepdims=True))
-    rows = jnp.concatenate(sums + sums_x + sums_y, axis=0)
+            sums.append(jnp.sum(totals[ty], axis=0, keepdims=True))
+            sums_x.append(jnp.sum(totals_x[ty], axis=0, keepdims=True))
+            sums_y.append(jnp.sum(totals[ty] * offset_y, axis=0, keepdims=True))
+    lines = jnp.concatenate(sums + sums_x + sums_y, axis=0)
     z = iota((128, 128), 0)
     pick = (z // 8 == iota((128, 128), 1) % 16).astype(F32)
     by_z = pick * ((z % 8).astype(F32) - 3.5)
-    folded = jnp.dot(rows, pick, precision=HIGH, preferred_element_type=F32)
-    folded_z = jnp.dot(rows[0:8], by_z, precision=HIGH, preferred_element_type=F32)
+    folded = jnp.dot(lines, pick, precision=HIGH, preferred_element_type=F32)
+    folded_z = jnp.dot(lines[0:8], by_z, precision=HIGH, preferred_element_type=F32)
     mass = fold_rows(folded[0:8], 16)
     dipole = [fold_rows(folded[8:16], 16), fold_rows(folded[16:24], 16), fold_rows(folded_z, 16)]
 
@@ -151,124 +151,52 @@
         above_old = above
 
 
-def shift_up(values, lane):
-    return jnp.where(lane == NZ - 1, values, pltpu.roll(values, NZ - 1, 1))
-
-
-def shift_down(values, lane):
-    return jnp.where(lane == 0, values, pltpu.roll(values, 1, 1))
-
-
-def divergence_kernel(
-    place, state, x_one, x_two, y_one, y_two, fine_pairs, fine_count, coarse_pairs,
-    out, fine_uses, coarse_uses, inverse_of, sound, x_low, x_high, y_low, y_high,
-):
-    morton, octant = place[0], place[1]
-    morton_last, oct_last = place[2] - 1, place[3] - 1
+def sides(one, two, low, high, rank, last, edges, length):
+    even = rank % 2 == 0
+    for field in range(5):
+        first, final = edges(field)
+        for layer in range(3):
+            row = (field * 3 + layer) * length
+            a, b = one[row : row + length, :], two[row : row + length, :]
+            low[row : row + length, :] = jnp.where(rank == 0, first, jnp.where(even, b, a))
+            high[row : row + length, :] = jnp.where(rank == last, final, jnp.where(even, a, b))
+
+
+def split_kernel(place, state, x_one, x_two, y_one, y_two, padded, inverse_of, sound):
+    even, oct_even = place[0] % 2 == 0, place[1] % 2 == 0
+    x_starts = (jnp.where(even, NX - 3, 0), jnp.where(even, 0, NX - 3))
+    y_starts = (jnp.where(oct_even, NY - 3, 0), jnp.where(oct_even, 0, NY - 3))
+    for f in range(5):
+        for out, start in ((x_one, x_starts[0]), (x_two, x_starts[1])):
+            out[f * 96 : f * 96 + 96, :] = state[pl.ds(pl.multiple_of(f * ROWS + start * NY, 32), 96), :]
+    for x in range(NX):
+        for y in range(0, NY, 8):
+            row = x * NY + y
+            q = [state[f * ROWS + row : f * ROWS + row + 8, :] for f in range(5)]
+            inverse = reciprocal(q[0])
+            at = x * PITCH + y
+            for f in range(5):
+                padded[f * NX * PITCH + at : f * NX * PITCH + at + 8, :] = q[f]
+            inverse_of[at : at + 8, :] = inverse
+            sound[at : at + 8, :] = sound_of(q, inverse)
+    for f in range(5):
+        for out, start in ((y_one, y_starts[0]), (y_two, y_starts[1])):
+            for layer in range(3):
+                row = (f * 3 + layer) * 16
+                out[row : row + 16, :] = padded[pl.ds(f * NX * PITCH + start + layer, 16, stride=PITCH), :]
+
+
+def turn_kernel(place, state, fine_pairs, fine_count, coarse_pairs, turned, fine_uses, coarse_uses):
+    def turn(step, _):
+        flat = state[pl.ds(pl.multiple_of(step * 128, 128), 128), :].T
+        base = pl.multiple_of(step * TALL, 8)
+        turned[pl.ds(base + 8, 128), :] = flat
+        turned[pl.ds(base, 8), :] = jnp.broadcast_to(flat[0:1], (8, 128))
+        turned[pl.ds(base + 136, 8), :] = jnp.broadcast_to(flat[127:128], (8, 128))
+        return 0
+
+    lax.fori_loop(0, 20, turn, 0, unroll=4)
     lane = iota((8, 128), 1)
-
-    for field in range(5):
-        edges = [state[field * ROWS : field * ROWS + NY, :], state[field * ROWS + ROWS - NY : field * ROWS + ROWS, :]]
-        for layer in range(3):
-            row = (field * 3 + layer) * NY
-            one, two = x_one[row : row + NY, :], x_two[row : row + NY, :]
-            even = morton % 2 == 0
-            x_low[row : row + NY, :] = jnp.where(morton == 0, edges[0], jnp.where(even, two, one))
-            x_high[row : row + NY, :] = jnp.where(morton == morton_last, edges[1], jnp.where(even, one, two))
-        edges = [state[pl.ds(field * ROWS + y, NX, stride=NY), :] for y in (0, NY - 1)]
-        for layer in range(3):
-            row = (field * 3 + layer) * NX
-            one, two = y_one[row : row + NX, :], y_two[row : row + NX, :]
-            even = octant % 2 == 0
-            y_low[row : row + NX, :] = jnp.where(octant == 0, edges[0], jnp.where(even, two, one))
-            y_high[row : row + NX, :] = jnp.where(octant == oct_last, edges[1], jnp.where(even, one, two))
-
-    def along_z(step, _):
-        row = pl.multiple_of(step * 8, 8)
-        q = [state[pl.ds(pl.multiple_of(f * ROWS + row, 8), 8), :] for f in range(5)]
-        inverse = reciprocal(q[0])
-        speed_of_sound = sound_of(q, inverse)
-        inverse_of[pl.ds(row, 8), :] = inverse
-        sound[pl.ds(row, 8), :] = speed_of_sound
-        speed = jnp.abs(q[3]) * inverse + speed_of_sound
-        speed = jnp.maximum(speed, shift_up(speed, lane))
-        upper, lower = [], []
-        for values in q:
-            right = shift_up(values, lane)
-            above = faces(shift_down(values, lane), values, right, shift_up(right, lane))
-            below = jnp.where(lane == 0, values, pltpu.roll(above, 1, 1))
-            u, l = upper_and_lower(values, above, below)
-            upper.append(u)
-            lower.append(jnp.where(lane == NZ - 1, values, pltpu.roll(l, NZ - 1, 1)))
-        flux = twice_flux(upper, lower, speed, 2)
-        first = [2.0 * each for each in flux_of(q, 2)]
-        for f in range(5):
-            below = jnp.where(lane == 0, first[f], pltpu.roll(flux[f], 1, 1))
-            out[pl.ds(pl.multiple_of(f * ROWS + row, 8), 8), :] = flux[f] - below
-        return 0
-
-    lax.fori_loop(0, ROWS // 8, along_z, 0, unroll=2)
-
-    def along_x(step, _):
-        column = pl.multiple_of(step * 8, 8)
-
-        def rows(f, i):
-            return pl.ds(pl.multiple_of(f * ROWS + i * NY + column, 8), 8)
-
-        def load(f, i):
-            if i < 0:
-                return x_low[pl.ds(pl.multiple_of((f * 3 + i + 3) * NY + column, 8), 8), :]
-            if i >= NX:
-                return x_high[pl.ds(pl.multiple_of((f * 3 + i - NX) * NY + column, 8), 8), :]
-            return state[rows(f, i), :]
-
-        def speed_at(i, q):
-            if 0 <= i < NX:
-                inverse, own = inverse_of[rows(0, i), :], sound[rows(0, i), :]
-            else:
-                inverse = reciprocal(q[0])
-                own = sound_of(q, inverse)
-            return jnp.abs(q[1]) * inverse + own
-
-        def store(i, values):
-            for f in range(5):
-                out[rows(f, i), :] = out[rows(f, i), :] + values[f]
-
-        sweep(load, speed_at, store, NX, 0)
-        return 0
-
-    lax.fori_loop(0, NY // 8, along_x, 0)
-
-    def along_y(step, _):
-        start = pl.multiple_of(step * 8, 8)
-
-        def rows(f, i):
-            return pl.ds(f * ROWS + start * NY + i, 8, stride=NY)
-
-        def load(f, i):
-            if i < 0:
-                return y_low[pl.ds(pl.multiple_of((f * 3 + i + 3) * NX + start, 8), 8), :]
-            if i >= NY:
-                return y_high[pl.ds(pl.multiple_of((f * 3 + i - NY) * NX + start, 8), 8), :]
-            return state[rows(f, i), :]
-
-        def speed_at(i, q):
-            if 0 <= i < NY:
-                inverse, own = inverse_of[rows(0, i), :], sound[rows(0, i), :]
-            else:
-                inverse = reciprocal(q[0])
-                own = sound_of(q, inverse)
-            return jnp.abs(q[2]) * inverse + own
-
-        def store(i, values):
-            for f in range(5):
-                out[rows(f, i), :] = out[rows(f, i), :] + values[f]
-
-        sweep(load, speed_at, store, NY, 1)
-        return 0
-
-    lax.fori_loop(0, NX // 8, along_y, 0)
-
     codes = jnp.concatenate([fine_pairs[...].astype(F32)] * 4, axis=1).T[0:32]
     spread = (iota((16, 128), 1) % 16 == iota((16, 128), 0)).astype(F32)
     used = fold_rows(
@@ -283,15 +211,124 @@
             count = count + jnp.where(each == plane, 1.0, 0.0)
         fine_uses[plane * 8 : plane * 8 + 8, :] = count
 
+    lane = iota((8, 128), 1)
+    device = lane % place[2] * place[3] + lane // place[2]
     for half in range(2):
         named = coarse_pairs[half * 8 : half * 8 + 8, :]
-        named = [jnp.broadcast_to(named[:, j : j + 1], (8, 128)) - 16 * lane for j in range(32)]
+        named = [jnp.broadcast_to(named[:, j : j + 1], (8, 128)) - 16 * device for j in range(32)]
         for lp in range(16):
             count = jnp.zeros((8, 128), F32)
             for each in named:
                 count = count + jnp.where(each == lp, 1.0, 0.0)
             row = (lp * 2 + half) * 8
             coarse_uses[row : row + 8, :] = count
+
+
+def along_z_kernel(turned, changes):
+    def column(step, _):
+        def load(f, i):
+            return turned[pl.ds(pl.multiple_of((f * 4 + step) * TALL, 8) + 8 + i, 8, stride=16), :]
+
+        def speed_at(i, q):
+            inverse = reciprocal(q[0])
+            return jnp.abs(q[3]) * inverse + sound_of(q, inverse)
+
+        def store(i, values):
+            for f in range(5):
+                changes[pl.ds(pl.multiple_of((f * 4 + step) * 128, 8) + i, 8, stride=16), :] = values[f]
+
+        sweep(load, speed_at, store, 16, 2)
+        return 0
+
+    lax.fori_loop(0, 4, column, 0)
+
+
+def along_x_kernel(place, state, x_one, x_two, inverse_of, sound, others, out, low, high):
+    def edges(f):
+        return state[f * ROWS : f * ROWS + NY, :], state[f * ROWS + ROWS - NY : f * ROWS + ROWS, :]
+
+    sides(x_one, x_two, low, high, place[0], place[2] - 1, edges, NY)
+
+    def column(step, _):
+        start = pl.multiple_of(step * 8, 8)
+
+        def rows(f, i):
+            return pl.ds(pl.multiple_of(f * ROWS + i * NY + start, 8), 8)
+
+        def load(f, i):
+            if i < 0:
+                return low[pl.ds(pl.multiple_of((f * 3 + i + 3) * NY + start, 8), 8), :]
+            if i >= NX:
+                return high[pl.ds(pl.multiple_of((f * 3 + i - NX) * NY + start, 8), 8), :]
+            return state[rows(f, i), :]
+
+        def speed_at(i, q):
+            if 0 <= i < NX:
+                at = pl.ds(i * PITCH + start, 8)
+                inverse, own = inverse_of[at, :], sound[at, :]
+            else:
+                inverse = reciprocal(q[0])
+                own = sound_of(q, inverse)
+            return jnp.abs(q[1]) * inverse + own
+
+        def store(i, values):
+            for f in range(5):
+                out[rows(f, i), :] = others[rows(f, i), :] + values[f]
+
+        sweep(load, speed_at, store, NX, 0)
+        return 0
+
+    lax.fori_loop(0, NY // 8, column, 0)
+
+
+def along_y_kernel(place, padded, y_one, y_two, inverse_of, sound, changes, out, low, high, by_y):
+    def edges(f):
+        return [padded[pl.ds(f * NX * PITCH + y, NX, stride=PITCH), :] for y in (0, NY - 1)]
+
+    sides(y_one, y_two, low, high, place[1], place[3] - 1, edges, NX)
+
+    def column(step, _):
+        start = pl.multiple_of(step * 8, 8)
+
+        def rows(f, i):
+            return pl.ds((f * NX + start) * PITCH + i, 8, stride=PITCH)
+
+        def load(f, i):
+            if i < 0:
+                return low[pl.ds(pl.multiple_of((f * 3 + i + 3) * NX + start, 8), 8), :]
+            if i >= NY:
+                return high[pl.ds(pl.multiple_of((f * 3 + i - NY) * NX + start, 8), 8), :]
+            return padded[rows(f, i), :]
+
+        def speed_at(i, q):
+            if 0 <= i < NY:
+                inverse, own = inverse_of[rows(0, i), :], sound[rows(0, i), :]
+            else:
+                inverse = reciprocal(q[0])
+                own = sound_of(q, inverse)
+            return jnp.abs(q[2]) * inverse + own
+
+        def store(i, values):
+            for f in range(5):
+                by_y[rows(f, i), :] = values[f]
+
+        for f in range(5):
+            for half in range(2):
+                block = pl.multiple_of(f * ROWS + (step * 2 + half) * 128, 128)
+                out[pl.ds(block, 128), :] = changes[pl.ds(block, 128), :].T
+        sweep(load, speed_at, store, NY, 1)
+        return 0
+
+    lax.fori_loop(0, NX // 8, column, 0)
+
+    def total(x, _):
+        for f in range(5):
+            for y in range(0, NY, 8):
+                row = pl.ds(pl.multiple_of(f * ROWS + x * NY + y, 8), 8)
+                out[row, :] = out[row, :] + by_y[pl.ds((f * NX + x) * PITCH + y, 8), :]
+        return 0
+
+    lax.fori_loop(0, NX, total, 0, unroll=2)
 
 
 def tensors(r, square):
@@ -327,12 +364,12 @@
     time_step = COURANT / jnp.max(rows[:, 64:128])
     moments = rows.T
     target_z = iota((8, 128), 0)
-    rx = 16.0 * (lane // 4 - morton).astype(F32)
+    rx = 16.0 * (lane % mortons - morton).astype(F32)
     coarse = []
     for half in range(2):
         totals = [jnp.zeros((8, 128), F32) for _ in range(9)]
         for lp in range(16):
-            ry = 16.0 * (lane % 4 * 2 + lp // 8 - (2 * octant + half)).astype(F32)
+            ry = 16.0 * (lane // mortons * 2 + lp // 8 - (2 * octant + half)).astype(F32)
             rz = 16.0 * (lp % 8 - target_z).astype(F32)
             own = [jnp.broadcast_to(moments[m * 16 + lp : m * 16 + lp + 1], (8, 128)) for m in range(4)]
             row = (lp * 2 + half) * 8
@@ -354,7 +391,7 @@
         for dx in (-1, 0, 1):
             at_x, at_y = morton + dx, octant + dy
             inside = (at_x >= 0) & (at_x < mortons) & (at_y >= 0) & (at_y < octs)
-            device = jnp.clip(at_x, 0, mortons - 1) * octs + jnp.clip(at_y, 0, octs - 1)
+            device = jnp.clip(at_y, 0, octs - 1) * mortons + jnp.clip(at_x, 0, mortons - 1)
             for m in range(4):
                 block.append(jnp.where(inside, got[pl.ds(device * SENT + m, 1), :], 0.0))
         blocks.append(jnp.concatenate(block + [jnp.zeros((4, 128), F32)], axis=0))
@@ -443,38 +480,38 @@
             new[4, row : row + 8, :] = moved[4] + time_step * gain
 
 
-def whole(count):
-    return [pl.BlockSpec(memory_space=pltpu.SMEM)] + [pl.BlockSpec(memory_space=pltpu.VMEM)] * count
-
-
-LIMIT = pltpu.CompilerParams(vmem_limit_bytes=48 * 1024 * 1024)
+VMEM = pl.BlockSpec(memory_space=pltpu.VMEM)
+SMEM = pl.BlockSpec(memory_space=pltpu.SMEM)
+LIMIT = pltpu.CompilerParams(vmem_limit_bytes=12 * 1024 * 1024)
+SMALL = pl.CostEstimate(flops=1000, bytes_accessed=1000, transcendentals=0)
 
 
 def shaped(*shape):
     return jax.ShapeDtypeStruct(shape, F32)
 
 
-def prepare(place, rows):
+def call(kernel, outs, scratch, *args):
     return pl.pallas_call(
-        prepare_kernel,
-        out_shape=[shaped(128 * SENT, 128), shaped(480, 128), shaped(480, 128), shaped(240, 128), shaped(240, 128)],
-        in_specs=whole(1),
-        out_specs=[pl.BlockSpec(memory_space=pltpu.VMEM)] * 5,
+        kernel,
+        out_shape=[shaped(rows, 128) for rows in outs],
+        in_specs=[SMEM if a.shape == (4,) else VMEM for a in args],
+        out_specs=[VMEM] * len(outs),
+        scratch_shapes=[pltpu.VMEM((rows, 128), F32) for rows in scratch],
         compiler_params=LIMIT,
-    )(place, rows)
-
-
-def diverge(place, rows, halos, fine_pairs, fine_count, coarse_pairs):
+        cost_estimate=SMALL,
+    )(*args)
+
+
+def moments_of(fields):
     return pl.pallas_call(
-        divergence_kernel,
-        out_shape=[shaped(5 * ROWS, 128), shaped(200, 128), shaped(256, 128)],
-        in_specs=whole(8),
-        out_specs=[pl.BlockSpec(memory_space=pltpu.VMEM)] * 3,
-        scratch_shapes=[pltpu.VMEM((ROWS, 128), F32)] * 2
-        + [pltpu.VMEM((480, 128), F32)] * 2
-        + [pltpu.VMEM((240, 128), F32)] * 2,
+        moments_kernel,
+        out_shape=shaped(128 * SENT, 128),
+        in_specs=[pl.BlockSpec(memory_space=pltpu.HBM)],
+        out_specs=VMEM,
+        scratch_shapes=[pltpu.VMEM((5, ROWS, 128), F32), pltpu.SemaphoreType.DMA((4,))],
         compiler_params=LIMIT,
-    )(place, rows, *halos, fine_pairs, fine_count, coarse_pairs)
+        cost_estimate=SMALL,
+    )(fields)
 
 
 def update(place, rows, twice, uses_fine, uses_coarse, got):
@@ -503,23 +540,37 @@
 def local(state, fine_pairs, fine_count, coarse_pairs):
     mortons, octs = lax.axis_size("morton"), lax.axis_size("oct")
     place = jnp.stack([lax.axis_index("morton"), lax.axis_index("oct"), mortons, octs]).astype(jnp.int32)
+    many = NX * PITCH
+
+    def swap(values, pair):
+        pairs = [(m, o) for m in range(mortons) for o in range(octs)]
+        index = lambda place: place[0] * octs + place[1]
+        return lax.ppermute(values, AXES, [(index(p), index(pair(*p))) for p in pairs])
+
+    def other(i):
+        return (i - 1 ^ 1) + 1
+
+    sent = moments_of(pltpu.with_memory_space_constraint(state.reshape(5, ROWS, 128), pltpu.HBM))
+    got = lax.all_to_all(sent.reshape(mortons * octs, 1, SENT * 128), AXES[::-1], 0, 0, tiled=True)
     rows = state.reshape(5 * ROWS, 128)
-    sent, x_one, x_two, y_one, y_two = prepare(place, rows)
-
-    def swap(values, axis, devices, first):
-        pairs = [(i, i + 1) for i in range(first, devices - 1, 2)]
-        return lax.ppermute(values, axis, pairs + [(j, i) for i, j in pairs])
-
-    halos = [
-        swap(x_one, "morton", mortons, 0),
-        swap(x_two, "morton", mortons, 1),
-        swap(y_one, "oct", octs, 0),
-        swap(y_two, "oct", octs, 1),
-    ]
-    got = lax.all_to_all(sent.reshape(mortons * octs, 1, SENT * 128), AXES, 0, 0, tiled=True)
-    twice, uses_fine, uses_coarse = diverge(
-        place, rows, halos, fine_pairs.reshape(128, 32), fine_count.reshape(8, 16), coarse_pairs.reshape(16, 32)
+    rows, _ = lax.optimization_barrier((rows, sent))
+    x_one, x_two, y_one, y_two, padded, inverse_of, sound = call(
+        split_kernel, [480, 480, 240, 240, 5 * many, many, many], [], place, rows
     )
+    y_one = swap(y_one, lambda m, o: (m, o ^ 1))
+    y_two = swap(y_two, lambda m, o: (m, other(o)) if 0 < o < octs - 1 else (m ^ 4, o))
+    x_one = swap(x_one, lambda m, o: (m ^ 1, o))
+    turned, uses_fine, uses_coarse = call(
+        turn_kernel, [20 * TALL, 200, 256], [],
+        place, rows, fine_pairs.reshape(128, 32), fine_count.reshape(8, 16), coarse_pairs.reshape(16, 32),
+    )
+    x_two = swap(x_two, lambda m, o: (other(m), o) if 0 < m < mortons - 1 else (m, o ^ 1))
+    (changes,) = call(along_z_kernel, [5 * ROWS], [], turned)
+    (twice,) = call(
+        along_y_kernel, [5 * ROWS], [240, 240, 5 * many],
+        place, padded, y_one, y_two, inverse_of, sound, changes,
+    )
+    (twice,) = call(along_x_kernel, [5 * ROWS], [480, 480], place, rows, x_one, x_two, inverse_of, sound, twice)
     new, gravity = update(place, rows, twice, uses_fine, uses_coarse, got.reshape(mortons * octs * SENT, 128))
     return new.reshape(state.shape), gravity.reshape(3, NX, NY, NZ)
 

time: 55.5 us -> 39.4 us (0.71)
  the two profiles are of different devices: /device:TPU:4 before, /device:TPU:5 now
where the time goes in v2:
time: 39.4 us; the launch traced here: 39.2 us
  starting transfers between devices  19.4 us (49%)
  Pallas kernels  16.5 us (42%)
  waiting for transfers between devices  2.51 us (6%)
  between operations  0.74 us (2%)
    all_to_all x1, starting transfers between devices, local(): lax.all_to_all(sent.reshape(mortons * octs, 1, SENT * 128), AXES[::-1], 0...  10.8 us
    pallas_call x5, Pallas kernels, call(): pl.pallas_call(kernel, out_shape=[shaped(rows, 128) for rows in outs], in...  10.2 us
    ppermute x4, starting transfers between devices, swap(): lax.ppermute(values, AXES, [(index(p), index(pair(*p))) for p in pairs])  8.57 us
    pallas_call x1, Pallas kernels, update(): pl.pallas_call(update_kernel, grid=(slabs,), out_shape=[shaped(5, ROWS, 1...  3.64 us
    pallas_call x1, Pallas kernels, moments_of(): pl.pallas_call(moments_kernel, out_shape=shaped(128 * SENT, 128), in_spec...  2.67 us
    ppermute x4, waiting for transfers between devices, swap(): lax.ppermute(values, AXES, [(index(p), index(pair(*p))) for p in pairs])  2.51 us
  transfers between devices with their start and end apart: 5, of which 1 were waited for; matrix products, arithmetic and copies ran while one was open for 0% of the time, Pallas kernels for 26%

profile of v2, /device:TPU:5, one launch (start us, length us, event | category | flops | bytes accessed | tf_op | source)
XLA Modules:
  0.0 39.2 jit_solution(3150827316069673752)
XLA Ops:
  0.6 0.0 copy-start
  0.6 2.7 %shard_map.59 = f32[640,128]{1,0:T(8,128)} custom-call(f32[5,512,128]{2,1,0:T(8,128)} %bitcast.13), custom_call_target="tpu_custom_call" | custom-call | flops 1000 | bytes 1000 | tf_op jit(solution)/shard_map/pallas_call | solution.py:506
  3.3 0.0 copy-start.1
  3.3 0.0 copy-start.2
  3.3 0.0 copy-start.3
  3.4 10.8 %all-to-all-start = ((f32[128,1,640]{2,1,0:T(1,128)}), f32[128,1,640]{2,1,0:T(1,128)S(1)}, u32[]{:S(2)}, u32[]{:S(2)}) async-start(f32[128,1,640]{2,1,0:T(1,128)} %bitcast.9), calls=%async_computation | async-start | bytes 655360 | tf_op jit(solution)/shard_map/all_to_all | solution.py:554
  14.2 0.1 pad_add_fusion.place
  14.3 0.0 copy-done
  14.3 0.8 %shard_map.60 = (f32[480,128]{1,0:T(8,128)S(1)}, f32[480,128]{1,0:T(8,128)S(1)}, f32[240,128]{1,0:T(8,128)S(1)}, f32[240,128]{1,0:T(8,128)S(1)}, f32[2640,128]{1...) custom-call(s32[4]{0:T(128)S(1)} %pad_add_fusion.place, f32[2560,128]{1,0:T(8,128)S(1)} %bitcast.14), custom_call_target="tpu_custom_call" | custom-call | flops 1000 | bytes 1000 | tf_op jit(solution)/shard_map/pallas_call | solution.py:494
  15.1 1.3 %collective-permute-start = (f32[480,128]{1,0:T(8,128)S(1)}, f32[480,128]{1,0:T(8,128)S(1)}, u32[]{:S(2)}, u32[]{:S(2)}) collective-permute-start(f32[480,128]{1,0:T(8,128)S(1)} %get-tuple-element.16), channel_id=1, source_target_pairs={{0,4},{1,5},{2,6},{3,7},{4,0},{5,1},{6,2},{7,3},{8,12},{9,13},{10,... | collective-permute-start | bytes 737288 | tf_op jit(solution)/shard_map/ppermute | solution.py:548
  16.3 4.7 %collective-permute-start.1 = (f32[480,128]{1,0:T(8,128)S(1)}, f32[480,128]{1,0:T(8,128)S(1)}, u32[]{:S(2)}, u32[]{:S(2)}) collective-permute-start(f32[480,128]{1,0:T(8,128)S(1)} %get-tuple-element.17), channel_id=1, source_target_pairs={{0,1},{1,0},{2,3},{3,2},{4,8},{5,9},{6,10},{7,11},{8,4},{9,5},{10,... | collective-permute-start | bytes 737288 | tf_op jit(solution)/shard_map/ppermute | solution.py:548
  21.0 0.9 %collective-permute-start.2 = (f32[240,128]{1,0:T(8,128)S(1)}, f32[240,128]{1,0:T(8,128)S(1)}, u32[]{:S(2)}, u32[]{:S(2)}) collective-permute-start(f32[240,128]{1,0:T(8,128)S(1)} %get-tuple-element.21), channel_id=1, source_target_pairs={{0,1},{1,0},{2,3},{3,2},{4,5},{5,4},{6,7},{7,6},{8,9},{9,8},{10,11... | collective-permute-start | bytes 368648 | tf_op jit(solution)/shard_map/ppermute | solution.py:548
  21.9 1.7 %collective-permute-start.3 = (f32[240,128]{1,0:T(8,128)S(1)}, f32[240,128]{1,0:T(8,128)S(1)}, u32[]{:S(2)}, u32[]{:S(2)}) collective-permute-start(f32[240,128]{1,0:T(8,128)S(1)} %get-tuple-element.22), channel_id=1, source_target_pairs={{0,16},{1,2},{2,1},{3,19},{4,20},{5,6},{6,5},{7,23},{8,24},{9,10},... | collective-permute-start | bytes 368648 | tf_op jit(solution)/shard_map/ppermute | solution.py:548
  23.6 0.0 copy-done.1
  23.6 0.0 copy-done.2
  23.6 0.0 copy-done.3
  23.6 2.1 %shard_map.61 = (f32[2880,128]{1,0:T(8,128)S(1)}, f32[200,128]{1,0:T(8,128)S(1)}, f32[256,128]{1,0:T(8,128)S(1)}) custom-call(s32[4]{0:T(128)S(1)} %pad_add_fusion.place, f32[2560,128]{1,0:T(8,128)S(1)} %bitcast.15, s32[128,32]{1,0:T(8,128)S(1)} %bitcast.20, s32[8,16]{1,0:T(8,128)S(1)} %bitcast.22, s32[16,32]{1,0:T(8,128)S(1)} %bitcast.21), custom_call_target="tpu_custom_call" | custom-call | flops 1000 | bytes 1000 | tf_op jit(solution)/shard_map/pallas_call | solution.py:494
  25.7 2.4 %shard_map.62.changes = f32[2560,128]{1,0:T(8,128)S(1)} custom-call(f32[2880,128]{1,0:T(8,128)S(1)} %get-tuple-element.23.turned), custom_call_target="tpu_custom_call" | custom-call | flops 1000 | bytes 1000 | tf_op jit(solution)/shard_map/pallas_call | solution.py:494
  28.1 0.0 collective-permute-done.2.y_one
  28.1 2.5 %collective-permute-done.3.y_two = f32[240,128]{1,0:T(8,128)S(1)} collective-permute-done((f32[240,128]{1,0:T(8,128)S(1)}, f32[240,128]{1,0:T(8,128)S(1)}, u32[]{:S(2)}, u32[]{:S(2)}) %collective-permute-start.3) | collective-permute-done | bytes 122912 | tf_op jit(solution)/shard_map/ppermute | solution.py:548
  30.6 2.5 %shard_map.63.others = f32[2560,128]{1,0:T(8,128)S(1)} custom-call(s32[4]{0:T(128)S(1)} %pad_add_fusion.place, f32[2640,128]{1,0:T(8,128)S(1)} %get-tuple-element.20.padded, f32[240,128]{1,0:T(8,128)S(1)} %collective-permute-done.2.y_one, f32[240,128]{1,0:T(8,128)S(1)} %collective-permute-done.3.y_two, f32[528,128]{1,0:T(8,128)S(1)} %get-tuple-element.18.inverse_of, ...), custom_call_target="tpu_custom_call" | custom-call | flops 1000 | bytes 1000 | tf_op jit(solution)/shard_map/pallas_call | solution.py:494
  33.1 0.0 collective-permute-done.x_one
  33.1 0.0 collective-permute-done.1.x_two
  33.2 2.4 %shard_map.64 = f32[2560,128]{1,0:T(8,128)S(1)} custom-call(s32[4]{0:T(128)S(1)} %pad_add_fusion.place, f32[2560,128]{1,0:T(8,128)S(1)} %bitcast.16, f32[480,128]{1,0:T(8,128)S(1)} %collective-permute-done.x_one, f32[480,128]{1,0:T(8,128)S(1)} %collective-permute-done.1.x_two, f32[528,128]{1,0:T(8,128)S(1)} %get-tuple-element.18.inverse_of, ...), custom_call_target="tpu_custom_call" | custom-call | flops 1000 | bytes 1000 | tf_op jit(solution)/shard_map/pallas_call | solution.py:494
  35.6 0.0 all-to-all-done
  35.6 3.6 %shard_map.65 = (f32[5,512,128]{2,1,0:T(8,128)}, f32[3,512,128]{2,1,0:T(8,128)}) custom-call(s32[4]{0:T(128)S(1)} %pad_add_fusion.place, f32[5,512,128]{2,1,0:T(8,128)S(1)} %bitcast.17, f32[5,512,128]{2,1,0:T(8,128)S(1)} %bitcast.18, f32[200,128]{1,0:T(8,128)S(1)} %get-tuple-element.24.uses_fine, f32[256,128]{1,0:T(8,128)S(1)} %get-tuple-element.25.uses_coarse, ...), custom_call_target="tpu_custom_call" | custom-call | tf_op jit(solution)/shard_map/pallas_call | solution.py:522
Async XLA Ops:
  0.6 13.6 %copy-start = (f32[5,16,32,128]{3,2,1,0:T(8,128)S(1)}, f32[5,16,32,128]{3,2,1,0:T(8,128)}, u32[]{:S(2)}) copy-start(f32[5,16,32,128]{3,2,1,0:T(8,128)} %param.4) | copy-start | bytes 3932164
  3.3 20.3 %copy-start.1 = (s32[2,4,16,32]{3,2,1,0:T(8,128)S(1)}, s32[2,4,16,32]{3,2,1,0:T(8,128)}, u32[]{:S(2)}) copy-start(s32[2,4,16,32]{3,2,1,0:T(8,128)} %param.5) | copy-start | bytes 49156
  3.3 20.3 %copy-start.2 = (s32[1,2,8,32]{3,2,1,0:T(8,128)S(1)}, s32[1,2,8,32]{3,2,1,0:T(8,128)}, u32[]{:S(2)}) copy-start(s32[1,2,8,32]{3,2,1,0:T(8,128)} %param.7) | copy-start | bytes 6148
  3.3 20.3 %copy-start.3 = (s32[2,4,16]{2,1,0:T(4,128)S(1)}, s32[2,4,16]{2,1,0:T(4,128)}, u32[]{:S(2)}) copy-start(s32[2,4,16]{2,1,0:T(4,128)} %param.6) | copy-start | bytes 1540
  3.4 32.2 %all-to-all-start = ((f32[128,1,640]{2,1,0:T(1,128)}), f32[128,1,640]{2,1,0:T(1,128)S(1)}, u32[]{:S(2)}, u32[]{:S(2)}) async-start(f32[128,1,640]{2,1,0:T(1,128)} %bitcast.9), calls=%async_computation | async-start | bytes 655360 | tf_op jit(solution)/shard_map/all_to_all | solution.py:554
  15.1 18.1 %collective-permute-start = (f32[480,128]{1,0:T(8,128)S(1)}, f32[480,128]{1,0:T(8,128)S(1)}, u32[]{:S(2)}, u32[]{:S(2)}) collective-permute-start(f32[480,128]{1,0:T(8,128)S(1)} %get-tuple-element.16), channel_id=1, source_target_pairs={{0,4},{1,5},{2,6},{3,7},{4,0},{5,1},{6,2},{7,3},{8,12},{9,13},{10,... | collective-permute-start | bytes 737288 | tf_op jit(solution)/shard_map/ppermute | solution.py:548
  16.3 16.8 %collective-permute-start.1 = (f32[480,128]{1,0:T(8,128)S(1)}, f32[480,128]{1,0:T(8,128)S(1)}, u32[]{:S(2)}, u32[]{:S(2)}) collective-permute-start(f32[480,128]{1,0:T(8,128)S(1)} %get-tuple-element.17), channel_id=1, source_target_pairs={{0,1},{1,0},{2,3},{3,2},{4,8},{5,9},{6,10},{7,11},{8,4},{9,5},{10,... | collective-permute-start | bytes 737288 | tf_op jit(solution)/shard_map/ppermute | solution.py:548
  21.0 7.1 %collective-permute-start.2 = (f32[240,128]{1,0:T(8,128)S(1)}, f32[240,128]{1,0:T(8,128)S(1)}, u32[]{:S(2)}, u32[]{:S(2)}) collective-permute-start(f32[240,128]{1,0:T(8,128)S(1)} %get-tuple-element.21), channel_id=1, source_target_pairs={{0,1},{1,0},{2,3},{3,2},{4,5},{5,4},{6,7},{7,6},{8,9},{9,8},{10,11... | collective-permute-start | bytes 368648 | tf_op jit(solution)/shard_map/ppermute | solution.py:548
  21.9 8.7 %collective-permute-start.3 = (f32[240,128]{1,0:T(8,128)S(1)}, f32[240,128]{1,0:T(8,128)S(1)}, u32[]{:S(2)}, u32[]{:S(2)}) collective-permute-start(f32[240,128]{1,0:T(8,128)S(1)} %get-tuple-element.22), channel_id=1, source_target_pairs={{0,16},{1,2},{2,1},{3,19},{4,20},{5,6},{6,5},{7,23},{8,24},{9,10},... | collective-permute-start | bytes 368648 | tf_op jit(solution)/shard_map/ppermute | solution.py:548

commit v3 on v2

v3 whole, which is shorter than its diff:
```python
import functools

import functools

import jax
import jax.numpy as jnp
from jax import lax
from jax.experimental import pallas as pl
from jax.experimental.pallas import tpu as pltpu
from jax.sharding import PartitionSpec as P

ADIABATIC = 5.0 / 3.0
COURANT = 0.2
GRAVITY = 1.0
AXES = ("morton", "oct")
F32 = jnp.float32
HIGH = lax.Precision.HIGHEST

NX, NY, NZ = 16, 32, 128
ROWS = NX * NY
PITCH = 33
TALL = 144
SENT = 5
SYM = ((0, 0), (0, 1), (0, 2), (1, 1), (1, 2), (2, 2))


def iota(shape, dim):
    return lax.broadcasted_iota(jnp.int32, shape, dim)


def sym(i, j):
    return SYM.index((min(i, j), max(i, j)))


def reciprocal(x):
    return pl.reciprocal(x, approx=True)


def sound_of(q, inverse):
    kinetic = (q[1] * q[1] + q[2] * q[2] + q[3] * q[3]) * inverse
    pressure = (2.0 / 3.0) * q[4] - (1.0 / 3.0) * kinetic
    square = ADIABATIC * pressure * inverse
    return square * lax.rsqrt(square)


def fold_rows(values, group):
    keep = iota(values.shape, 1) // group == iota(values.shape, 0)
    return jnp.sum(jnp.where(keep, values, 0.0), axis=0, keepdims=True)


def moments_kernel(
    place, state, sent, x_one, x_two, y_one, y_two, rows, near_sent, near_one, near_two, arrived, taken, written
):
    part = ROWS // 4
    copies = [
        pltpu.make_async_copy(
            state.at[:, pl.ds(c * part, part), :], rows.at[:, pl.ds(c * part, part), :], arrived.at[c]
        )
        for c in range(4)
    ]
    even, oct_even = place[0] % 2 == 0, place[1] % 2 == 0
    x_starts = (jnp.where(even, NX - 3, 0), jnp.where(even, 0, NX - 3))
    y_starts = (jnp.where(oct_even, NY - 3, 0), jnp.where(oct_even, 0, NY - 3))
    edges = [
        pltpu.make_async_copy(
            rows.at[f, pl.ds(pl.multiple_of(start * NY, 32), 96), :], out.at[pl.ds(f * 96, 96), :], taken.at[n, f]
        )
        for n, (out, start) in enumerate(((x_one, x_starts[0]), (x_two, x_starts[1])))
        for f in range(5)
    ]
    for copy in copies:
        copy.start()
    offset_y = iota((8, 128), 0).astype(F32) - 3.5
    fastest = jnp.zeros((8, 128), F32)
    sums, sums_x, sums_y = [], [], []
    for tx in range(2):
        totals, totals_x = [jnp.zeros((8, 128), F32)] * 4, [jnp.zeros((8, 128), F32)] * 4
        for half in range(2):
            copies[tx * 2 + half].wait()
            for x in range(half * 4, half * 4 + 4):
                for ty in range(4):
                    row = (tx * 8 + x) * NY + ty * 8
                    q = [rows[f, row : row + 8, :] for f in range(5)]
                    inverse = reciprocal(q[0])
                    speed_of_sound = sound_of(q, inverse)
                    largest = jnp.maximum(jnp.maximum(jnp.abs(q[1]), jnp.abs(q[2])), jnp.abs(q[3]))
                    fastest = jnp.maximum(fastest, largest * inverse + speed_of_sound)
                    totals[ty] = totals[ty] + q[0]
                    totals_x[ty] = totals_x[ty] + q[0] * (x - 3.5)
        for ty in range(4):
            sums.append(jnp.sum(totals[ty], axis=0, keepdims=True))
            sums_x.append(jnp.sum(totals_x[ty], axis=0, keepdims=True))
            sums_y.append(jnp.sum(totals[ty] * offset_y, axis=0, keepdims=True))
    for copy in edges:
        copy.start()
    for out, start in ((near_one, y_starts[0]), (near_two, y_starts[1])):
        for f in range(5):
            for x in range(NX):
                row = (f * NX + x) * 3
                out[row : row + 3, :] = rows[f, pl.ds(x * NY + start, 3), :]
    writes = [
        pltpu.make_async_copy(near, out, written.at[n])
        for n, (near, out) in enumerate(((near_one, y_one), (near_two, y_two), (near_sent, sent)))
    ]
    writes[0].start()
    writes[1].start()
    lines = jnp.concatenate(sums + sums_x + sums_y, axis=0)
    z = iota((128, 128), 0)
    pick = (z // 8 == iota((128, 128), 1) % 16).astype(F32)
    by_z = pick * ((z % 8).astype(F32) - 3.5)
    folded = jnp.dot(lines, pick, precision=HIGH, preferred_element_type=F32)
    folded_z = jnp.dot(lines[0:8], by_z, precision=HIGH, preferred_element_type=F32)
    mass = fold_rows(folded[0:8], 16)
    dipole = [fold_rows(folded[8:16], 16), fold_rows(folded[16:24], 16), fold_rows(folded_z, 16)]

    lane = iota((1, 128), 1)
    odd = [lane // 64, lane // 16 % 2, lane % 2]
    shifted = [d + 4.0 * (2 * o - 1).astype(F32) * mass for d, o in zip(dipole, odd, strict=True)]
    t = iota((128, 128), 0)
    parent = t // 32 % 2 * 8 + t % 16 // 2
    pick = (parent == iota((128, 128), 1) % 16).astype(F32)
    families = jnp.concatenate([mass] + shifted + [jnp.zeros((4, 128), F32)], axis=0)
    families = jnp.dot(families, pick, precision=HIGH, preferred_element_type=F32)
    last = jnp.where(lane < 64, fold_rows(families, 16), jnp.max(fastest))
    five = jnp.concatenate([mass] + dipole + [last], axis=0)
    many = jnp.concatenate([five] * 8, axis=0)
    for copy in range(16):
        near_sent[copy * 40 : copy * 40 + 40, :] = many
    writes[2].start()
    for copy in edges + writes:
        copy.wait()


def rise(before, here, after):
    value = 0.5 * here + (1.0 / 12.0) * (before - after)
    return jnp.minimum(jnp.maximum(value, jnp.minimum(here, 0.0)), jnp.maximum(here, 0.0))


def upper_and_lower(centre, up, down):
    most_up, most_down = jnp.abs(down + down), jnp.abs(up + up)
    upper = centre + jnp.minimum(jnp.maximum(up, -most_up), most_up)
    lower = centre + jnp.minimum(jnp.maximum(down, -most_down), most_down)
    return upper, lower


def flux_of(q, k):
    inverse = reciprocal(q[0])
    velocity = q[1 + k] * inverse
    kinetic = (q[1] * q[1] + q[2] * q[2] + q[3] * q[3]) * inverse
    pressure = (2.0 / 3.0) * q[4] - (1.0 / 3.0) * kinetic
    out = [q[1 + k]] + [q[1 + c] * velocity for c in range(3)] + [(q[4] + pressure) * velocity]
    out[1 + k] = out[1 + k] + pressure
    return out


def twice_flux(left, right, speed, k):
    from_left, from_right = flux_of(left, k), flux_of(right, k)
    return [
        (a + b) - speed * (r - l) for a, b, l, r in zip(from_left, from_right, left, right, strict=True)
    ]


def sweep(load, speed_at, store, length, k, beside=()):
    beside = list(beside)
    share = -(-len(beside) // length)
    last = [load(f, -1) for f in range(5)]
    steps = [[load(f, i + 1) - load(f, i) for f in range(5)] for i in (-3, -2)]
    cell = [load(f, -2) for f in range(5)], last
    ups = upper_old = speed_old = flux_old = None
    for i in range(-2, length + 1):
        ahead = [load(f, i + 2) for f in range(5)]
        steps.append([a - b for a, b in zip(ahead, cell[1], strict=True)])
        now = [rise(*each) for each in zip(*steps, strict=True)]
        if ups is not None:
            downs = [u - d for u, d in zip(ups, steps[0], strict=True)]
            pairs = [upper_and_lower(*each) for each in zip(cell[0], now, downs, strict=True)]
            upper, lower = [p[0] for p in pairs], [p[1] for p in pairs]
            speed = speed_at(i, cell[0])
            if upper_old is not None:
                flux = twice_flux(upper_old, lower, jnp.maximum(speed_old, speed), k)
                if flux_old is not None:
                    store(i - 1, [a - b for a, b in zip(flux, flux_old, strict=True)])
                flux_old = flux
            upper_old, speed_old = upper, speed
        for call in beside[:share]:
            call()
        beside = beside[share:]
        ups, cell, steps = now, (cell[1], ahead), steps[1:]
    for call in beside:
        call()


def sides(one, two, low, high, rank):
    even = rank % 2 == 0
    for row in range(0, one.shape[0], 8):
        a, b = one[row : row + 8, :], two[row : row + 8, :]
        low[row : row + 8, :] = jnp.where(even, b, a)
        high[row : row + 8, :] = jnp.where(even, a, b)


def inner_kernel(
    place, state, far_pairs, far_count, far_coarse, by_z, padded, inverse_of, sound, fine_uses, coarse_uses,
    turned_even, turned_odd, changes_even, changes_odd, fine_pairs, fine_count, coarse_pairs, arrived,
):
    turned, changes = (turned_even, turned_odd), (changes_even, changes_odd)

    def turn(block, f):
        into, base = turned[block % 2], f * TALL
        flat = state[f * ROWS + block * 128 : f * ROWS + block * 128 + 128, :].T
        into[base + 8 : base + 136, :] = flat
        into[base : base + 8, :] = jnp.broadcast_to(flat[0:1], (8, 128))
        into[base + 136 : base + 144, :] = jnp.broadcast_to(flat[127:128], (8, 128))

    def turn_back(block, f):
        flat = changes[block % 2][f * 128 : f * 128 + 128, :]
        by_z[f * ROWS + block * 128 : f * ROWS + block * 128 + 128, :] = flat.T

    def along_z(block, beside):
        source, into = turned[block % 2], changes[block % 2]

        def load(f, i):
            return source[pl.ds(f * TALL + 8 + i, 8, stride=16), :]

        def speed_at(i, q):
            inverse = reciprocal(q[0])
            return jnp.abs(q[3]) * inverse + sound_of(q, inverse)

        def store(i, values):
            for f in range(5):
                into[pl.ds(f * 128 + i, 8, stride=16), :] = values[f]

        sweep(load, speed_at, store, 16, 2, beside)

    reads = [
        pltpu.make_async_copy(source, into, arrived.at[n])
        for n, (source, into) in enumerate(
            ((far_pairs, fine_pairs), (far_count, fine_count), (far_coarse, coarse_pairs))
        )
    ]
    for copy in reads:
        copy.start()
    for f in range(5):
        turn(0, f)
    for block in range(4):
        beside = []
        for f in range(5):
            if block < 3:
                beside.append(functools.partial(turn, block + 1, f))
            if block > 0:
                beside.append(functools.partial(turn_back, block - 1, f))
        along_z(block, beside)
    for f in range(5):
        turn_back(3, f)
    for copy in reads:
        copy.wait()
    codes = jnp.concatenate([fine_pairs[...].astype(F32)] * 4, axis=1).T[0:32]
    spread = (iota((16, 128), 1) % 16 == iota((16, 128), 0)).astype(F32)
    used = fold_rows(
        jnp.dot(fine_count[...].astype(F32), spread, precision=HIGH, preferred_element_type=F32), 16
    )
    codes = jnp.where(iota((32, 128), 0).astype(F32) < used, codes, 1000.0)
    along = jnp.floor((codes + 0.5) * 0.04)
    plane = codes - 25.0 * along
    group = jnp.floor((plane + 0.5) * 0.2)
    one = jnp.left_shift(1, (6.0 * (plane - 5.0 * group)).astype(jnp.int32))
    ones = [jnp.where(group == g, one, 0) for g in range(5)]
    for g in range(5):
        lines = []
        for ox in range(5):
            hits = jnp.where(along == ox, ones[g], 0)
            hits = (hits[0:8] + hits[8:16]) + (hits[16:24] + hits[24:32])
            lines.append(jnp.sum(hits, axis=0, keepdims=True))
        fine_uses[g * 8 : g * 8 + 8, :] = jnp.concatenate(lines + [jnp.zeros((3, 128), jnp.int32)], axis=0)

    slot = iota((8, 128), 1)
    device = slot % place[2] * place[3] + slot // place[2]
    for half in range(2):
        named = coarse_pairs[half * 8 : half * 8 + 8, :]
        coded = named // 16 + named % 4 * (6 * 256) + named // 4 % 4 * 65536
        counts = [jnp.zeros((8, 128), jnp.int32) for _ in range(4)]
        for j in range(32):
            code = jnp.broadcast_to(coded[:, j : j + 1], (8, 128))
            one = jnp.where((code & 255) == device, jnp.left_shift(1, (code >> 8) & 255), 0)
            group = code >> 16
            counts = [each + jnp.where(group == g, one, 0) for g, each in enumerate(counts)]
        for g in range(4):
            coarse_uses[(g * 2 + half) * 8 : (g * 2 + half) * 8 + 8, :] = counts[g]
    for x in range(NX):
        for y in range(0, NY, 8):
            row = x * NY + y
            q = [state[f * ROWS + row : f * ROWS + row + 8, :] for f in range(5)]
            inverse = reciprocal(q[0])
            at = x * PITCH + y
            for f in range(5):
                padded[f * NX * PITCH + at : f * NX * PITCH + at + 8, :] = q[f]
            inverse_of[at : at + 8, :] = inverse
            sound[at : at + 8, :] = sound_of(q, inverse)


def tensors(r, square):
    root = lax.rsqrt(jnp.maximum(square, 1.0))
    cube = root * root * root
    three = 3.0 * cube * (root * root)
    scaled = [three * each for each in r]
    pull = [each * cube for each in r]
    tide = [scaled[i] * r[j] - cube if i == j else scaled[i] * r[j] for i, j in SYM]
    return pull, tide


def add_terms(totals, uses, r, square, mass, dipole):
    pull, tide = tensors(r, square)
    mass = uses * mass
    dipole = [uses * d for d in dipole]
    for i in range(3):
        term = mass * pull[i]
        for j in range(3):
            term = term - tide[sym(i, j)] * dipole[j]
        totals[i] = totals[i] + term
    for e in range(6):
        totals[3 + e] = totals[3 + e] + mass * tide[e]


def far_fields(place, uses_fine, uses_coarse, got, around):
    morton, octant = place[0], place[1]
    mortons, octs = place[2], place[3]
    lane = iota((8, 128), 1)
    lane_row = iota((1, 128), 1)

    rows = jnp.concatenate([got[pl.ds(g * 8 * SENT + 4, 8, stride=SENT), :] for g in range(16)], axis=0)
    time_step = COURANT / jnp.max(rows[:, 64:128])
    moments = rows.T
    target_z = iota((8, 128), 0)
    rx = 16.0 * (lane % mortons - morton).astype(F32)
    coarse = []
    for half in range(2):
        totals = [jnp.zeros((8, 128), F32) for _ in range(9)]
        for lp in range(16):
            ry = 16.0 * (lane // mortons * 2 + lp // 8 - (2 * octant + half)).astype(F32)
            rz = 16.0 * (lp % 8 - target_z).astype(F32)
            own = [jnp.broadcast_to(moments[m * 16 + lp : m * 16 + lp + 1], (8, 128)) for m in range(4)]
            row = (lp // 4 * 2 + half) * 8
            uses = ((uses_coarse[row : row + 8, :] >> (lp % 4 * 6)) & 63).astype(F32)
            add_terms(totals, uses, (rx, ry, rz), rx * rx + ry * ry + rz * rz, own[0], own[1:])
        coarse.append([jnp.sum(each, axis=1, keepdims=True) for each in totals])
    result = []
    for e in range(9):
        column = jnp.where(lane // 32 % 2 == 0, coarse[0][e], coarse[1][e])
        column = jnp.where(lane % 16 // 2 == iota((8, 128), 0), column, 0.0)
        result.append(jnp.sum(column, axis=0, keepdims=True))
    side = [4.0 * (2 * s - 1).astype(F32) for s in (lane_row // 64, lane_row // 16 % 2, lane_row % 2)]
    for i in range(3):
        for j in range(3):
            result[i] = result[i] + result[3 + sym(i, j)] * side[j]

    blocks = []
    for dy in (-1, 0, 1):
        block = []
        for dx in (-1, 0, 1):
            at_x, at_y = morton + dx, octant + dy
            inside = (at_x >= 0) & (at_x < mortons) & (at_y >= 0) & (at_y < octs)
            device = jnp.clip(at_y, 0, octs - 1) * mortons + jnp.clip(at_x, 0, mortons - 1)
            for m in range(4):
                block.append(jnp.where(inside, got[pl.ds(device * SENT + m, 1), :], 0.0))
        blocks.append(jnp.concatenate(block + [jnp.zeros((4, 128), F32)], axis=0))
    wide = iota((16, 128), 1)
    around[...] = jnp.zeros(around.shape, F32)
    for oy in range(-2, 3):
        if oy == 0:
            moved = blocks[1]
        else:
            moved = pltpu.roll(blocks[1], (-16 * oy) % 128, 1)
            if oy > 0:
                moved = jnp.where(wide // 16 % 4 + oy > 3, pltpu.roll(blocks[2], (64 - 16 * oy) % 128, 1), moved)
            else:
                moved = jnp.where(wide // 16 % 4 + oy < 0, pltpu.roll(blocks[0], (-64 - 16 * oy) % 128, 1), moved)
        swapped = pltpu.roll(moved, 64, 1)
        for m in range(4):
            low, own, high = [(moved[d * 4 + m : d * 4 + m + 1], swapped[d * 4 + m : d * 4 + m + 1]) for d in range(3)]
            first = lane_row < 64
            lines = [
                low[0], jnp.where(first, low[1], own[1]), own[0], jnp.where(first, own[1], high[1]), high[0],
            ]
            row = (m * 5 + oy + 2) * 8
            around[row : row + 5, :] = jnp.concatenate(lines, axis=0)
    totals = [jnp.zeros((8, 128), F32) for _ in range(9)]
    rx = 8.0 * (iota((8, 128), 0) - 2).astype(F32)
    square_x = rx * rx
    for oy in range(-2, 3):
        base = [around[(m * 5 + oy + 2) * 8 : (m * 5 + oy + 2) * 8 + 8, :] for m in range(4)]
        for oz in range(-2, 3):
            moved = base
            if oz:
                ok = (lane % 16 + oz >= 0) & (lane % 16 + oz < 16)
                moved = [jnp.where(ok, pltpu.roll(each, (-oz) % 128, 1), 0.0) for each in base]
            uses = ((uses_fine[(oy + 2) * 8 : (oy + 2) * 8 + 8, :] >> ((oz + 2) * 6)) & 63).astype(F32)
            add_terms(
                totals, uses, (rx, 8.0 * oy, 8.0 * oz),
                square_x + (64.0 * oy * oy + 64.0 * oz * oz), moved[0], moved[1:],
            )
    for e in range(9):
        result[e] = GRAVITY * (result[e] + jnp.sum(totals[e], axis=0, keepdims=True))
    return result, time_step


def along_y_kernel(place, padded, inverse_of, sound, y_one, y_two, by_z, out, low, high, by_y):
    sides(y_one, y_two, low, high, place[1])

    def edge(beyond, y):
        for f in range(5):
            cells = padded[pl.ds(f * NX * PITCH + y, NX, stride=PITCH), :]
            for layer in range(3):
                beyond[pl.ds(f * NX * 3 + layer, NX, stride=3), :] = cells

    pl.when(place[1] == 0)(lambda: edge(low, 0))
    pl.when(place[1] == place[3] - 1)(lambda: edge(high, NY - 1))

    def column(step, _):
        start = pl.multiple_of(step * 8, 8)

        def rows(f, i):
            return pl.ds((f * NX + start) * PITCH + i, 8, stride=PITCH)

        def load(f, i):
            if i < 0:
                return low[pl.ds((f * NX + start) * 3 + i + 3, 8, stride=3), :]
            if i >= NY:
                return high[pl.ds((f * NX + start) * 3 + i - NY, 8, stride=3), :]
            return padded[rows(f, i), :]

        def speed_at(i, q):
            if 0 <= i < NY:
                return jnp.abs(q[2]) * inverse_of[rows(0, i), :] + sound[rows(0, i), :]
            inverse = reciprocal(q[0])
            return jnp.abs(q[2]) * inverse + sound_of(q, inverse)

        def store(i, values):
            for f in range(5):
                by_y[rows(f, i), :] = values[f]

        sweep(load, speed_at, store, NY, 1)
        return 0

    lax.fori_loop(0, NX // 8, column, 0)

    def total(x, _):
        for f in range(5):
            for y in range(0, NY, 8):
                row = pl.ds(pl.multiple_of(f * ROWS + x * NY + y, 8), 8)
                out[row, :] = by_z[row, :] + by_y[pl.ds((f * NX + x) * PITCH + y, 8), :]
        return 0

    lax.fori_loop(0, NX, total, 0, unroll=2)


def outer_kernel(
    place, state, x_one, x_two, others, uses_fine, uses_coarse, got, new, gravity,
    low, high, around, field, made, pulls, written,
):
    sides(x_one, x_two, low, high, place[0])

    def edge(beyond, x):
        for f in range(5):
            cells = state[f * ROWS + x * NY : f * ROWS + x * NY + NY, :]
            for layer in range(3):
                beyond[(f * 3 + layer) * NY : (f * 3 + layer) * NY + NY, :] = cells

    pl.when(place[0] == 0)(lambda: edge(low, 0))
    pl.when(place[0] == place[2] - 1)(lambda: edge(high, NX - 1))
    result, time_step = far_fields(place, uses_fine, uses_coarse, got, around)
    half_step = 0.5 * time_step
    keep = iota((8, 128), 1) // 16 == iota((8, 128), 0)
    spread = (iota((128, 128), 0) % 16 == iota((128, 128), 1) // 8).astype(F32)
    lines = jnp.concatenate([jnp.where(keep, each, 0.0) for each in result], axis=0)
    lines = jnp.dot(lines, spread, precision=HIGH, preferred_element_type=F32)
    lines = [lines[e * 8 : e * 8 + 8] for e in range(9)]
    offset_z = (iota((8, 128), 1) % 8).astype(F32) - 3.5
    for i in range(3):
        field[i * 8 : i * 8 + 8, :] = lines[i] + lines[3 + sym(i, 2)] * offset_z
        field[(3 + i) * 8 : (3 + i) * 8 + 8, :] = lines[3 + sym(i, 0)]
        field[(6 + i) * 8 : (6 + i) * 8 + 8, :] = lines[3 + sym(i, 1)]
    offset_y = iota((8, 128), 0).astype(F32) - 3.5

    def writes(step):
        rows = pl.ds(pl.multiple_of(step * 8, 8), 8)
        return [
            pltpu.make_async_copy(made.at[:, :, rows, :], new.at[:, :, rows, :], written.at[0, step]),
            pltpu.make_async_copy(pulls.at[:, :, rows, :], gravity.at[:, :, rows, :], written.at[1, step]),
        ]

    def along_x(step, _):
        start = pl.multiple_of(step * 8, 8)

        def rows(f, i):
            return pl.ds(pl.multiple_of(f * ROWS + i * NY + start, 8), 8)

        def load(f, i):
            if i < 0:
                return low[pl.ds(pl.multiple_of((f * 3 + i + 3) * NY + start, 8), 8), :]
            if i >= NX:
                return high[pl.ds(pl.multiple_of((f * 3 + i - NX) * NY + start, 8), 8), :]
            return state[rows(f, i), :]

        lines = []
        for tx in range(2):
            at = [field[pl.ds(e * 8 + tx * 4 + step, 1), :] for e in range(9)]
            lines.append(([at[e] + at[6 + e] * offset_y for e in range(3)], at[3:6]))

        def store(i, values):
            base, slope = lines[i // 8]
            q = [state[rows(f, i), :] for f in range(5)]
            pull = [base[e] + slope[e] * (i % 8 - 3.5) for e in range(3)]
            moved = []
            for f in range(5):
                moved.append(q[f] - half_step * (values[f] + others[rows(f, i), :]))
            weight = time_step * q[0]
            gain = q[1] * pull[0] + q[2] * pull[1] + q[3] * pull[2]
            made[0, i, pl.ds(start, 8), :] = moved[0]
            for e in range(3):
                pulls[e, i, pl.ds(start, 8), :] = pull[e]
                made[1 + e, i, pl.ds(start, 8), :] = moved[1 + e] + weight * pull[e]
            made[4, i, pl.ds(start, 8), :] = moved[4] + time_step * gain

        def speed_at(i, q):
            inverse = reciprocal(q[0])
            return jnp.abs(q[1]) * inverse + sound_of(q, inverse)

        sweep(load, speed_at, store, NX, 0)
        for copy in writes(step):
            copy.start()
        return 0

    lax.fori_loop(0, NY // 8, along_x, 0)
    for step in range(NY // 8):
        for copy in writes(step):
            copy.wait()


VMEM = pl.BlockSpec(memory_space=pltpu.VMEM)
SMEM = pl.BlockSpec(memory_space=pltpu.SMEM)
FAR = pl.BlockSpec(memory_space=pltpu.HBM)
LIMIT = pltpu.CompilerParams(vmem_limit_bytes=12 * 1024 * 1024)
SMALL = pl.CostEstimate(flops=1000, bytes_accessed=1000, transcendentals=0)


def far(values):
    return pltpu.with_memory_space_constraint(values, pltpu.HBM)


def call(kernel, outs, scratch, *args, sources=None, far_outs=(), whole_numbers=()):
    shapes = [(o, 128) if isinstance(o, int) else o for o in outs]
    return pl.pallas_call(
        kernel,
        out_shape=[
            pltpu.HBM(s, F32) if n in far_outs else jax.ShapeDtypeStruct(s, jnp.int32 if n in whole_numbers else F32)
            for n, s in enumerate(shapes)
        ],
        in_specs=[SMEM] + (sources or [VMEM] * (len(args) - 1)),
        out_specs=[FAR if n in far_outs else VMEM for n in range(len(outs))],
        scratch_shapes=[pltpu.VMEM((s, 128), F32) if isinstance(s, int) else s for s in scratch],
        compiler_params=LIMIT,
        cost_estimate=SMALL,
    )(*args)


def local(state, fine_pairs, fine_count, coarse_pairs):
    mortons, octs = lax.axis_size("morton"), lax.axis_size("oct")
    place = jnp.stack([lax.axis_index("morton"), lax.axis_index("oct"), mortons, octs]).astype(jnp.int32)
    many = NX * PITCH

    def swap(values, pair):
        pairs = [(m, o) for m in range(mortons) for o in range(octs)]
        index = lambda place: place[0] * octs + place[1]
        return lax.ppermute(values, AXES, [(index(p), index(pair(*p))) for p in pairs])

    def other(i):
        return (i - 1 ^ 1) + 1

    block = pltpu.VMEM((5, ROWS, 128), F32)
    sent, x_one, x_two, y_one, y_two = call(
        moments_kernel, [128 * SENT, 480, 480, 240, 240],
        [block, 128 * SENT, 240, 240, pltpu.SemaphoreType.DMA((4,)), pltpu.SemaphoreType.DMA((2, 5)),
         pltpu.SemaphoreType.DMA((3,))],
        place, far(state.reshape(5, ROWS, 128)), sources=[FAR], far_outs=range(5),
    )
    got = lax.all_to_all(sent.reshape(mortons * octs, 1, SENT * 128), AXES[::-1], 0, 0, tiled=True)
    x_one = swap(x_one, lambda m, o: (m ^ 1, o))
    x_two = swap(x_two, lambda m, o: (other(m), o) if 0 < m < mortons - 1 else (m, o ^ 1))
    y_one = swap(y_one, lambda m, o: (m, o ^ 1))
    y_two = swap(y_two, lambda m, o: (m, other(o)) if 0 < o < octs - 1 else (m, octs - 1 - o))
    rows = state.reshape(5 * ROWS, 128)
    rows, sent = lax.optimization_barrier((rows, sent))
    by_z, padded, inverse_of, sound, uses_fine, uses_coarse = call(
        inner_kernel, [5 * ROWS, 5 * many, many, many, 40, 64],
        [5 * TALL, 5 * TALL, 640, 640, pltpu.VMEM((128, 32), jnp.int32), pltpu.VMEM((8, 16), jnp.int32),
         pltpu.VMEM((16, 32), jnp.int32), pltpu.SemaphoreType.DMA((3,))],
        place, rows, far(fine_pairs.reshape(128, 32)), far(fine_count.reshape(8, 16)), far(coarse_pairs.reshape(16, 32)),
        sources=[VMEM, FAR, FAR, FAR], whole_numbers=(4, 5),
    )
    (others,) = call(
        along_y_kernel, [5 * ROWS], [240, 240, 5 * many], place, padded, inverse_of, sound, y_one, y_two, by_z
    )
    return call(
        outer_kernel, [(5, NX, NY, NZ), (3, NX, NY, NZ)],
        [480, 480, 160, 72, pltpu.VMEM((5, NX, NY, NZ), F32), pltpu.VMEM((3, NX, NY, NZ), F32),
         pltpu.SemaphoreType.DMA((2, 4))],
        place, rows, x_one, x_two, others, uses_fine, uses_coarse, got.reshape(mortons * octs * SENT, 128),
        far_outs=range(2),
    )


def solution(mesh):
    in_specs = (
        P(None, "morton", "oct", None),
        P("morton", "oct", None, None),
        P("morton", "oct", None),
        P("morton", "oct", None, None),
    )
    out_specs = (P(None, "morton", "oct", None), P(None, "morton", "oct", None))
    return jax.shard_map(local, mesh=mesh, in_specs=in_specs, out_specs=out_specs, check_vma=False)
```

time: 39.4 us -> 38.7 us (0.982)
  Pallas kernels: 16.5 us -> 13.9 us
  waiting for transfers between devices: 2.51 us -> 4.46 us
    pallas_call x7 -> x4, Pallas kernels: 16.5 us -> 13.9 us  [call(): pl.pallas_call(kernel, out_shape=[pltpu.HBM(s, F32) if n in far_outs else...]
    ppermute x4, waiting for transfers between devices: 2.51 us -> 4.46 us  [swap(): lax.ppermute(values, AXES, [(index(p), index(pair(*p))) for p in pairs])]
  transfers between devices with their start and end apart: 5 -> 5, of which waited for: 1 -> 1; matrix products, arithmetic and copies ran while one was open for 0% -> 0% of each run, Pallas kernels for 26% -> 16%
where the time goes in v3:
time: 38.7 us; the launch traced here: 38.5 us
  starting transfers between devices  19.4 us (50%)
  Pallas kernels  13.9 us (36%)
  waiting for transfers between devices  4.46 us (12%)
  between operations  0.7 us (2%)
    pallas_call x4, Pallas kernels, call(): pl.pallas_call(kernel, out_shape=[pltpu.HBM(s, F32) if n in far_outs else...  13.9 us
    all_to_all x1, starting transfers between devices, local(): lax.all_to_all(sent.reshape(mortons * octs, 1, SENT * 128), AXES[::-1], 0...  10.8 us
    ppermute x4, starting transfers between devices, swap(): lax.ppermute(values, AXES, [(index(p), index(pair(*p))) for p in pairs])  8.57 us
    ppermute x4, waiting for transfers between devices, swap(): lax.ppermute(values, AXES, [(index(p), index(pair(*p))) for p in pairs])  4.46 us
  transfers between devices with their start and end apart: 5, of which 1 were waited for; matrix products, arithmetic and copies ran while one was open for 0% of the time, Pallas kernels for 16%

profile of v3, /device:TPU:5, one launch (start us, length us, event | category | flops | bytes accessed | tf_op | source)
XLA Modules:
  0.0 38.5 jit_solution(10006731167629880257)
XLA Ops:
  0.6 0.0 copy-start
  0.6 0.1 pad_add_fusion.place
  0.7 3.2 %shard_map.59 = (f32[640,128]{1,0:T(8,128)}, f32[480,128]{1,0:T(8,128)}, f32[480,128]{1,0:T(8,128)}, f32[240,128]{1,0:T(8,128)}, f32[240,128]{1,0:T(8,128)}) custom-call(s32[4]{0:T(128)S(1)} %pad_add_fusion.place, f32[5,512,128]{2,1,0:T(8,128)} %bitcast.9), custom_call_target="tpu_custom_call" | custom-call | flops 1000 | bytes 1000 | tf_op jit(solution)/shard_map/pallas_call | solution.py:551
  4.0 10.8 %all-to-all-start = ((f32[128,1,640]{2,1,0:T(1,128)}), f32[128,1,640]{2,1,0:T(1,128)S(1)}, u32[]{:S(2)}, u32[]{:S(2)}) async-start(f32[128,1,640]{2,1,0:T(1,128)} %bitcast.13), calls=%async_computation | async-start | bytes 655360 | tf_op jit(solution)/shard_map/all_to_all | solution.py:585
  14.8 1.3 %collective-permute-start = (f32[480,128]{1,0:T(8,128)}, f32[480,128]{1,0:T(8,128)S(1)}, u32[]{:S(2)}, u32[]{:S(2)}) collective-permute-start(f32[480,128]{1,0:T(8,128)} %get-tuple-element.16), channel_id=1, source_target_pairs={{0,4},{1,5},{2,6},{3,7},{4,0},{5,1},{6,2},{7,3},{8,12},{9,13},{10,... | collective-permute-start | bytes 737288 | tf_op jit(solution)/shard_map/ppermute | solution.py:573
  16.1 4.7 %collective-permute-start.1 = (f32[480,128]{1,0:T(8,128)}, f32[480,128]{1,0:T(8,128)S(1)}, u32[]{:S(2)}, u32[]{:S(2)}) collective-permute-start(f32[480,128]{1,0:T(8,128)} %get-tuple-element.17), channel_id=1, source_target_pairs={{0,1},{1,0},{2,3},{3,2},{4,8},{5,9},{6,10},{7,11},{8,4},{9,5},{10,... | collective-permute-start | bytes 737288 | tf_op jit(solution)/shard_map/ppermute | solution.py:573
  20.7 0.9 %collective-permute-start.2 = (f32[240,128]{1,0:T(8,128)}, f32[240,128]{1,0:T(8,128)S(1)}, u32[]{:S(2)}, u32[]{:S(2)}) collective-permute-start(f32[240,128]{1,0:T(8,128)} %get-tuple-element.21), channel_id=1, source_target_pairs={{0,1},{1,0},{2,3},{3,2},{4,5},{5,4},{6,7},{7,6},{8,9},{9,8},{10,11... | collective-permute-start | bytes 368648 | tf_op jit(solution)/shard_map/ppermute | solution.py:573
  21.7 1.7 %collective-permute-start.3 = (f32[240,128]{1,0:T(8,128)}, f32[240,128]{1,0:T(8,128)S(1)}, u32[]{:S(2)}, u32[]{:S(2)}) collective-permute-start(f32[240,128]{1,0:T(8,128)} %get-tuple-element.22), channel_id=1, source_target_pairs={{0,3},{1,2},{2,1},{3,0},{4,7},{5,6},{6,5},{7,4},{8,11},{9,10},{10,... | collective-permute-start | bytes 368648 | tf_op jit(solution)/shard_map/ppermute | solution.py:573
  23.4 0.0 copy-done
  23.4 3.8 %shard_map.60 = (f32[2560,128]{1,0:T(8,128)S(1)}, f32[2640,128]{1,0:T(8,128)S(1)}, f32[528,128]{1,0:T(8,128)S(1)}, f32[528,128]{1,0:T(8,128)S(1)}, s32[40,128]{1,0:T(8,128)S(1)}, /*index=5*/s32[64,128]{1,0:T(8,128)S(1)}) custom-call(s32[4]{0:T(128)S(1)} %pad_add_fusion.place, f32[2560,128]{1,0:T(8,128)S(1)} %bitcast.10, s32[128,32]{1,0:T(8,128)} %bitcast.14, ...), custom_call_target="tpu_custom_call" | custom-call | flops 1000 | bytes 1000 | tf_op jit(solution)/shard_map/pallas_call | solution.py:551
  27.1 0.0 collective-permute-done.2.y_one
  27.2 4.5 %collective-permute-done.3.y_two = f32[240,128]{1,0:T(8,128)S(1)} collective-permute-done((f32[240,128]{1,0:T(8,128)}, f32[240,128]{1,0:T(8,128)S(1)}, u32[]{:S(2)}, u32[]{:S(2)}) %collective-permute-start.3) | collective-permute-done | bytes 122912 | tf_op jit(solution)/shard_map/ppermute | solution.py:573
  31.6 2.3 %shard_map.61.others = f32[2560,128]{1,0:T(8,128)S(1)} custom-call(s32[4]{0:T(128)S(1)} %pad_add_fusion.place, f32[2640,128]{1,0:T(8,128)S(1)} %get-tuple-element.18.padded, f32[528,128]{1,0:T(8,128)S(1)} %get-tuple-element.19.inverse_of, f32[528,128]{1,0:T(8,128)S(1)} %get-tuple-element.20.sound, f32[240,128]{1,0:T(8,128)S(1)} %collective-permute-done.2.y_one, ...), custom_call_target="tpu_custom_call" | custom-call | flops 1000 | bytes 1000 | tf_op jit(solution)/shard_map/pallas_call | solution.py:551
  33.9 0.0 collective-permute-done.x_one
  34.0 0.0 collective-permute-done.1.x_two
  34.0 0.0 all-to-all-done
  34.0 4.6 %shard_map.62 = (f32[5,16,32,128]{3,2,1,0:T(8,128)}, f32[3,16,32,128]{3,2,1,0:T(8,128)}) custom-call(s32[4]{0:T(128)S(1)} %pad_add_fusion.place, f32[2560,128]{1,0:T(8,128)S(1)} %bitcast.11, f32[480,128]{1,0:T(8,128)S(1)} %collective-permute-done.x_one, f32[480,128]{1,0:T(8,128)S(1)} %collective-permute-done.1.x_two, f32[2560,128]{1,0:T(8,128)S(1)} %shard_map.61.others, ...), custom_call_target="tpu_custom_call" | custom-call | flops 1000 | bytes 1000 | tf_op jit(solution)/shard_map/pallas_call | solution.py:551
Async XLA Ops:
  0.6 22.7 %copy-start = (f32[5,16,32,128]{3,2,1,0:T(8,128)S(1)}, f32[5,16,32,128]{3,2,1,0:T(8,128)}, u32[]{:S(2)}) copy-start(f32[5,16,32,128]{3,2,1,0:T(8,128)} %param.4) | copy-start | bytes 3932164
  4.0 30.0 %all-to-all-start = ((f32[128,1,640]{2,1,0:T(1,128)}), f32[128,1,640]{2,1,0:T(1,128)S(1)}, u32[]{:S(2)}, u32[]{:S(2)}) async-start(f32[128,1,640]{2,1,0:T(1,128)} %bitcast.13), calls=%async_computation | async-start | bytes 655360 | tf_op jit(solution)/shard_map/all_to_all | solution.py:585
  14.8 19.2 %collective-permute-start = (f32[480,128]{1,0:T(8,128)}, f32[480,128]{1,0:T(8,128)S(1)}, u32[]{:S(2)}, u32[]{:S(2)}) collective-permute-start(f32[480,128]{1,0:T(8,128)} %get-tuple-element.16), channel_id=1, source_target_pairs={{0,4},{1,5},{2,6},{3,7},{4,0},{5,1},{6,2},{7,3},{8,12},{9,13},{10,... | collective-permute-start | bytes 737288 | tf_op jit(solution)/shard_map/ppermute | solution.py:573
  16.1 17.9 %collective-permute-start.1 = (f32[480,128]{1,0:T(8,128)}, f32[480,128]{1,0:T(8,128)S(1)}, u32[]{:S(2)}, u32[]{:S(2)}) collective-permute-start(f32[480,128]{1,0:T(8,128)} %get-tuple-element.17), channel_id=1, source_target_pairs={{0,1},{1,0},{2,3},{3,2},{4,8},{5,9},{6,10},{7,11},{8,4},{9,5},{10,... | collective-permute-start | bytes 737288 | tf_op jit(solution)/shard_map/ppermute | solution.py:573
  20.7 6.4 %collective-permute-start.2 = (f32[240,128]{1,0:T(8,128)}, f32[240,128]{1,0:T(8,128)S(1)}, u32[]{:S(2)}, u32[]{:S(2)}) collective-permute-start(f32[240,128]{1,0:T(8,128)} %get-tuple-element.21), channel_id=1, source_target_pairs={{0,1},{1,0},{2,3},{3,2},{4,5},{5,4},{6,7},{7,6},{8,9},{9,8},{10,11... | collective-permute-start | bytes 368648 | tf_op jit(solution)/shard_map/ppermute | solution.py:573
  21.7 9.9 %collective-permute-start.3 = (f32[240,128]{1,0:T(8,128)}, f32[240,128]{1,0:T(8,128)S(1)}, u32[]{:S(2)}, u32[]{:S(2)}) collective-permute-start(f32[240,128]{1,0:T(8,128)} %get-tuple-element.22), channel_id=1, source_target_pairs={{0,3},{1,2},{2,1},{3,0},{4,7},{5,6},{6,5},{7,4},{8,11},{9,10},{10,... | collective-permute-start | bytes 368648 | tf_op jit(solution)/shard_map/ppermute | solution.py:573

commit v4 on v3

--- a/solution.py
+++ b/solution.py
@@ -20,6 +20,7 @@
 ROWS = NX * NY
 PITCH = 33
 TALL = 144
+RIM = 17
 SENT = 5
 SYM = ((0, 0), (0, 1), (0, 2), (1, 1), (1, 2), (2, 2))
 
@@ -59,7 +60,7 @@
         for c in range(4)
     ]
     even, oct_even = place[0] % 2 == 0, place[1] % 2 == 0
-    x_starts = (jnp.where(even, NX - 3, 0), jnp.where(even, 0, NX - 3))
+    x_starts = (jnp.where(even, 0, NX - 3), jnp.where(even, NX - 3, 0))
     y_starts = (jnp.where(oct_even, NY - 3, 0), jnp.where(oct_even, 0, NY - 3))
     edges = [
         pltpu.make_async_copy(
@@ -160,14 +161,14 @@
     ]
 
 
-def sweep(load, speed_at, store, length, k, beside=()):
+def sweep(load, speed_at, store, begin, end, k, beside=()):
     beside = list(beside)
-    share = -(-len(beside) // length)
-    last = [load(f, -1) for f in range(5)]
-    steps = [[load(f, i + 1) - load(f, i) for f in range(5)] for i in (-3, -2)]
-    cell = [load(f, -2) for f in range(5)], last
+    share = -(-len(beside) // (end - begin))
+    start = [[load(f, begin + i) for f in range(5)] for i in (-3, -2, -1)]
+    steps = [[b - a for a, b in zip(start[i], start[i + 1], strict=True)] for i in range(2)]
+    cell = start[1], start[2]
     ups = upper_old = speed_old = flux_old = None
-    for i in range(-2, length + 1):
+    for i in range(begin - 2, end + 1):
         ahead = [load(f, i + 2) for f in range(5)]
         steps.append([a - b for a, b in zip(ahead, cell[1], strict=True)])
         now = [rise(*each) for each in zip(*steps, strict=True)]
@@ -199,8 +200,9 @@
 
 
 def inner_kernel(
-    place, state, far_pairs, far_count, far_coarse, by_z, padded, inverse_of, sound, fine_uses, coarse_uses,
-    turned_even, turned_odd, changes_even, changes_odd, fine_pairs, fine_count, coarse_pairs, arrived,
+    place, state, far_pairs, far_count, far_coarse, out, fine_uses, coarse_uses,
+    turned_even, turned_odd, changes_even, changes_odd, padded, inverse_of, sound, by_y,
+    fine_pairs, fine_count, coarse_pairs, arrived,
 ):
     turned, changes = (turned_even, turned_odd), (changes_even, changes_odd)
 
@@ -213,7 +215,7 @@
 
     def turn_back(block, f):
         flat = changes[block % 2][f * 128 : f * 128 + 128, :]
-        by_z[f * ROWS + block * 128 : f * ROWS + block * 128 + 128, :] = flat.T
+        out[f * ROWS + block * 128 : f * ROWS + block * 128 + 128, :] = flat.T
 
     def along_z(block, beside):
         source, into = turned[block % 2], changes[block % 2]
@@ -229,7 +231,7 @@
             for f in range(5):
                 into[pl.ds(f * 128 + i, 8, stride=16), :] = values[f]
 
-        sweep(load, speed_at, store, 16, 2, beside)
+        sweep(load, speed_at, store, 0, 16, 2, beside)
 
     reads = [
         pltpu.make_async_copy(source, into, arrived.at[n])
@@ -295,6 +297,54 @@
                 padded[f * NX * PITCH + at : f * NX * PITCH + at + 8, :] = q[f]
             inverse_of[at : at + 8, :] = inverse
             sound[at : at + 8, :] = sound_of(q, inverse)
+
+    def along_x(step, _):
+        start = pl.multiple_of(step * 8, 8)
+
+        def rows(f, i):
+            return pl.ds(pl.multiple_of(f * ROWS + i * NY + start, 8), 8)
+
+        def speed_at(i, q):
+            at = pl.ds(i * PITCH + start, 8)
+            return jnp.abs(q[1]) * inverse_of[at, :] + sound[at, :]
+
+        def store(i, values):
+            for f in range(5):
+                out[rows(f, i), :] = out[rows(f, i), :] + values[f]
+
+        sweep(lambda f, i: state[rows(f, i), :], speed_at, store, 3, NX - 3, 0)
+        return 0
+
+    lax.fori_loop(0, NY // 8, along_x, 0)
+
+    def along_y(step, _):
+        start = pl.multiple_of(step * 8, 8)
+
+        def rows(f, i):
+            return pl.ds((f * NX + start) * PITCH + i, 8, stride=PITCH)
+
+        def speed_at(i, q):
+            return jnp.abs(q[2]) * inverse_of[rows(0, i), :] + sound[rows(0, i), :]
+
+        def store(i, values):
+            for f in range(5):
+                by_y[rows(f, i), :] = values[f]
+
+        for i in (0, 1, 2, NY - 3, NY - 2, NY - 1):
+            store(i, [jnp.zeros((8, 128), F32)] * 5)
+        sweep(lambda f, i: padded[rows(f, i), :], speed_at, store, 3, NY - 3, 1)
+        return 0
+
+    lax.fori_loop(0, NX // 8, along_y, 0)
+
+    def total(x, _):
+        for f in range(5):
+            for y in range(0, NY, 8):
+                row = pl.ds(pl.multiple_of(f * ROWS + x * NY + y, 8), 8)
+                out[row, :] = out[row, :] + by_y[pl.ds((f * NX + x) * PITCH + y, 8), :]
+        return 0
+
+    lax.fori_loop(0, NX, total, 0, unroll=2)
 
 
 def tensors(r, square):
@@ -402,70 +452,96 @@
     return result, time_step
 
 
-def along_y_kernel(place, padded, inverse_of, sound, y_one, y_two, by_z, out, low, high, by_y):
-    sides(y_one, y_two, low, high, place[1])
-
-    def edge(beyond, y):
-        for f in range(5):
-            cells = padded[pl.ds(f * NX * PITCH + y, NX, stride=PITCH), :]
-            for layer in range(3):
-                beyond[pl.ds(f * NX * 3 + layer, NX, stride=3), :] = cells
-
-    pl.when(place[1] == 0)(lambda: edge(low, 0))
-    pl.when(place[1] == place[3] - 1)(lambda: edge(high, NY - 1))
-
-    def column(step, _):
-        start = pl.multiple_of(step * 8, 8)
-
-        def rows(f, i):
-            return pl.ds((f * NX + start) * PITCH + i, 8, stride=PITCH)
-
-        def load(f, i):
-            if i < 0:
-                return low[pl.ds((f * NX + start) * 3 + i + 3, 8, stride=3), :]
-            if i >= NY:
-                return high[pl.ds((f * NX + start) * 3 + i - NY, 8, stride=3), :]
-            return padded[rows(f, i), :]
-
-        def speed_at(i, q):
-            if 0 <= i < NY:
-                return jnp.abs(q[2]) * inverse_of[rows(0, i), :] + sound[rows(0, i), :]
-            inverse = reciprocal(q[0])
-            return jnp.abs(q[2]) * inverse + sound_of(q, inverse)
-
-        def store(i, values):
-            for f in range(5):
-                by_y[rows(f, i), :] = values[f]
-
-        sweep(load, speed_at, store, NY, 1)
-        return 0
-
-    lax.fori_loop(0, NX // 8, column, 0)
-
-    def total(x, _):
-        for f in range(5):
-            for y in range(0, NY, 8):
-                row = pl.ds(pl.multiple_of(f * ROWS + x * NY + y, 8), 8)
-                out[row, :] = by_z[row, :] + by_y[pl.ds((f * NX + x) * PITCH + y, 8), :]
-        return 0
-
-    lax.fori_loop(0, NX, total, 0, unroll=2)
-
-
 def outer_kernel(
-    place, state, x_one, x_two, others, uses_fine, uses_coarse, got, new, gravity,
-    low, high, around, field, made, pulls, written,
+    place, state, inner, x_one, x_two, far_y_one, far_y_two, uses_fine, uses_coarse, got, new, gravity,
+    y_one, y_two, x_low, x_high, y_low, y_high, rims, by_x, by_y, around, field, made, pulls, arrived, written,
 ):
-    sides(x_one, x_two, low, high, place[0])
-
-    def edge(beyond, x):
+    reads = [
+        pltpu.make_async_copy(far_y_one, y_one, arrived.at[0]),
+        pltpu.make_async_copy(far_y_two, y_two, arrived.at[1]),
+    ]
+    for copy in reads:
+        copy.start()
+    sides(x_two, x_one, x_low, x_high, place[0])
+
+    def x_edge(beyond, x):
         for f in range(5):
             cells = state[f * ROWS + x * NY : f * ROWS + x * NY + NY, :]
             for layer in range(3):
                 beyond[(f * 3 + layer) * NY : (f * 3 + layer) * NY + NY, :] = cells
 
-    pl.when(place[0] == 0)(lambda: edge(low, 0))
-    pl.when(place[0] == place[2] - 1)(lambda: edge(high, NX - 1))
+    pl.when(place[0] == 0)(lambda: x_edge(x_low, 0))
+    pl.when(place[0] == place[2] - 1)(lambda: x_edge(x_high, NX - 1))
+
+    def speed_of(k):
+        def speed_at(i, q):
+            inverse = reciprocal(q[0])
+            return jnp.abs(q[1 + k]) * inverse + sound_of(q, inverse)
+
+        return speed_at
+
+    def along_x(step, _):
+        start = pl.multiple_of(step * 8, 8)
+
+        def load(f, i):
+            if i < 0:
+                return x_low[pl.ds(pl.multiple_of((f * 3 + i + 3) * NY + start, 8), 8), :]
+            if i >= NX:
+                return x_high[pl.ds(pl.multiple_of((f * 3 + i - NX) * NY + start, 8), 8), :]
+            return state[pl.ds(pl.multiple_of(f * ROWS + i * NY + start, 8), 8), :]
+
+        def store(i, values):
+            for f in range(5):
+                by_x[pl.ds(pl.multiple_of((f * 6 + (i if i < 3 else i - 10)) * NY + start, 8), 8), :] = values[f]
+
+        sweep(load, speed_of(0), store, 0, 3, 0)
+        sweep(load, speed_of(0), store, NX - 3, NX, 0)
+        return 0
+
+    lax.fori_loop(0, NY // 8, along_x, 0)
+
+    for f in range(5):
+        for x in range(NX):
+            for side, y in ((0, 0), (8, NY - 8)):
+                row = (f * NX + x) * RIM + side
+                rims[row : row + 8, :] = state[f * ROWS + x * NY + y : f * ROWS + x * NY + y + 8, :]
+                by_y[row : row + 8, :] = jnp.zeros((8, 128), F32)
+    for copy in reads:
+        copy.wait()
+    sides(y_one, y_two, y_low, y_high, place[1])
+
+    def y_edge(beyond, row):
+        for f in range(5):
+            cells = rims[pl.ds(f * NX * RIM + row, NX, stride=RIM), :]
+            for layer in range(3):
+                beyond[pl.ds(f * NX * 3 + layer, NX, stride=3), :] = cells
+
+    pl.when(place[1] == 0)(lambda: y_edge(y_low, 0))
+    pl.when(place[1] == place[3] - 1)(lambda: y_edge(y_high, 15))
+
+    def along_y(step, _):
+        start = pl.multiple_of(step * 8, 8)
+
+        def rows(f, i):
+            return pl.ds((f * NX + start) * RIM + (i if i < 8 else i - 16), 8, stride=RIM)
+
+        def load(f, i):
+            if i < 0:
+                return y_low[pl.ds((f * NX + start) * 3 + i + 3, 8, stride=3), :]
+            if i >= NY:
+                return y_high[pl.ds((f * NX + start) * 3 + i - NY, 8, stride=3), :]
+            return rims[rows(f, i), :]
+
+        def store(i, values):
+            for f in range(5):
+                by_y[rows(f, i), :] = values[f]
+
+        sweep(load, speed_of(1), store, 0, 3, 1)
+        sweep(load, speed_of(1), store, NY - 3, NY, 1)
+        return 0
+
+    lax.fori_loop(0, NX // 8, along_y, 0)
+
     result, time_step = far_fields(place, uses_fine, uses_coarse, got, around)
     half_step = 0.5 * time_step
     keep = iota((8, 128), 1) // 16 == iota((8, 128), 0)
@@ -480,58 +556,45 @@
         field[(6 + i) * 8 : (6 + i) * 8 + 8, :] = lines[3 + sym(i, 1)]
     offset_y = iota((8, 128), 0).astype(F32) - 3.5
 
-    def writes(step):
-        rows = pl.ds(pl.multiple_of(step * 8, 8), 8)
+    def writes(part):
+        rows = pl.ds(part * 4, 4)
         return [
-            pltpu.make_async_copy(made.at[:, :, rows, :], new.at[:, :, rows, :], written.at[0, step]),
-            pltpu.make_async_copy(pulls.at[:, :, rows, :], gravity.at[:, :, rows, :], written.at[1, step]),
+            pltpu.make_async_copy(made.at[:, rows, :, :], new.at[:, rows, :, :], written.at[0, part]),
+            pltpu.make_async_copy(pulls.at[:, rows, :, :], gravity.at[:, rows, :, :], written.at[1, part]),
         ]
 
-    def along_x(step, _):
-        start = pl.multiple_of(step * 8, 8)
-
-        def rows(f, i):
-            return pl.ds(pl.multiple_of(f * ROWS + i * NY + start, 8), 8)
-
-        def load(f, i):
-            if i < 0:
-                return low[pl.ds(pl.multiple_of((f * 3 + i + 3) * NY + start, 8), 8), :]
-            if i >= NX:
-                return high[pl.ds(pl.multiple_of((f * 3 + i - NX) * NY + start, 8), 8), :]
-            return state[rows(f, i), :]
-
-        lines = []
-        for tx in range(2):
-            at = [field[pl.ds(e * 8 + tx * 4 + step, 1), :] for e in range(9)]
-            lines.append(([at[e] + at[6 + e] * offset_y for e in range(3)], at[3:6]))
-
-        def store(i, values):
-            base, slope = lines[i // 8]
-            q = [state[rows(f, i), :] for f in range(5)]
-            pull = [base[e] + slope[e] * (i % 8 - 3.5) for e in range(3)]
+    lines = {}
+    for x in range(NX):
+        for ty in range(4):
+            tx, y = x // 8, ty * 8
+            if x % 8 == 0:
+                at = [field[e * 8 + tx * 4 + ty : e * 8 + tx * 4 + ty + 1, :] for e in range(9)]
+                lines[ty] = ([at[e] + at[6 + e] * offset_y for e in range(3)], at[3:6])
+            base, slope = lines[ty]
+            q = [state[f * ROWS + x * NY + y : f * ROWS + x * NY + y + 8, :] for f in range(5)]
+            pull = [base[e] + slope[e] * (x % 8 - 3.5) for e in range(3)]
             moved = []
             for f in range(5):
-                moved.append(q[f] - half_step * (values[f] + others[rows(f, i), :]))
+                total = inner[f * ROWS + x * NY + y : f * ROWS + x * NY + y + 8, :]
+                if x < 3 or x >= NX - 3:
+                    row = (f * 6 + (x if x < 3 else x - 10)) * NY + y
+                    total = total + by_x[row : row + 8, :]
+                if ty in (0, 3):
+                    row = (f * NX + x) * RIM + (0 if ty == 0 else 8)
+                    total = total + by_y[row : row + 8, :]
+                moved.append(q[f] - half_step * total)
             weight = time_step * q[0]
             gain = q[1] * pull[0] + q[2] * pull[1] + q[3] * pull[2]
-            made[0, i, pl.ds(start, 8), :] = moved[0]
+            made[0, x, y : y + 8, :] = moved[0]
             for e in range(3):
-                pulls[e, i, pl.ds(start, 8), :] = pull[e]
-                made[1 + e, i, pl.ds(start, 8), :] = moved[1 + e] + weight * pull[e]
-            made[4, i, pl.ds(start, 8), :] = moved[4] + time_step * gain
-
-        def speed_at(i, q):
-            inverse = reciprocal(q[0])
-            return jnp.abs(q[1]) * inverse + sound_of(q, inverse)
-
-        sweep(load, speed_at, store, NX, 0)
-        for copy in writes(step):
-            copy.start()
-        return 0
-
-    lax.fori_loop(0, NY // 8, along_x, 0)
-    for step in range(NY // 8):
-        for copy in writes(step):
+                pulls[e, x, y : y + 8, :] = pull[e]
+                made[1 + e, x, y : y + 8, :] = moved[1 + e] + weight * pull[e]
+            made[4, x, y : y + 8, :] = moved[4] + time_step * gain
+        if x % 4 == 3:
+            for copy in writes(x // 4):
+                copy.start()
+    for part in range(4):
+        for copy in writes(part):
             copy.wait()
 
 
@@ -583,28 +646,27 @@
         place, far(state.reshape(5, ROWS, 128)), sources=[FAR], far_outs=range(5),
     )
     got = lax.all_to_all(sent.reshape(mortons * octs, 1, SENT * 128), AXES[::-1], 0, 0, tiled=True)
-    x_one = swap(x_one, lambda m, o: (m ^ 1, o))
-    x_two = swap(x_two, lambda m, o: (other(m), o) if 0 < m < mortons - 1 else (m, o ^ 1))
+    x_one = swap(x_one, lambda m, o: (other(m), o) if 0 < m < mortons - 1 else (m, o ^ 1))
+    x_two = swap(x_two, lambda m, o: (m ^ 1, o))
     y_one = swap(y_one, lambda m, o: (m, o ^ 1))
     y_two = swap(y_two, lambda m, o: (m, other(o)) if 0 < o < octs - 1 else (m, octs - 1 - o))
     rows = state.reshape(5 * ROWS, 128)
     rows, sent = lax.optimization_barrier((rows, sent))
-    by_z, padded, inverse_of, sound, uses_fine, uses_coarse = call(
-        inner_kernel, [5 * ROWS, 5 * many, many, many, 40, 64],
-        [5 * TALL, 5 * TALL, 640, 640, pltpu.VMEM((128, 32), jnp.int32), pltpu.VMEM((8, 16), jnp.int32),
-         pltpu.VMEM((16, 32), jnp.int32), pltpu.SemaphoreType.DMA((3,))],
+    inner, uses_fine, uses_coarse = call(
+        inner_kernel, [5 * ROWS, 40, 64],
+        [5 * TALL, 5 * TALL, 640, 640, 5 * many, many, many, 5 * many, pltpu.VMEM((128, 32), jnp.int32),
+         pltpu.VMEM((8, 16), jnp.int32), pltpu.VMEM((16, 32), jnp.int32), pltpu.SemaphoreType.DMA((3,))],
         place, rows, far(fine_pairs.reshape(128, 32)), far(fine_count.reshape(8, 16)), far(coarse_pairs.reshape(16, 32)),
-        sources=[VMEM, FAR, FAR, FAR], whole_numbers=(4, 5),
+        sources=[VMEM, FAR, FAR, FAR], whole_numbers=(1, 2),
     )
-    (others,) = call(
-        along_y_kernel, [5 * ROWS], [240, 240, 5 * many], place, padded, inverse_of, sound, y_one, y_two, by_z
-    )
+    rim = 5 * NX * RIM
     return call(
         outer_kernel, [(5, NX, NY, NZ), (3, NX, NY, NZ)],
-        [480, 480, 160, 72, pltpu.VMEM((5, NX, NY, NZ), F32), pltpu.VMEM((3, NX, NY, NZ), F32),
-         pltpu.SemaphoreType.DMA((2, 4))],
-        place, rows, x_one, x_two, others, uses_fine, uses_coarse, got.reshape(mortons * octs * SENT, 128),
-        far_outs=range(2),
+        [240, 240, 480, 480, 240, 240, rim, 960, rim, 160, 72, pltpu.VMEM((5, NX, NY, NZ), F32),
+         pltpu.VMEM((3, NX, NY, NZ), F32), pltpu.SemaphoreType.DMA((2,)), pltpu.SemaphoreType.DMA((2, 4))],
+        place, rows, inner, x_one, x_two, far(y_one), far(y_two), uses_fine, uses_coarse,
+        got.reshape(mortons * octs * SENT, 128),
+        sources=[VMEM] * 4 + [FAR] * 2 + [VMEM] * 3, far_outs=range(2),
     )
 
 

time: 38.7 us -> 37 us (0.956)
  waiting for transfers between devices: 4.46 us -> 2.08 us
  Pallas kernels: 13.9 us -> 14.7 us
  starting transfers between devices: 19.4 us -> 18.6 us
  local copies, waits for them, and re-layouts: 0.01 us -> 0.64 us
    ppermute x4, waiting for transfers between devices: 4.46 us -> 2.08 us  [swap(): lax.ppermute(values, AXES, [(index(p), index(pair(*p))) for p in pairs])]
    pallas_call x4 -> x3, Pallas kernels: 13.9 us -> 14.7 us  [call(): pl.pallas_call(kernel, out_shape=[pltpu.HBM(s, F32) if n in far_outs else...]
    ppermute x4, starting transfers between devices: 8.57 us -> 7.78 us  [swap(): lax.ppermute(values, AXES, [(index(p), index(pair(*p))) for p in pairs])]
    unnamed x2 -> x6, local copies, waits for them, and re-layouts: 0.01 us -> 0.64 us
  transfers between devices with their start and end apart: 5 -> 5, of which waited for: 1 -> 1; matrix products, arithmetic and copies ran while one was open for 0% -> 0% of each run, Pallas kernels for 16% -> 17%
where the time goes in v4:
time: 37 us; the launch traced here: 36.8 us
  starting transfers between devices  18.6 us (50%)
  Pallas kernels  14.7 us (40%)
  waiting for transfers between devices  2.08 us (6%)
  between operations  0.69 us (2%)
  local copies, waits for them, and re-layouts  0.64 us (2%)
    pallas_call x3, Pallas kernels, call(): pl.pallas_call(kernel, out_shape=[pltpu.HBM(s, F32) if n in far_outs else...  14.7 us
    all_to_all x1, starting transfers between devices, local(): lax.all_to_all(sent.reshape(mortons * octs, 1, SENT * 128), AXES[::-1], 0...  10.8 us
    ppermute x4, starting transfers between devices, swap(): lax.ppermute(values, AXES, [(index(p), index(pair(*p))) for p in pairs])  7.78 us
    ppermute x4, waiting for transfers between devices, swap(): lax.ppermute(values, AXES, [(index(p), index(pair(*p))) for p in pairs])  2.08 us
  transfers between devices with their start and end apart: 5, of which 1 were waited for; matrix products, arithmetic and copies ran while one was open for 0% of the time, Pallas kernels for 17%

profile of v4, /device:TPU:5, one launch (start us, length us, event | category | flops | bytes accessed | tf_op | source)
XLA Modules:
  0.0 36.8 jit_solution(16800666647832659471)
XLA Ops:
  0.6 0.0 copy-start
  0.6 0.1 pad_add_fusion.place
  0.7 3.2 %shard_map.59 = (f32[640,128]{1,0:T(8,128)}, f32[480,128]{1,0:T(8,128)}, f32[480,128]{1,0:T(8,128)}, f32[240,128]{1,0:T(8,128)}, f32[240,128]{1,0:T(8,128)}) custom-call(s32[4]{0:T(128)S(1)} %pad_add_fusion.place, f32[5,512,128]{2,1,0:T(8,128)} %bitcast.9), custom_call_target="tpu_custom_call" | custom-call | flops 1000 | bytes 1000 | tf_op jit(solution)/shard_map/pallas_call | solution.py:614
  4.0 10.8 %all-to-all-start = ((f32[128,1,640]{2,1,0:T(1,128)}), f32[128,1,640]{2,1,0:T(1,128)S(1)}, u32[]{:S(2)}, u32[]{:S(2)}) async-start(f32[128,1,640]{2,1,0:T(1,128)} %bitcast.13), calls=%async_computation | async-start | bytes 655360 | tf_op jit(solution)/shard_map/all_to_all | solution.py:648
  14.8 5.4 %collective-permute-start = (f32[480,128]{1,0:T(8,128)}, f32[480,128]{1,0:T(8,128)S(1)}, u32[]{:S(2)}, u32[]{:S(2)}) collective-permute-start(f32[480,128]{1,0:T(8,128)} %get-tuple-element.14), channel_id=1, source_target_pairs={{0,1},{1,0},{2,3},{3,2},{4,8},{5,9},{6,10},{7,11},{8,4},{9,5},{10,... | collective-permute-start | bytes 737288 | tf_op jit(solution)/shard_map/ppermute | solution.py:636
  20.2 0.0 collective-permute-start.1
  20.2 0.6 %collective-permute-start.2 = (f32[240,128]{1,0:T(8,128)}, f32[240,128]{1,0:T(8,128)S(1)}, u32[]{:S(2)}, u32[]{:S(2)}) collective-permute-start(f32[240,128]{1,0:T(8,128)} %get-tuple-element.16), channel_id=1, source_target_pairs={{0,1},{1,0},{2,3},{3,2},{4,5},{5,4},{6,7},{7,6},{8,9},{9,8},{10,11... | collective-permute-start | bytes 368648 | tf_op jit(solution)/shard_map/ppermute | solution.py:636
  20.9 1.7 %collective-permute-start.3 = (f32[240,128]{1,0:T(8,128)}, f32[240,128]{1,0:T(8,128)S(1)}, u32[]{:S(2)}, u32[]{:S(2)}) collective-permute-start(f32[240,128]{1,0:T(8,128)} %get-tuple-element.17), channel_id=1, source_target_pairs={{0,3},{1,2},{2,1},{3,0},{4,7},{5,6},{6,5},{7,4},{8,11},{9,10},{10,... | collective-permute-start | bytes 368648 | tf_op jit(solution)/shard_map/ppermute | solution.py:636
  22.6 0.0 copy-done
  22.6 6.4 %shard_map.60 = (f32[2560,128]{1,0:T(8,128)S(1)}, s32[40,128]{1,0:T(8,128)S(1)}, s32[64,128]{1,0:T(8,128)S(1)}) custom-call(s32[4]{0:T(128)S(1)} %pad_add_fusion.place, f32[2560,128]{1,0:T(8,128)S(1)} %bitcast.10, s32[128,32]{1,0:T(8,128)} %bitcast.14, s32[8,16]{1,0:T(8,128)} %bitcast.16, s32[16,32]{1,0:T(8,128)} %bitcast.15), custom_call_target="tpu_custom_call" | custom-call | flops 1000 | bytes 1000 | tf_op jit(solution)/shard_map/pallas_call | solution.py:614
  29.0 0.0 collective-permute-done.2.far_y_one
  29.0 0.0 copy-start.1
  29.0 2.1 %collective-permute-done.3.far_y_two = f32[240,128]{1,0:T(8,128)S(1)} collective-permute-done((f32[240,128]{1,0:T(8,128)}, f32[240,128]{1,0:T(8,128)S(1)}, u32[]{:S(2)}, u32[]{:S(2)}) %collective-permute-start.3) | collective-permute-done | bytes 122912 | tf_op jit(solution)/shard_map/ppermute | solution.py:636
  31.1 0.0 copy-start.2
  31.1 0.0 collective-permute-done.x_one
  31.1 0.0 copy-done.1
  31.1 0.6 %copy-done.2 = f32[240,128]{1,0:T(8,128)} copy-done((f32[240,128]{1,0:T(8,128)}, f32[240,128]{1,0:T(8,128)S(1)}, u32[]{:S(2)}) %copy-start.2) | copy-done | bytes 122904
  31.7 0.0 collective-permute-done.1.x_two
  31.7 0.0 all-to-all-done
  31.7 5.1 %shard_map.61 = (f32[5,16,32,128]{3,2,1,0:T(8,128)}, f32[3,16,32,128]{3,2,1,0:T(8,128)}) custom-call(s32[4]{0:T(128)S(1)} %pad_add_fusion.place, f32[2560,128]{1,0:T(8,128)S(1)} %bitcast.11, f32[2560,128]{1,0:T(8,128)S(1)} %get-tuple-element.13.inner, f32[480,128]{1,0:T(8,128)S(1)} %collective-permute-done.x_one, ...), custom_call_target="tpu_custom_call" | custom-call | flops 1000 | bytes 1000 | tf_op jit(solution)/shard_map/pallas_call | solution.py:614
Async XLA Ops:
  0.6 21.9 %copy-start = (f32[5,16,32,128]{3,2,1,0:T(8,128)S(1)}, f32[5,16,32,128]{3,2,1,0:T(8,128)}, u32[]{:S(2)}) copy-start(f32[5,16,32,128]{3,2,1,0:T(8,128)} %param.4) | copy-start | bytes 3932164
  4.0 27.8 %all-to-all-start = ((f32[128,1,640]{2,1,0:T(1,128)}), f32[128,1,640]{2,1,0:T(1,128)S(1)}, u32[]{:S(2)}, u32[]{:S(2)}) async-start(f32[128,1,640]{2,1,0:T(1,128)} %bitcast.13), calls=%async_computation | async-start | bytes 655360 | tf_op jit(solution)/shard_map/all_to_all | solution.py:648
  14.8 16.3 %collective-permute-start = (f32[480,128]{1,0:T(8,128)}, f32[480,128]{1,0:T(8,128)S(1)}, u32[]{:S(2)}, u32[]{:S(2)}) collective-permute-start(f32[480,128]{1,0:T(8,128)} %get-tuple-element.14), channel_id=1, source_target_pairs={{0,1},{1,0},{2,3},{3,2},{4,8},{5,9},{6,10},{7,11},{8,4},{9,5},{10,... | collective-permute-start | bytes 737288 | tf_op jit(solution)/shard_map/ppermute | solution.py:636
  20.2 11.5 %collective-permute-start.1 = (f32[480,128]{1,0:T(8,128)}, f32[480,128]{1,0:T(8,128)S(1)}, u32[]{:S(2)}, u32[]{:S(2)}) collective-permute-start(f32[480,128]{1,0:T(8,128)} %get-tuple-element.15), channel_id=1, source_target_pairs={{0,4},{1,5},{2,6},{3,7},{4,0},{5,1},{6,2},{7,3},{8,12},{9,13},{10,... | collective-permute-start | bytes 737288 | tf_op jit(solution)/shard_map/ppermute | solution.py:636
  20.2 8.8 %collective-permute-start.2 = (f32[240,128]{1,0:T(8,128)}, f32[240,128]{1,0:T(8,128)S(1)}, u32[]{:S(2)}, u32[]{:S(2)}) collective-permute-start(f32[240,128]{1,0:T(8,128)} %get-tuple-element.16), channel_id=1, source_target_pairs={{0,1},{1,0},{2,3},{3,2},{4,5},{5,4},{6,7},{7,6},{8,9},{9,8},{10,11... | collective-permute-start | bytes 368648 | tf_op jit(solution)/shard_map/ppermute | solution.py:636
  20.9 10.2 %collective-permute-start.3 = (f32[240,128]{1,0:T(8,128)}, f32[240,128]{1,0:T(8,128)S(1)}, u32[]{:S(2)}, u32[]{:S(2)}) collective-permute-start(f32[240,128]{1,0:T(8,128)} %get-tuple-element.17), channel_id=1, source_target_pairs={{0,3},{1,2},{2,1},{3,0},{4,7},{5,6},{6,5},{7,4},{8,11},{9,10},{10,... | collective-permute-start | bytes 368648 | tf_op jit(solution)/shard_map/ppermute | solution.py:636
  29.0 2.1 %copy-start.1 = (f32[240,128]{1,0:T(8,128)}, f32[240,128]{1,0:T(8,128)S(1)}, u32[]{:S(2)}) copy-start(f32[240,128]{1,0:T(8,128)S(1)} %collective-permute-done.2.far_y_one) | copy-start | bytes 368644
  31.1 0.6 %copy-start.2 = (f32[240,128]{1,0:T(8,128)}, f32[240,128]{1,0:T(8,128)S(1)}, u32[]{:S(2)}) copy-start(f32[240,128]{1,0:T(8,128)S(1)} %collective-permute-done.3.far_y_two) | copy-start | bytes 368644

commit v5 on v4

--- a/solution.py
+++ b/solution.py
@@ -20,8 +20,9 @@
 ROWS = NX * NY
 PITCH = 33
 TALL = 144
+LONG = 488
 RIM = 17
-SENT = 5
+SENT = 3
 SYM = ((0, 0), (0, 1), (0, 2), (1, 1), (1, 2), (2, 2))
 
 
@@ -50,7 +51,7 @@
 
 
 def moments_kernel(
-    place, state, sent, x_one, x_two, y_one, y_two, rows, near_sent, near_one, near_two, arrived, taken, written
+    place, state, sent, x_one, x_two, y_one, y_two, own, rows, near_sent, near_one, near_two, arrived, taken, written
 ):
     part = ROWS // 4
     copies = [
@@ -123,12 +124,28 @@
     families = jnp.concatenate([mass] + shifted + [jnp.zeros((4, 128), F32)], axis=0)
     families = jnp.dot(families, pick, precision=HIGH, preferred_element_type=F32)
     last = jnp.where(lane < 64, fold_rows(families, 16), jnp.max(fastest))
-    five = jnp.concatenate([mass] + dipole + [last], axis=0)
-    many = jnp.concatenate([five] * 8, axis=0)
-    for copy in range(16):
-        near_sent[copy * 40 : copy * 40 + 40, :] = many
+    own[...] = jnp.concatenate([mass] + dipole + [jnp.zeros((4, 128), F32)], axis=0)
+    extra = [
+        pltpu.make_async_copy(own, out.at[pl.ds(480, 8), :], taken.at[n, 5]) for n, out in enumerate((x_one, x_two))
+    ]
+    for copy in extra:
+        copy.start()
+    patterns = []
+    for side in range(2):
+        packed = [
+            jnp.where(lane < 32, pltpu.roll(v, (-32 * side) % 128, 1), pltpu.roll(v, (-32 - 32 * side) % 128, 1))
+            for v in [mass] + dipole
+        ]
+        pairs = [jnp.where(lane < 64, packed[m], pltpu.roll(packed[m + 1], 64, 1)) for m in (0, 2)]
+        patterns.append(jnp.concatenate([last] + pairs, axis=0))
+    patterns = [jnp.concatenate([p] * 8, axis=0) for p in patterns]
+    for octant in range(4):
+        chosen = jnp.where(octant > place[1], patterns[1], patterns[0])
+        for part in range(4):
+            row = octant * 96 + part * 24
+            near_sent[row : row + 24, :] = chosen
     writes[2].start()
-    for copy in edges + writes:
+    for copy in edges + extra + writes:
         copy.wait()
 
 
@@ -193,7 +210,7 @@
 
 def sides(one, two, low, high, rank):
     even = rank % 2 == 0
-    for row in range(0, one.shape[0], 8):
+    for row in range(0, low.shape[0], 8):
         a, b = one[row : row + 8, :], two[row : row + 8, :]
         low[row : row + 8, :] = jnp.where(even, b, a)
         high[row : row + 8, :] = jnp.where(even, a, b)
@@ -370,13 +387,13 @@
         totals[3 + e] = totals[3 + e] + mass * tide[e]
 
 
-def far_fields(place, uses_fine, uses_coarse, got, around):
+def far_fields(place, uses_fine, uses_coarse, got, own, beside, around):
     morton, octant = place[0], place[1]
     mortons, octs = place[2], place[3]
     lane = iota((8, 128), 1)
     lane_row = iota((1, 128), 1)
 
-    rows = jnp.concatenate([got[pl.ds(g * 8 * SENT + 4, 8, stride=SENT), :] for g in range(16)], axis=0)
+    rows = jnp.concatenate([got[pl.ds(g * 8 * SENT, 8, stride=SENT), :] for g in range(16)], axis=0)
     time_step = COURANT / jnp.max(rows[:, 64:128])
     moments = rows.T
     target_z = iota((8, 128), 0)
@@ -387,10 +404,10 @@
         for lp in range(16):
             ry = 16.0 * (lane // mortons * 2 + lp // 8 - (2 * octant + half)).astype(F32)
             rz = 16.0 * (lp % 8 - target_z).astype(F32)
-            own = [jnp.broadcast_to(moments[m * 16 + lp : m * 16 + lp + 1], (8, 128)) for m in range(4)]
+            families = [jnp.broadcast_to(moments[m * 16 + lp : m * 16 + lp + 1], (8, 128)) for m in range(4)]
             row = (lp // 4 * 2 + half) * 8
             uses = ((uses_coarse[row : row + 8, :] >> (lp % 4 * 6)) & 63).astype(F32)
-            add_terms(totals, uses, (rx, ry, rz), rx * rx + ry * ry + rz * rz, own[0], own[1:])
+            add_terms(totals, uses, (rx, ry, rz), rx * rx + ry * ry + rz * rz, families[0], families[1:])
         coarse.append([jnp.sum(each, axis=1, keepdims=True) for each in totals])
     result = []
     for e in range(9):
@@ -402,15 +419,31 @@
         for j in range(3):
             result[i] = result[i] + result[3 + sym(i, j)] * side[j]
 
+    def inside(dx, dy):
+        at_x, at_y = morton + dx, octant + dy
+        return (at_x >= 0) & (at_x < mortons) & (at_y >= 0) & (at_y < octs)
+
     blocks = []
     for dy in (-1, 0, 1):
         block = []
-        for dx in (-1, 0, 1):
-            at_x, at_y = morton + dx, octant + dy
-            inside = (at_x >= 0) & (at_x < mortons) & (at_y >= 0) & (at_y < octs)
-            device = jnp.clip(at_y, 0, octs - 1) * mortons + jnp.clip(at_x, 0, mortons - 1)
-            for m in range(4):
-                block.append(jnp.where(inside, got[pl.ds(device * SENT + m, 1), :], 0.0))
+        if dy:
+            halves = []
+            for dx in (-1, 0, 1):
+                device = jnp.clip(octant + dy, 0, octs - 1) * mortons + jnp.clip(morton + dx, 0, mortons - 1)
+                for n in (1, 2):
+                    halves.append(jnp.where(inside(dx, dy), got[pl.ds(device * SENT + n, 1), :], 0.0))
+            halves = jnp.concatenate(halves + [jnp.zeros((2, 128), F32)], axis=0)
+            back = 32 if dy < 0 else 0
+            unpacked = [
+                jnp.where(lane < 64, pltpu.roll(each, back, 1), pltpu.roll(each, 32 + back, 1)) if back
+                else jnp.where(lane < 64, each, pltpu.roll(each, 32, 1))
+                for each in (halves, pltpu.roll(halves, 64, 1))
+            ]
+            for n in range(6):
+                block += [unpacked[0][n : n + 1], unpacked[1][n : n + 1]]
+        else:
+            for dx, source in ((-1, beside[0:4, :]), (0, own[0:4, :]), (1, beside[8:12, :])):
+                block.append(jnp.where(inside(dx, 0), source, 0.0))
         blocks.append(jnp.concatenate(block + [jnp.zeros((4, 128), F32)], axis=0))
     wide = iota((16, 128), 1)
     around[...] = jnp.zeros(around.shape, F32)
@@ -452,9 +485,9 @@
     return result, time_step
 
 
-def outer_kernel(
-    place, state, inner, x_one, x_two, far_y_one, far_y_two, uses_fine, uses_coarse, got, new, gravity,
-    y_one, y_two, x_low, x_high, y_low, y_high, rims, by_x, by_y, around, field, made, pulls, arrived, written,
+def edge_kernel(
+    place, state, inner, x_one, x_two, far_y_one, far_y_two, out, beside,
+    y_one, y_two, x_low, x_high, y_low, y_high, rims, by_x, by_y, arrived,
 ):
     reads = [
         pltpu.make_async_copy(far_y_one, y_one, arrived.at[0]),
@@ -463,6 +496,10 @@
     for copy in reads:
         copy.start()
     sides(x_two, x_one, x_low, x_high, place[0])
+    even = place[0] % 2 == 0
+    moments = x_one[480:488, :], x_two[480:488, :]
+    beside[0:8, :] = jnp.where(even, moments[0], moments[1])
+    beside[8:16, :] = jnp.where(even, moments[1], moments[0])
 
     def x_edge(beyond, x):
         for f in range(5):
@@ -542,13 +579,29 @@
 
     lax.fori_loop(0, NX // 8, along_y, 0)
 
-    result, time_step = far_fields(place, uses_fine, uses_coarse, got, around)
+    for f in range(5):
+        for x in range(NX):
+            for y in range(0, NY, 8):
+                row = f * ROWS + x * NY + y
+                total = inner[row : row + 8, :]
+                if x < 3 or x >= NX - 3:
+                    at = (f * 6 + (x if x < 3 else x - 10)) * NY + y
+                    total = total + by_x[at : at + 8, :]
+                if y in (0, NY - 8):
+                    at = (f * NX + x) * RIM + (0 if y == 0 else 8)
+                    total = total + by_y[at : at + 8, :]
+                out[row : row + 8, :] = total
+
+
+def update_kernel(
+    place, state, twice, uses_fine, uses_coarse, got, own, beside, new, gravity, around, field, made, pulls, written
+):
+    result, time_step = far_fields(place, uses_fine, uses_coarse, got, own, beside, around)
     half_step = 0.5 * time_step
-    keep = iota((8, 128), 1) // 16 == iota((8, 128), 0)
-    spread = (iota((128, 128), 0) % 16 == iota((128, 128), 1) // 8).astype(F32)
-    lines = jnp.concatenate([jnp.where(keep, each, 0.0) for each in result], axis=0)
-    lines = jnp.dot(lines, spread, precision=HIGH, preferred_element_type=F32)
-    lines = [lines[e * 8 : e * 8 + 8] for e in range(9)]
+    source = iota((8, 128), 0) * 16 + iota((8, 128), 1) // 8
+    lines = [
+        jnp.take_along_axis(jnp.broadcast_to(each, (8, 128)), source, axis=1, mode="promise_in_bounds") for each in result
+    ]
     offset_z = (iota((8, 128), 1) % 8).astype(F32) - 3.5
     for i in range(3):
         field[i * 8 : i * 8 + 8, :] = lines[i] + lines[3 + sym(i, 2)] * offset_z
@@ -575,13 +628,7 @@
             pull = [base[e] + slope[e] * (x % 8 - 3.5) for e in range(3)]
             moved = []
             for f in range(5):
-                total = inner[f * ROWS + x * NY + y : f * ROWS + x * NY + y + 8, :]
-                if x < 3 or x >= NX - 3:
-                    row = (f * 6 + (x if x < 3 else x - 10)) * NY + y
-                    total = total + by_x[row : row + 8, :]
-                if ty in (0, 3):
-                    row = (f * NX + x) * RIM + (0 if ty == 0 else 8)
-                    total = total + by_y[row : row + 8, :]
+                total = twice[f * ROWS + x * NY + y : f * ROWS + x * NY + y + 8, :]
                 moved.append(q[f] - half_step * total)
             weight = time_step * q[0]
             gain = q[1] * pull[0] + q[2] * pull[1] + q[3] * pull[2]
@@ -639,9 +686,9 @@
         return (i - 1 ^ 1) + 1
 
     block = pltpu.VMEM((5, ROWS, 128), F32)
-    sent, x_one, x_two, y_one, y_two = call(
-        moments_kernel, [128 * SENT, 480, 480, 240, 240],
-        [block, 128 * SENT, 240, 240, pltpu.SemaphoreType.DMA((4,)), pltpu.SemaphoreType.DMA((2, 5)),
+    sent, x_one, x_two, y_one, y_two, own = call(
+        moments_kernel, [128 * SENT, LONG, LONG, 240, 240, 8],
+        [block, 128 * SENT, 240, 240, pltpu.SemaphoreType.DMA((4,)), pltpu.SemaphoreType.DMA((2, 6)),
          pltpu.SemaphoreType.DMA((3,))],
         place, far(state.reshape(5, ROWS, 128)), sources=[FAR], far_outs=range(5),
     )
@@ -660,13 +707,15 @@
         sources=[VMEM, FAR, FAR, FAR], whole_numbers=(1, 2),
     )
     rim = 5 * NX * RIM
+    twice, beside = call(
+        edge_kernel, [5 * ROWS, 16], [240, 240, 480, 480, 240, 240, rim, 960, rim, pltpu.SemaphoreType.DMA((2,))],
+        place, rows, inner, x_one, x_two, far(y_one), far(y_two), sources=[VMEM] * 4 + [FAR] * 2,
+    )
     return call(
-        outer_kernel, [(5, NX, NY, NZ), (3, NX, NY, NZ)],
-        [240, 240, 480, 480, 240, 240, rim, 960, rim, 160, 72, pltpu.VMEM((5, NX, NY, NZ), F32),
-         pltpu.VMEM((3, NX, NY, NZ), F32), pltpu.SemaphoreType.DMA((2,)), pltpu.SemaphoreType.DMA((2, 4))],
-        place, rows, inner, x_one, x_two, far(y_one), far(y_two), uses_fine, uses_coarse,
-        got.reshape(mortons * octs * SENT, 128),
-        sources=[VMEM] * 4 + [FAR] * 2 + [VMEM] * 3, far_outs=range(2),
+        update_kernel, [(5, NX, NY, NZ), (3, NX, NY, NZ)],
+        [160, 72, pltpu.VMEM((5, NX, NY, NZ), F32), pltpu.VMEM((3, NX, NY, NZ), F32), pltpu.SemaphoreType.DMA((2, 4))],
+        place, rows, twice, uses_fine, uses_coarse, got.reshape(mortons * octs * SENT, 128), own, beside,
+        far_outs=range(2),
     )
 
 

time: 37 us -> 32.7 us (0.88)
  the two profiles are of different devices: /device:TPU:5 before, /device:TPU:1 now
where the time goes in v5:
time: 32.7 us; the launch traced here: 32.5 us
  starting transfers between devices  15.9 us (49%)
  Pallas kernels  15.1 us (46%)
  between operations  0.73 us (2%)
  local copies, waits for them, and re-layouts  0.65 us (2%)
    pallas_call x4, Pallas kernels, call(): pl.pallas_call(kernel, out_shape=[pltpu.HBM(s, F32) if n in far_outs else...  15.1 us
    all_to_all x1, starting transfers between devices, local(): lax.all_to_all(sent.reshape(mortons * octs, 1, SENT * 128), AXES[::-1], 0...  10.5 us
    ppermute x4, starting transfers between devices, swap(): lax.ppermute(values, AXES, [(index(p), index(pair(*p))) for p in pairs])  5.38 us
    unnamed x6, local copies, waits for them, and re-layouts  0.65 us
  transfers between devices with their start and end apart: 5, of which 0 were waited for; matrix products, arithmetic and copies ran while one was open for 0% of the time, Pallas kernels for 27%

profile of v5, /device:TPU:1, one launch (start us, length us, event | category | flops | bytes accessed | tf_op | source)
XLA Modules:
  0.0 32.5 jit_solution(14379990878913294469)
XLA Ops:
  0.6 0.0 copy-start
  0.6 0.1 pad_add_fusion.place
  0.7 3.2 %shard_map.59 = (f32[384,128]{1,0:T(8,128)}, f32[488,128]{1,0:T(8,128)}, f32[488,128]{1,0:T(8,128)}, f32[240,128]{1,0:T(8,128)}, f32[240,128]{1,0:T(8,128)}, /*index=5*/f32[8,128]{1,0:T(8,128)S(1)}) custom-call(s32[4]{0:T(128)S(1)} %pad_add_fusion.place, f32[5,512,128]{2,1,0:T(8,128)} %bitcast.9), custom_call_target="tpu_custom_call" | custom-call | flops 1000 | bytes 1000 | tf_op jit(solution)/shard_map/pallas_call | solution.py:661
  4.0 1.5 %collective-permute-start = (f32[488,128]{1,0:T(8,128)}, f32[488,128]{1,0:T(8,128)S(1)}, u32[]{:S(2)}, u32[]{:S(2)}) collective-permute-start(f32[488,128]{1,0:T(8,128)} %get-tuple-element.17), channel_id=1, source_target_pairs={{0,1},{1,0},{2,3},{3,2},{4,8},{5,9},{6,10},{7,11},{8,4},{9,5},{10,... | collective-permute-start | bytes 749576 | tf_op jit(solution)/shard_map/ppermute | solution.py:683
  5.5 2.0 %collective-permute-start.1 = (f32[488,128]{1,0:T(8,128)}, f32[488,128]{1,0:T(8,128)S(1)}, u32[]{:S(2)}, u32[]{:S(2)}) collective-permute-start(f32[488,128]{1,0:T(8,128)} %get-tuple-element.18), channel_id=1, source_target_pairs={{0,4},{1,5},{2,6},{3,7},{4,0},{5,1},{6,2},{7,3},{8,12},{9,13},{10,... | collective-permute-start | bytes 749576 | tf_op jit(solution)/shard_map/ppermute | solution.py:683
  7.5 10.5 %all-to-all-start = ((f32[128,1,384]{2,1,0:T(1,128)}), f32[128,1,384]{2,1,0:T(1,128)S(1)}, u32[]{:S(2)}, u32[]{:S(2)}) async-start(f32[128,1,384]{2,1,0:T(1,128)} %bitcast.14), calls=%async_computation | async-start | bytes 393216 | tf_op jit(solution)/shard_map/all_to_all | solution.py:695
  18.0 1.1 %collective-permute-start.2 = (f32[240,128]{1,0:T(8,128)}, f32[240,128]{1,0:T(8,128)S(1)}, u32[]{:S(2)}, u32[]{:S(2)}) collective-permute-start(f32[240,128]{1,0:T(8,128)} %get-tuple-element.19), channel_id=1, source_target_pairs={{0,1},{1,0},{2,3},{3,2},{4,5},{5,4},{6,7},{7,6},{8,9},{9,8},{10,11... | collective-permute-start | bytes 368648 | tf_op jit(solution)/shard_map/ppermute | solution.py:683
  19.1 0.7 %collective-permute-start.3 = (f32[240,128]{1,0:T(8,128)}, f32[240,128]{1,0:T(8,128)S(1)}, u32[]{:S(2)}, u32[]{:S(2)}) collective-permute-start(f32[240,128]{1,0:T(8,128)} %get-tuple-element.20), channel_id=1, source_target_pairs={{0,3},{1,2},{2,1},{3,0},{4,7},{5,6},{6,5},{7,4},{8,11},{9,10},{10,... | collective-permute-start | bytes 368648 | tf_op jit(solution)/shard_map/ppermute | solution.py:683
  19.9 0.0 copy-done
  19.9 6.4 %shard_map.60 = (f32[2560,128]{1,0:T(8,128)S(1)}, s32[40,128]{1,0:T(8,128)S(1)}, s32[64,128]{1,0:T(8,128)S(1)}) custom-call(s32[4]{0:T(128)S(1)} %pad_add_fusion.place, f32[2560,128]{1,0:T(8,128)S(1)} %bitcast.10, s32[128,32]{1,0:T(8,128)} %bitcast.15, s32[8,16]{1,0:T(8,128)} %bitcast.17, s32[16,32]{1,0:T(8,128)} %bitcast.16), custom_call_target="tpu_custom_call" | custom-call | flops 1000 | bytes 1000 | tf_op jit(solution)/shard_map/pallas_call | solution.py:661
  26.3 0.0 collective-permute-done.2.far_y_one
  26.3 0.0 copy-start.1
  26.3 0.0 collective-permute-done.3.far_y_two
  26.3 0.0 copy-start.2
  26.3 0.0 collective-permute-done.x_one
  26.3 0.0 collective-permute-done.1.x_two
  26.4 0.6 %copy-done.1 = f32[240,128]{1,0:T(8,128)} copy-done((f32[240,128]{1,0:T(8,128)}, f32[240,128]{1,0:T(8,128)S(1)}, u32[]{:S(2)}) %copy-start.1) | copy-done | bytes 122904
  27.0 0.0 copy-done.2
  27.0 2.3 %shard_map.61 = (f32[2560,128]{1,0:T(8,128)S(1)}, f32[16,128]{1,0:T(8,128)S(1)}) custom-call(s32[4]{0:T(128)S(1)} %pad_add_fusion.place, f32[2560,128]{1,0:T(8,128)S(1)} %bitcast.11, f32[2560,128]{1,0:T(8,128)S(1)} %get-tuple-element.16.inner, f32[488,128]{1,0:T(8,128)S(1)} %collective-permute-done.x_one, f32[488,128]{1,0:T(8,128)S(1)} %collective-permute-done.1.x_two, ...), custom_call_target="tpu_custom_call" | custom-call | flops 1000 | bytes 1000 | tf_op jit(solution)/shard_map/pallas_call | solution.py:661
  29.3 0.0 all-to-all-done
  29.4 3.1 %shard_map.62 = (f32[5,16,32,128]{3,2,1,0:T(8,128)}, f32[3,16,32,128]{3,2,1,0:T(8,128)}) custom-call(s32[4]{0:T(128)S(1)} %pad_add_fusion.place, f32[2560,128]{1,0:T(8,128)S(1)} %bitcast.12, f32[2560,128]{1,0:T(8,128)S(1)} %get-tuple-element.21.twice, s32[40,128]{1,0:T(8,128)S(1)} %get-tuple-element.22.uses_fine, ...), custom_call_target="tpu_custom_call" | custom-call | flops 1000 | bytes 1000 | tf_op jit(solution)/shard_map/pallas_call | solution.py:661
Async XLA Ops:
  0.6 19.2 %copy-start = (f32[5,16,32,128]{3,2,1,0:T(8,128)S(1)}, f32[5,16,32,128]{3,2,1,0:T(8,128)}, u32[]{:S(2)}) copy-start(f32[5,16,32,128]{3,2,1,0:T(8,128)} %param.4) | copy-start | bytes 3932164
  4.0 22.4 %collective-permute-start = (f32[488,128]{1,0:T(8,128)}, f32[488,128]{1,0:T(8,128)S(1)}, u32[]{:S(2)}, u32[]{:S(2)}) collective-permute-start(f32[488,128]{1,0:T(8,128)} %get-tuple-element.17), channel_id=1, source_target_pairs={{0,1},{1,0},{2,3},{3,2},{4,8},{5,9},{6,10},{7,11},{8,4},{9,5},{10,... | collective-permute-start | bytes 749576 | tf_op jit(solution)/shard_map/ppermute | solution.py:683
  5.5 20.9 %collective-permute-start.1 = (f32[488,128]{1,0:T(8,128)}, f32[488,128]{1,0:T(8,128)S(1)}, u32[]{:S(2)}, u32[]{:S(2)}) collective-permute-start(f32[488,128]{1,0:T(8,128)} %get-tuple-element.18), channel_id=1, source_target_pairs={{0,4},{1,5},{2,6},{3,7},{4,0},{5,1},{6,2},{7,3},{8,12},{9,13},{10,... | collective-permute-start | bytes 749576 | tf_op jit(solution)/shard_map/ppermute | solution.py:683
  7.5 21.9 %all-to-all-start = ((f32[128,1,384]{2,1,0:T(1,128)}), f32[128,1,384]{2,1,0:T(1,128)S(1)}, u32[]{:S(2)}, u32[]{:S(2)}) async-start(f32[128,1,384]{2,1,0:T(1,128)} %bitcast.14), calls=%async_computation | async-start | bytes 393216 | tf_op jit(solution)/shard_map/all_to_all | solution.py:695
  18.0 8.3 %collective-permute-start.2 = (f32[240,128]{1,0:T(8,128)}, f32[240,128]{1,0:T(8,128)S(1)}, u32[]{:S(2)}, u32[]{:S(2)}) collective-permute-start(f32[240,128]{1,0:T(8,128)} %get-tuple-element.19), channel_id=1, source_target_pairs={{0,1},{1,0},{2,3},{3,2},{4,5},{5,4},{6,7},{7,6},{8,9},{9,8},{10,11... | collective-permute-start | bytes 368648 | tf_op jit(solution)/shard_map/ppermute | solution.py:683
  19.1 7.2 %collective-permute-start.3 = (f32[240,128]{1,0:T(8,128)}, f32[240,128]{1,0:T(8,128)S(1)}, u32[]{:S(2)}, u32[]{:S(2)}) collective-permute-start(f32[240,128]{1,0:T(8,128)} %get-tuple-element.20), channel_id=1, source_target_pairs={{0,3},{1,2},{2,1},{3,0},{4,7},{5,6},{6,5},{7,4},{8,11},{9,10},{10,... | collective-permute-start | bytes 368648 | tf_op jit(solution)/shard_map/ppermute | solution.py:683
  26.3 0.7 %copy-start.1 = (f32[240,128]{1,0:T(8,128)}, f32[240,128]{1,0:T(8,128)S(1)}, u32[]{:S(2)}) copy-start(f32[240,128]{1,0:T(8,128)S(1)} %collective-permute-done.2.far_y_one) | copy-start | bytes 368644
  26.3 0.7 %copy-start.2 = (f32[240,128]{1,0:T(8,128)}, f32[240,128]{1,0:T(8,128)S(1)}, u32[]{:S(2)}) copy-start(f32[240,128]{1,0:T(8,128)S(1)} %collective-permute-done.3.far_y_two) | copy-start | bytes 368644

commit v6 on v5

--- a/solution.py
+++ b/solution.py
@@ -51,7 +51,7 @@
 
 
 def moments_kernel(
-    place, state, sent, x_one, x_two, y_one, y_two, own, rows, near_sent, near_one, near_two, arrived, taken, written
+    place, state, sent, x_one, x_two, y_one, y_two, own, rows, arrived
 ):
     part = ROWS // 4
     copies = [
@@ -63,13 +63,6 @@
     even, oct_even = place[0] % 2 == 0, place[1] % 2 == 0
     x_starts = (jnp.where(even, 0, NX - 3), jnp.where(even, NX - 3, 0))
     y_starts = (jnp.where(oct_even, NY - 3, 0), jnp.where(oct_even, 0, NY - 3))
-    edges = [
-        pltpu.make_async_copy(
-            rows.at[f, pl.ds(pl.multiple_of(start * NY, 32), 96), :], out.at[pl.ds(f * 96, 96), :], taken.at[n, f]
-        )
-        for n, (out, start) in enumerate(((x_one, x_starts[0]), (x_two, x_starts[1])))
-        for f in range(5)
-    ]
     for copy in copies:
         copy.start()
     offset_y = iota((8, 128), 0).astype(F32) - 3.5
@@ -93,43 +86,43 @@
             sums.append(jnp.sum(totals[ty], axis=0, keepdims=True))
             sums_x.append(jnp.sum(totals_x[ty], axis=0, keepdims=True))
             sums_y.append(jnp.sum(totals[ty] * offset_y, axis=0, keepdims=True))
-    for copy in edges:
-        copy.start()
-    for out, start in ((near_one, y_starts[0]), (near_two, y_starts[1])):
+    for out, start in ((x_one, x_starts[0]), (x_two, x_starts[1])):
+        for f in range(5):
+            out[f * 96 : f * 96 + 96, :] = rows[f, pl.ds(pl.multiple_of(start * NY, 32), 96), :]
+    for out, start in ((y_one, y_starts[0]), (y_two, y_starts[1])):
         for f in range(5):
             for x in range(NX):
                 row = (f * NX + x) * 3
                 out[row : row + 3, :] = rows[f, pl.ds(x * NY + start, 3), :]
-    writes = [
-        pltpu.make_async_copy(near, out, written.at[n])
-        for n, (near, out) in enumerate(((near_one, y_one), (near_two, y_two), (near_sent, sent)))
+    parents = []
+    for py in range(2):
+        children = [(tx, ty) for tx in range(2) for ty in (2 * py, 2 * py + 1)]
+        terms = [[], [], []]
+        for tx, ty in children:
+            n = tx * 4 + ty
+            terms[0].append(sums[n])
+            terms[1].append(sums_x[n] + (8.0 * tx - 4.0) * sums[n])
+            terms[2].append(sums_y[n] + (8.0 * (ty % 2) - 4.0) * sums[n])
+        parents.append([(t[0] + t[1]) + (t[2] + t[3]) for t in terms])
+    parents = [parents[py][m] for m in range(3) for py in range(2)]
+    lines = jnp.concatenate(sums + sums_x + sums_y + parents + [jnp.zeros((2, 128), F32)], axis=0)
+    z, lanes = iota((128, 128), 0), iota((128, 128), 1)
+    pick = (z // 8 == lanes % 16).astype(F32)
+    pick_parent = (z // 16 == lanes % 8).astype(F32)
+    picks = [
+        pick, pick * ((z % 8).astype(F32) - 3.5), pick_parent, pick_parent * ((z % 16).astype(F32) - 7.5)
     ]
-    writes[0].start()
-    writes[1].start()
-    lines = jnp.concatenate(sums + sums_x + sums_y, axis=0)
-    z = iota((128, 128), 0)
-    pick = (z // 8 == iota((128, 128), 1) % 16).astype(F32)
-    by_z = pick * ((z % 8).astype(F32) - 3.5)
-    folded = jnp.dot(lines, pick, precision=HIGH, preferred_element_type=F32)
-    folded_z = jnp.dot(lines[0:8], by_z, precision=HIGH, preferred_element_type=F32)
-    mass = fold_rows(folded[0:8], 16)
-    dipole = [fold_rows(folded[8:16], 16), fold_rows(folded[16:24], 16), fold_rows(folded_z, 16)]
-
+    folded = jnp.dot(lines, jnp.concatenate(picks, axis=1), precision=HIGH, preferred_element_type=F32)
+    mass = fold_rows(folded[0:8, 0:128], 16)
+    dipole = [
+        fold_rows(folded[8:16, 0:128], 16), fold_rows(folded[16:24, 0:128], 16), fold_rows(folded[0:8, 128:256], 16)
+    ]
     lane = iota((1, 128), 1)
-    odd = [lane // 64, lane // 16 % 2, lane % 2]
-    shifted = [d + 4.0 * (2 * o - 1).astype(F32) * mass for d, o in zip(dipole, odd, strict=True)]
-    t = iota((128, 128), 0)
-    parent = t // 32 % 2 * 8 + t % 16 // 2
-    pick = (parent == iota((128, 128), 1) % 16).astype(F32)
-    families = jnp.concatenate([mass] + shifted + [jnp.zeros((4, 128), F32)], axis=0)
-    families = jnp.dot(families, pick, precision=HIGH, preferred_element_type=F32)
-    last = jnp.where(lane < 64, fold_rows(families, 16), jnp.max(fastest))
+    families = jnp.concatenate([folded[24:30, 256:384], folded[24:26, 384:512]], axis=0)
+    last = jnp.where(lane < 64, fold_rows(families, 8), jnp.max(fastest))
     own[...] = jnp.concatenate([mass] + dipole + [jnp.zeros((4, 128), F32)], axis=0)
-    extra = [
-        pltpu.make_async_copy(own, out.at[pl.ds(480, 8), :], taken.at[n, 5]) for n, out in enumerate((x_one, x_two))
-    ]
-    for copy in extra:
-        copy.start()
+    x_one[480:488, :] = own[...]
+    x_two[480:488, :] = own[...]
     patterns = []
     for side in range(2):
         packed = [
@@ -143,10 +136,7 @@
         chosen = jnp.where(octant > place[1], patterns[1], patterns[0])
         for part in range(4):
             row = octant * 96 + part * 24
-            near_sent[row : row + 24, :] = chosen
-    writes[2].start()
-    for copy in edges + extra + writes:
-        copy.wait()
+            sent[row : row + 24, :] = chosen
 
 
 def rise(before, here, after):
@@ -283,13 +273,14 @@
     group = jnp.floor((plane + 0.5) * 0.2)
     one = jnp.left_shift(1, (6.0 * (plane - 5.0 * group)).astype(jnp.int32))
     ones = [jnp.where(group == g, one, 0) for g in range(5)]
+    fine_uses[24:32, :] = jnp.zeros((8, 128), jnp.int32)
     for g in range(5):
         lines = []
         for ox in range(5):
             hits = jnp.where(along == ox, ones[g], 0)
             hits = (hits[0:8] + hits[8:16]) + (hits[16:24] + hits[24:32])
             lines.append(jnp.sum(hits, axis=0, keepdims=True))
-        fine_uses[g * 8 : g * 8 + 8, :] = jnp.concatenate(lines + [jnp.zeros((3, 128), jnp.int32)], axis=0)
+        fine_uses[g * 5 : g * 5 + 5, :] = jnp.concatenate(lines, axis=0)
 
     slot = iota((8, 128), 1)
     device = slot % place[2] * place[3] + slot // place[2]
@@ -475,7 +466,7 @@
             if oz:
                 ok = (lane % 16 + oz >= 0) & (lane % 16 + oz < 16)
                 moved = [jnp.where(ok, pltpu.roll(each, (-oz) % 128, 1), 0.0) for each in base]
-            uses = ((uses_fine[(oy + 2) * 8 : (oy + 2) * 8 + 8, :] >> ((oz + 2) * 6)) & 63).astype(F32)
+            uses = ((uses_fine[(oy + 2) * 5 : (oy + 2) * 5 + 8, :] >> ((oz + 2) * 6)) & 63).astype(F32)
             add_terms(
                 totals, uses, (rx, 8.0 * oy, 8.0 * oz),
                 square_x + (64.0 * oy * oy + 64.0 * oz * oz), moved[0], moved[1:],
@@ -486,15 +477,9 @@
 
 
 def edge_kernel(
-    place, state, inner, x_one, x_two, far_y_one, far_y_two, out, beside,
-    y_one, y_two, x_low, x_high, y_low, y_high, rims, by_x, by_y, arrived,
+    place, state, inner, x_one, x_two, y_one, y_two, out, beside,
+    x_low, x_high, y_low, y_high, rims, by_x, by_y,
 ):
-    reads = [
-        pltpu.make_async_copy(far_y_one, y_one, arrived.at[0]),
-        pltpu.make_async_copy(far_y_two, y_two, arrived.at[1]),
-    ]
-    for copy in reads:
-        copy.start()
     sides(x_two, x_one, x_low, x_high, place[0])
     even = place[0] % 2 == 0
     moments = x_one[480:488, :], x_two[480:488, :]
@@ -543,8 +528,6 @@
                 row = (f * NX + x) * RIM + side
                 rims[row : row + 8, :] = state[f * ROWS + x * NY + y : f * ROWS + x * NY + y + 8, :]
                 by_y[row : row + 8, :] = jnp.zeros((8, 128), F32)
-    for copy in reads:
-        copy.wait()
     sides(y_one, y_two, y_low, y_high, place[1])
 
     def y_edge(beyond, row):
@@ -688,9 +671,7 @@
     block = pltpu.VMEM((5, ROWS, 128), F32)
     sent, x_one, x_two, y_one, y_two, own = call(
         moments_kernel, [128 * SENT, LONG, LONG, 240, 240, 8],
-        [block, 128 * SENT, 240, 240, pltpu.SemaphoreType.DMA((4,)), pltpu.SemaphoreType.DMA((2, 6)),
-         pltpu.SemaphoreType.DMA((3,))],
-        place, far(state.reshape(5, ROWS, 128)), sources=[FAR], far_outs=range(5),
+        [block, pltpu.SemaphoreType.DMA((4,))], place, far(state.reshape(5, ROWS, 128)), sources=[FAR],
     )
     got = lax.all_to_all(sent.reshape(mortons * octs, 1, SENT * 128), AXES[::-1], 0, 0, tiled=True)
     x_one = swap(x_one, lambda m, o: (other(m), o) if 0 < m < mortons - 1 else (m, o ^ 1))
@@ -700,7 +681,7 @@
     rows = state.reshape(5 * ROWS, 128)
     rows, sent = lax.optimization_barrier((rows, sent))
     inner, uses_fine, uses_coarse = call(
-        inner_kernel, [5 * ROWS, 40, 64],
+        inner_kernel, [5 * ROWS, 32, 64],
         [5 * TALL, 5 * TALL, 640, 640, 5 * many, many, many, 5 * many, pltpu.VMEM((128, 32), jnp.int32),
          pltpu.VMEM((8, 16), jnp.int32), pltpu.VMEM((16, 32), jnp.int32), pltpu.SemaphoreType.DMA((3,))],
         place, rows, far(fine_pairs.reshape(128, 32)), far(fine_count.reshape(8, 16)), far(coarse_pairs.reshape(16, 32)),
@@ -708,8 +689,8 @@
     )
     rim = 5 * NX * RIM
     twice, beside = call(
-        edge_kernel, [5 * ROWS, 16], [240, 240, 480, 480, 240, 240, rim, 960, rim, pltpu.SemaphoreType.DMA((2,))],
-        place, rows, inner, x_one, x_two, far(y_one), far(y_two), sources=[VMEM] * 4 + [FAR] * 2,
+        edge_kernel, [5 * ROWS, 16], [480, 480, 240, 240, rim, 960, rim],
+        place, rows, inner, x_one, x_two, y_one, y_two,
     )
     return call(
         update_kernel, [(5, NX, NY, NZ), (3, NX, NY, NZ)],

time: 32.7 us -> 31.7 us (0.969)
  local copies, waits for them, and re-layouts: 0.65 us -> 0.01 us
    unnamed x6 -> x2, local copies, waits for them, and re-layouts: 0.65 us -> 0.01 us
  transfers between devices with their start and end apart: 5 -> 5, of which waited for: 0 -> 0; matrix products, arithmetic and copies ran while one was open for 0% -> 0% of each run, Pallas kernels for 27% -> 28%
where the time goes in v6:
time: 31.7 us; the launch traced here: 31.6 us
  starting transfers between devices  15.9 us (50%)
  Pallas kernels  14.9 us (47%)
  between operations  0.7 us (2%)
    pallas_call x4, Pallas kernels, call(): pl.pallas_call(kernel, out_shape=[pltpu.HBM(s, F32) if n in far_outs else...  14.9 us
    all_to_all x1, starting transfers between devices, local(): lax.all_to_all(sent.reshape(mortons * octs, 1, SENT * 128), AXES[::-1], 0...  10.5 us
    ppermute x4, starting transfers between devices, swap(): lax.ppermute(values, AXES, [(index(p), index(pair(*p))) for p in pairs])  5.38 us
  transfers between devices with their start and end apart: 5, of which 0 were waited for; matrix products, arithmetic and copies ran while one was open for 0% of the time, Pallas kernels for 28%

profile of v6, /device:TPU:1, one launch (start us, length us, event | category | flops | bytes accessed | tf_op | source)
XLA Modules:
  0.0 31.6 jit_solution(17233498045228994754)
XLA Ops:
  0.6 0.0 copy-start
  0.6 0.1 pad_add_fusion.place
  0.7 3.1 %shard_map.59 = (f32[384,128]{1,0:T(8,128)}, f32[488,128]{1,0:T(8,128)S(1)}, f32[488,128]{1,0:T(8,128)S(1)}, f32[240,128]{1,0:T(8,128)S(1)}, f32[240,128]{1,0:T(8,128)S(1)}, /*index=5*/f32[8,128]{1,0:T(8,128)S(1)}) custom-call(s32[4]{0:T(128)S(1)} %pad_add_fusion.place, f32[5,512,128]{2,1,0:T(8,128)} %bitcast.9), custom_call_target="tpu_custom_call" | custom-call | flops 1000 | bytes 1000 | tf_op jit(solution)/shard_map/pallas_call | solution.py:644
  3.8 1.5 %collective-permute-start = (f32[488,128]{1,0:T(8,128)S(1)}, f32[488,128]{1,0:T(8,128)S(1)}, u32[]{:S(2)}, u32[]{:S(2)}) collective-permute-start(f32[488,128]{1,0:T(8,128)S(1)} %get-tuple-element.17), channel_id=1, source_target_pairs={{0,1},{1,0},{2,3},{3,2},{4,8},{5,9},{6,10},{7,11},{8,4},{9,5},{10,... | collective-permute-start | bytes 749576 | tf_op jit(solution)/shard_map/ppermute | solution.py:666
  5.3 2.0 %collective-permute-start.1 = (f32[488,128]{1,0:T(8,128)S(1)}, f32[488,128]{1,0:T(8,128)S(1)}, u32[]{:S(2)}, u32[]{:S(2)}) collective-permute-start(f32[488,128]{1,0:T(8,128)S(1)} %get-tuple-element.18), channel_id=1, source_target_pairs={{0,4},{1,5},{2,6},{3,7},{4,0},{5,1},{6,2},{7,3},{8,12},{9,13},{10,... | collective-permute-start | bytes 749576 | tf_op jit(solution)/shard_map/ppermute | solution.py:666
  7.3 10.5 %all-to-all-start = ((f32[128,1,384]{2,1,0:T(1,128)}), f32[128,1,384]{2,1,0:T(1,128)S(1)}, u32[]{:S(2)}, u32[]{:S(2)}) async-start(f32[128,1,384]{2,1,0:T(1,128)} %bitcast.7), calls=%async_computation | async-start | bytes 393216 | tf_op jit(solution)/shard_map/all_to_all | solution.py:676
  17.8 1.1 %collective-permute-start.2 = (f32[240,128]{1,0:T(8,128)S(1)}, f32[240,128]{1,0:T(8,128)S(1)}, u32[]{:S(2)}, u32[]{:S(2)}) collective-permute-start(f32[240,128]{1,0:T(8,128)S(1)} %get-tuple-element.19), channel_id=1, source_target_pairs={{0,1},{1,0},{2,3},{3,2},{4,5},{5,4},{6,7},{7,6},{8,9},{9,8},{10,11... | collective-permute-start | bytes 368648 | tf_op jit(solution)/shard_map/ppermute | solution.py:666
  18.9 0.7 %collective-permute-start.3 = (f32[240,128]{1,0:T(8,128)S(1)}, f32[240,128]{1,0:T(8,128)S(1)}, u32[]{:S(2)}, u32[]{:S(2)}) collective-permute-start(f32[240,128]{1,0:T(8,128)S(1)} %get-tuple-element.20), channel_id=1, source_target_pairs={{0,3},{1,2},{2,1},{3,0},{4,7},{5,6},{6,5},{7,4},{8,11},{9,10},{10,... | collective-permute-start | bytes 368648 | tf_op jit(solution)/shard_map/ppermute | solution.py:666
  19.7 0.0 copy-done
  19.7 6.4 %shard_map.60 = (f32[2560,128]{1,0:T(8,128)S(1)}, s32[32,128]{1,0:T(8,128)S(1)}, s32[64,128]{1,0:T(8,128)S(1)}) custom-call(s32[4]{0:T(128)S(1)} %pad_add_fusion.place, f32[2560,128]{1,0:T(8,128)S(1)} %bitcast.10, s32[128,32]{1,0:T(8,128)} %bitcast.14, s32[8,16]{1,0:T(8,128)} %bitcast.16, s32[16,32]{1,0:T(8,128)} %bitcast.15), custom_call_target="tpu_custom_call" | custom-call | flops 1000 | bytes 1000 | tf_op jit(solution)/shard_map/pallas_call | solution.py:644
  26.1 0.0 collective-permute-done.2.y_one
  26.1 0.0 collective-permute-done.3.y_two
  26.1 0.0 collective-permute-done.x_one
  26.1 0.0 collective-permute-done.1.x_two
  26.1 2.3 %shard_map.61 = (f32[2560,128]{1,0:T(8,128)S(1)}, f32[16,128]{1,0:T(8,128)S(1)}) custom-call(s32[4]{0:T(128)S(1)} %pad_add_fusion.place, f32[2560,128]{1,0:T(8,128)S(1)} %bitcast.11, f32[2560,128]{1,0:T(8,128)S(1)} %get-tuple-element.16.inner, f32[488,128]{1,0:T(8,128)S(1)} %collective-permute-done.x_one, f32[488,128]{1,0:T(8,128)S(1)} %collective-permute-done.1.x_two, ...), custom_call_target="tpu_custom_call" | custom-call | flops 1000 | bytes 1000 | tf_op jit(solution)/shard_map/pallas_call | solution.py:644
  28.4 0.0 all-to-all-done
  28.5 3.1 %shard_map.62 = (f32[5,16,32,128]{3,2,1,0:T(8,128)}, f32[3,16,32,128]{3,2,1,0:T(8,128)}) custom-call(s32[4]{0:T(128)S(1)} %pad_add_fusion.place, f32[2560,128]{1,0:T(8,128)S(1)} %bitcast.12, f32[2560,128]{1,0:T(8,128)S(1)} %get-tuple-element.21.twice, s32[32,128]{1,0:T(8,128)S(1)} %get-tuple-element.22.uses_fine, ...), custom_call_target="tpu_custom_call" | custom-call | flops 1000 | bytes 1000 | tf_op jit(solution)/shard_map/pallas_call | solution.py:644
Async XLA Ops:
  0.6 19.0 %copy-start = (f32[5,16,32,128]{3,2,1,0:T(8,128)S(1)}, f32[5,16,32,128]{3,2,1,0:T(8,128)}, u32[]{:S(2)}) copy-start(f32[5,16,32,128]{3,2,1,0:T(8,128)} %param.4) | copy-start | bytes 3932164
  3.8 22.3 %collective-permute-start = (f32[488,128]{1,0:T(8,128)S(1)}, f32[488,128]{1,0:T(8,128)S(1)}, u32[]{:S(2)}, u32[]{:S(2)}) collective-permute-start(f32[488,128]{1,0:T(8,128)S(1)} %get-tuple-element.17), channel_id=1, source_target_pairs={{0,1},{1,0},{2,3},{3,2},{4,8},{5,9},{6,10},{7,11},{8,4},{9,5},{10,... | collective-permute-start | bytes 749576 | tf_op jit(solution)/shard_map/ppermute | solution.py:666
  5.3 20.8 %collective-permute-start.1 = (f32[488,128]{1,0:T(8,128)S(1)}, f32[488,128]{1,0:T(8,128)S(1)}, u32[]{:S(2)}, u32[]{:S(2)}) collective-permute-start(f32[488,128]{1,0:T(8,128)S(1)} %get-tuple-element.18), channel_id=1, source_target_pairs={{0,4},{1,5},{2,6},{3,7},{4,0},{5,1},{6,2},{7,3},{8,12},{9,13},{10,... | collective-permute-start | bytes 749576 | tf_op jit(solution)/shard_map/ppermute | solution.py:666
  7.3 21.2 %all-to-all-start = ((f32[128,1,384]{2,1,0:T(1,128)}), f32[128,1,384]{2,1,0:T(1,128)S(1)}, u32[]{:S(2)}, u32[]{:S(2)}) async-start(f32[128,1,384]{2,1,0:T(1,128)} %bitcast.7), calls=%async_computation | async-start | bytes 393216 | tf_op jit(solution)/shard_map/all_to_all | solution.py:676
  17.8 8.3 %collective-permute-start.2 = (f32[240,128]{1,0:T(8,128)S(1)}, f32[240,128]{1,0:T(8,128)S(1)}, u32[]{:S(2)}, u32[]{:S(2)}) collective-permute-start(f32[240,128]{1,0:T(8,128)S(1)} %get-tuple-element.19), channel_id=1, source_target_pairs={{0,1},{1,0},{2,3},{3,2},{4,5},{5,4},{6,7},{7,6},{8,9},{9,8},{10,11... | collective-permute-start | bytes 368648 | tf_op jit(solution)/shard_map/ppermute | solution.py:666
  18.9 7.2 %collective-permute-start.3 = (f32[240,128]{1,0:T(8,128)S(1)}, f32[240,128]{1,0:T(8,128)S(1)}, u32[]{:S(2)}, u32[]{:S(2)}) collective-permute-start(f32[240,128]{1,0:T(8,128)S(1)} %get-tuple-element.20), channel_id=1, source_target_pairs={{0,3},{1,2},{2,1},{3,0},{4,7},{5,6},{6,5},{7,4},{8,11},{9,10},{10,... | collective-permute-start | bytes 368648 | tf_op jit(solution)/shard_map/ppermute | solution.py:666

commit v7 on v6

--- a/solution.py
+++ b/solution.py
@@ -45,14 +45,19 @@
     return square * lax.rsqrt(square)
 
 
+def here():
+    return [of(axis) for of in (lax.axis_index, lax.axis_size) for axis in AXES]
+
+
 def fold_rows(values, group):
     keep = iota(values.shape, 1) // group == iota(values.shape, 0)
     return jnp.sum(jnp.where(keep, values, 0.0), axis=0, keepdims=True)
 
 
 def moments_kernel(
-    place, state, sent, x_one, x_two, y_one, y_two, own, rows, arrived
+    state, sent, x_one, x_two, y_one, y_two, own, rows, arrived
 ):
+    place = here()
     part = ROWS // 4
     copies = [
         pltpu.make_async_copy(
@@ -207,10 +212,11 @@
 
 
 def inner_kernel(
-    place, state, far_pairs, far_count, far_coarse, out, fine_uses, coarse_uses,
+    state, far_pairs, far_count, far_coarse, out, fine_uses, coarse_uses,
     turned_even, turned_odd, changes_even, changes_odd, padded, inverse_of, sound, by_y,
     fine_pairs, fine_count, coarse_pairs, arrived,
 ):
+    place = here()
     turned, changes = (turned_even, turned_odd), (changes_even, changes_odd)
 
     def turn(block, f):
@@ -477,9 +483,10 @@
 
 
 def edge_kernel(
-    place, state, inner, x_one, x_two, y_one, y_two, out, beside,
+    state, inner, x_one, x_two, y_one, y_two, out, beside,
     x_low, x_high, y_low, y_high, rims, by_x, by_y,
 ):
+    place = here()
     sides(x_two, x_one, x_low, x_high, place[0])
     even = place[0] % 2 == 0
     moments = x_one[480:488, :], x_two[480:488, :]
@@ -577,8 +584,9 @@
 
 
 def update_kernel(
-    place, state, twice, uses_fine, uses_coarse, got, own, beside, new, gravity, around, field, made, pulls, written
+    state, twice, uses_fine, uses_coarse, got, own, beside, new, gravity, around, field, made, pulls, written
 ):
+    place = here()
     result, time_step = far_fields(place, uses_fine, uses_coarse, got, own, beside, around)
     half_step = 0.5 * time_step
     source = iota((8, 128), 0) * 16 + iota((8, 128), 1) // 8
@@ -629,7 +637,6 @@
 
 
 VMEM = pl.BlockSpec(memory_space=pltpu.VMEM)
-SMEM = pl.BlockSpec(memory_space=pltpu.SMEM)
 FAR = pl.BlockSpec(memory_space=pltpu.HBM)
 LIMIT = pltpu.CompilerParams(vmem_limit_bytes=12 * 1024 * 1024)
 SMALL = pl.CostEstimate(flops=1000, bytes_accessed=1000, transcendentals=0)
@@ -647,7 +654,7 @@
             pltpu.HBM(s, F32) if n in far_outs else jax.ShapeDtypeStruct(s, jnp.int32 if n in whole_numbers else F32)
             for n, s in enumerate(shapes)
         ],
-        in_specs=[SMEM] + (sources or [VMEM] * (len(args) - 1)),
+        in_specs=sources or [VMEM] * len(args),
         out_specs=[FAR if n in far_outs else VMEM for n in range(len(outs))],
         scratch_shapes=[pltpu.VMEM((s, 128), F32) if isinstance(s, int) else s for s in scratch],
         compiler_params=LIMIT,
@@ -657,12 +664,11 @@
 
 def local(state, fine_pairs, fine_count, coarse_pairs):
     mortons, octs = lax.axis_size("morton"), lax.axis_size("oct")
-    place = jnp.stack([lax.axis_index("morton"), lax.axis_index("oct"), mortons, octs]).astype(jnp.int32)
     many = NX * PITCH
 
     def swap(values, pair):
         pairs = [(m, o) for m in range(mortons) for o in range(octs)]
-        index = lambda place: place[0] * octs + place[1]
+        index = lambda at: at[0] * octs + at[1]
         return lax.ppermute(values, AXES, [(index(p), index(pair(*p))) for p in pairs])
 
     def other(i):
@@ -671,7 +677,7 @@
     block = pltpu.VMEM((5, ROWS, 128), F32)
     sent, x_one, x_two, y_one, y_two, own = call(
         moments_kernel, [128 * SENT, LONG, LONG, 240, 240, 8],
-        [block, pltpu.SemaphoreType.DMA((4,))], place, far(state.reshape(5, ROWS, 128)), sources=[FAR],
+        [block, pltpu.SemaphoreType.DMA((4,))], far(state.reshape(5, ROWS, 128)), sources=[FAR],
     )
     got = lax.all_to_all(sent.reshape(mortons * octs, 1, SENT * 128), AXES[::-1], 0, 0, tiled=True)
     x_one = swap(x_one, lambda m, o: (other(m), o) if 0 < m < mortons - 1 else (m, o ^ 1))
@@ -684,18 +690,18 @@
         inner_kernel, [5 * ROWS, 32, 64],
         [5 * TALL, 5 * TALL, 640, 640, 5 * many, many, many, 5 * many, pltpu.VMEM((128, 32), jnp.int32),
          pltpu.VMEM((8, 16), jnp.int32), pltpu.VMEM((16, 32), jnp.int32), pltpu.SemaphoreType.DMA((3,))],
-        place, rows, far(fine_pairs.reshape(128, 32)), far(fine_count.reshape(8, 16)), far(coarse_pairs.reshape(16, 32)),
+        rows, far(fine_pairs.reshape(128, 32)), far(fine_count.reshape(8, 16)), far(coarse_pairs.reshape(16, 32)),
         sources=[VMEM, FAR, FAR, FAR], whole_numbers=(1, 2),
     )
     rim = 5 * NX * RIM
     twice, beside = call(
         edge_kernel, [5 * ROWS, 16], [480, 480, 240, 240, rim, 960, rim],
-        place, rows, inner, x_one, x_two, y_one, y_two,
+        rows, inner, x_one, x_two, y_one, y_two,
     )
     return call(
         update_kernel, [(5, NX, NY, NZ), (3, NX, NY, NZ)],
         [160, 72, pltpu.VMEM((5, NX, NY, NZ), F32), pltpu.VMEM((3, NX, NY, NZ), F32), pltpu.SemaphoreType.DMA((2, 4))],
-        place, rows, twice, uses_fine, uses_coarse, got.reshape(mortons * octs * SENT, 128), own, beside,
+        rows, twice, uses_fine, uses_coarse, got.reshape(mortons * octs * SENT, 128), own, beside,
         far_outs=range(2),
     )
 

time: 31.7 us -> 30.6 us (0.965)
  Pallas kernels: 14.9 us -> 12.7 us
  waiting for transfers between devices: 0.02 us -> 1.16 us
    pallas_call x4, Pallas kernels: 14.9 us -> 12.7 us  [call(): pl.pallas_call(kernel, out_shape=[pltpu.HBM(s, F32) if n in far_outs else...]
    all_to_all x1, waiting for transfers between devices: 0.01 us -> 1.15 us  [local(): lax.all_to_all(sent.reshape(mortons * octs, 1, SENT * 128), AXES[::-1], 0...]
  transfers between devices with their start and end apart: 5 -> 5, of which waited for: 0 -> 1; matrix products, arithmetic and copies ran while one was open for 0% -> 0% of each run, Pallas kernels for 28% -> 25%
where the time goes in v7:
time: 30.6 us; the launch traced here: 30.4 us
  starting transfers between devices  15.9 us (52%)
  Pallas kernels  12.7 us (42%)
  waiting for transfers between devices  1.16 us (4%)
  between operations  0.7 us (2%)
    pallas_call x4, Pallas kernels, call(): pl.pallas_call(kernel, out_shape=[pltpu.HBM(s, F32) if n in far_outs else...  12.7 us
    all_to_all x1, starting transfers between devices, local(): lax.all_to_all(sent.reshape(mortons * octs, 1, SENT * 128), AXES[::-1], 0...  10.5 us
    ppermute x4, starting transfers between devices, swap(): lax.ppermute(values, AXES, [(index(p), index(pair(*p))) for p in pairs])  5.38 us
    all_to_all x1, waiting for transfers between devices, local(): lax.all_to_all(sent.reshape(mortons * octs, 1, SENT * 128), AXES[::-1], 0...  1.15 us
  transfers between devices with their start and end apart: 5, of which 1 were waited for; matrix products, arithmetic and copies ran while one was open for 0% of the time, Pallas kernels for 25%

profile of v7, /device:TPU:1, one launch (start us, length us, event | category | flops | bytes accessed | tf_op | source)
XLA Modules:
  0.0 30.4 jit_solution(10738041424436920220)
XLA Ops:
  0.6 0.0 copy-start
  0.6 2.6 %shard_map.59 = (f32[384,128]{1,0:T(8,128)}, f32[488,128]{1,0:T(8,128)S(1)}, f32[488,128]{1,0:T(8,128)S(1)}, f32[240,128]{1,0:T(8,128)S(1)}, f32[240,128]{1,0:T(8,128)S(1)}, /*index=5*/f32[8,128]{1,0:T(8,128)S(1)}) custom-call(f32[5,512,128]{2,1,0:T(8,128)} %bitcast.7), custom_call_target="tpu_custom_call" | custom-call | flops 1000 | bytes 1000 | tf_op jit(solution)/shard_map/pallas_call | solution.py:651
  3.3 1.5 %collective-permute-start = (f32[488,128]{1,0:T(8,128)S(1)}, f32[488,128]{1,0:T(8,128)S(1)}, u32[]{:S(2)}, u32[]{:S(2)}) collective-permute-start(f32[488,128]{1,0:T(8,128)S(1)} %get-tuple-element.17), channel_id=1, source_target_pairs={{0,1},{1,0},{2,3},{3,2},{4,8},{5,9},{6,10},{7,11},{8,4},{9,5},{10,... | collective-permute-start | bytes 749576 | tf_op jit(solution)/shard_map/ppermute | solution.py:672
  4.8 2.0 %collective-permute-start.1 = (f32[488,128]{1,0:T(8,128)S(1)}, f32[488,128]{1,0:T(8,128)S(1)}, u32[]{:S(2)}, u32[]{:S(2)}) collective-permute-start(f32[488,128]{1,0:T(8,128)S(1)} %get-tuple-element.18), channel_id=1, source_target_pairs={{0,4},{1,5},{2,6},{3,7},{4,0},{5,1},{6,2},{7,3},{8,12},{9,13},{10,... | collective-permute-start | bytes 749576 | tf_op jit(solution)/shard_map/ppermute | solution.py:672
  6.8 10.5 %all-to-all-start = ((f32[128,1,384]{2,1,0:T(1,128)}), f32[128,1,384]{2,1,0:T(1,128)S(1)}, u32[]{:S(2)}, u32[]{:S(2)}) async-start(f32[128,1,384]{2,1,0:T(1,128)} %bitcast.5), calls=%async_computation | async-start | bytes 393216 | tf_op jit(solution)/shard_map/all_to_all | solution.py:682
  17.3 1.1 %collective-permute-start.2 = (f32[240,128]{1,0:T(8,128)S(1)}, f32[240,128]{1,0:T(8,128)S(1)}, u32[]{:S(2)}, u32[]{:S(2)}) collective-permute-start(f32[240,128]{1,0:T(8,128)S(1)} %get-tuple-element.19), channel_id=1, source_target_pairs={{0,1},{1,0},{2,3},{3,2},{4,5},{5,4},{6,7},{7,6},{8,9},{9,8},{10,11... | collective-permute-start | bytes 368648 | tf_op jit(solution)/shard_map/ppermute | solution.py:672
  18.4 0.7 %collective-permute-start.3 = (f32[240,128]{1,0:T(8,128)S(1)}, f32[240,128]{1,0:T(8,128)S(1)}, u32[]{:S(2)}, u32[]{:S(2)}) collective-permute-start(f32[240,128]{1,0:T(8,128)S(1)} %get-tuple-element.20), channel_id=1, source_target_pairs={{0,3},{1,2},{2,1},{3,0},{4,7},{5,6},{6,5},{7,4},{8,11},{9,10},{10,... | collective-permute-start | bytes 368648 | tf_op jit(solution)/shard_map/ppermute | solution.py:672
  19.1 0.0 copy-done
  19.1 5.9 %shard_map.60 = (f32[2560,128]{1,0:T(8,128)S(1)}, s32[32,128]{1,0:T(8,128)S(1)}, s32[64,128]{1,0:T(8,128)S(1)}) custom-call(f32[2560,128]{1,0:T(8,128)S(1)} %bitcast.8, s32[128,32]{1,0:T(8,128)} %bitcast.12, s32[8,16]{1,0:T(8,128)} %bitcast.14, s32[16,32]{1,0:T(8,128)} %bitcast.13), custom_call_target="tpu_custom_call" | custom-call | flops 1000 | bytes 1000 | tf_op jit(solution)/shard_map/pallas_call | solution.py:651
  25.0 0.0 collective-permute-done.2.y_one
  25.0 0.0 collective-permute-done.3.y_two
  25.0 0.0 collective-permute-done.x_one
  25.0 0.0 collective-permute-done.1.x_two
  25.0 1.7 %shard_map.61 = (f32[2560,128]{1,0:T(8,128)S(1)}, f32[16,128]{1,0:T(8,128)S(1)}) custom-call(f32[2560,128]{1,0:T(8,128)S(1)} %bitcast.9, f32[2560,128]{1,0:T(8,128)S(1)} %get-tuple-element.16.inner, f32[488,128]{1,0:T(8,128)S(1)} %collective-permute-done.x_one, f32[488,128]{1,0:T(8,128)S(1)} %collective-permute-done.1.x_two, ...), custom_call_target="tpu_custom_call" | custom-call | flops 1000 | bytes 1000 | tf_op jit(solution)/shard_map/pallas_call | solution.py:651
  26.8 1.1 %all-to-all-done = f32[128,1,384]{2,1,0:T(1,128)S(1)} async-done(((f32[128,1,384]{2,1,0:T(1,128)}), f32[128,1,384]{2,1,0:T(1,128)S(1)}, u32[]{:S(2)}, u32[]{:S(2)}) %all-to-all-start) | async-done | bytes 196640 | tf_op jit(solution)/shard_map/all_to_all | solution.py:682
  27.9 2.5 %shard_map.62 = (f32[5,16,32,128]{3,2,1,0:T(8,128)}, f32[3,16,32,128]{3,2,1,0:T(8,128)}) custom-call(f32[2560,128]{1,0:T(8,128)S(1)} %bitcast.10, f32[2560,128]{1,0:T(8,128)S(1)} %get-tuple-element.21.twice, s32[32,128]{1,0:T(8,128)S(1)} %get-tuple-element.22.uses_fine, s32[64,128]{1,0:T(8,128)S(1)} %get-tuple-element.23.uses_coarse, ...), custom_call_target="tpu_custom_call" | custom-call | flops 1000 | bytes 1000 | tf_op jit(solution)/shard_map/pallas_call | solution.py:651
Async XLA Ops:
  0.6 18.5 %copy-start = (f32[5,16,32,128]{3,2,1,0:T(8,128)S(1)}, f32[5,16,32,128]{3,2,1,0:T(8,128)}, u32[]{:S(2)}) copy-start(f32[5,16,32,128]{3,2,1,0:T(8,128)} %param.4) | copy-start | bytes 3932164
  3.3 21.8 %collective-permute-start = (f32[488,128]{1,0:T(8,128)S(1)}, f32[488,128]{1,0:T(8,128)S(1)}, u32[]{:S(2)}, u32[]{:S(2)}) collective-permute-start(f32[488,128]{1,0:T(8,128)S(1)} %get-tuple-element.17), channel_id=1, source_target_pairs={{0,1},{1,0},{2,3},{3,2},{4,8},{5,9},{6,10},{7,11},{8,4},{9,5},{10,... | collective-permute-start | bytes 749576 | tf_op jit(solution)/shard_map/ppermute | solution.py:672
  4.8 20.3 %collective-permute-start.1 = (f32[488,128]{1,0:T(8,128)S(1)}, f32[488,128]{1,0:T(8,128)S(1)}, u32[]{:S(2)}, u32[]{:S(2)}) collective-permute-start(f32[488,128]{1,0:T(8,128)S(1)} %get-tuple-element.18), channel_id=1, source_target_pairs={{0,4},{1,5},{2,6},{3,7},{4,0},{5,1},{6,2},{7,3},{8,12},{9,13},{10,... | collective-permute-start | bytes 749576 | tf_op jit(solution)/shard_map/ppermute | solution.py:672
  6.8 21.2 %all-to-all-start = ((f32[128,1,384]{2,1,0:T(1,128)}), f32[128,1,384]{2,1,0:T(1,128)S(1)}, u32[]{:S(2)}, u32[]{:S(2)}) async-start(f32[128,1,384]{2,1,0:T(1,128)} %bitcast.5), calls=%async_computation | async-start | bytes 393216 | tf_op jit(solution)/shard_map/all_to_all | solution.py:682
  17.3 7.7 %collective-permute-start.2 = (f32[240,128]{1,0:T(8,128)S(1)}, f32[240,128]{1,0:T(8,128)S(1)}, u32[]{:S(2)}, u32[]{:S(2)}) collective-permute-start(f32[240,128]{1,0:T(8,128)S(1)} %get-tuple-element.19), channel_id=1, source_target_pairs={{0,1},{1,0},{2,3},{3,2},{4,5},{5,4},{6,7},{7,6},{8,9},{9,8},{10,11... | collective-permute-start | bytes 368648 | tf_op jit(solution)/shard_map/ppermute | solution.py:672
  18.4 6.6 %collective-permute-start.3 = (f32[240,128]{1,0:T(8,128)S(1)}, f32[240,128]{1,0:T(8,128)S(1)}, u32[]{:S(2)}, u32[]{:S(2)}) collective-permute-start(f32[240,128]{1,0:T(8,128)S(1)} %get-tuple-element.20), channel_id=1, source_target_pairs={{0,3},{1,2},{2,1},{3,0},{4,7},{5,6},{6,5},{7,4},{8,11},{9,10},{10,... | collective-permute-start | bytes 368648 | tf_op jit(solution)/shard_map/ppermute | solution.py:672

commit v8 on v7

--- a/solution.py
+++ b/solution.py
@@ -58,12 +58,12 @@
     state, sent, x_one, x_two, y_one, y_two, own, rows, arrived
 ):
     place = here()
-    part = ROWS // 4
+    part = ROWS // 8
     copies = [
         pltpu.make_async_copy(
             state.at[:, pl.ds(c * part, part), :], rows.at[:, pl.ds(c * part, part), :], arrived.at[c]
         )
-        for c in range(4)
+        for c in range(8)
     ]
     even, oct_even = place[0] % 2 == 0, place[1] % 2 == 0
     x_starts = (jnp.where(even, 0, NX - 3), jnp.where(even, NX - 3, 0))
@@ -75,9 +75,9 @@
     sums, sums_x, sums_y = [], [], []
     for tx in range(2):
         totals, totals_x = [jnp.zeros((8, 128), F32)] * 4, [jnp.zeros((8, 128), F32)] * 4
-        for half in range(2):
-            copies[tx * 2 + half].wait()
-            for x in range(half * 4, half * 4 + 4):
+        for half in range(4):
+            copies[tx * 4 + half].wait()
+            for x in range(half * 2, half * 2 + 2):
                 for ty in range(4):
                     row = (tx * 8 + x) * NY + ty * 8
                     q = [rows[f, row : row + 8, :] for f in range(5)]
@@ -601,7 +601,7 @@
     offset_y = iota((8, 128), 0).astype(F32) - 3.5
 
     def writes(part):
-        rows = pl.ds(part * 4, 4)
+        rows = pl.ds(part * 2, 2)
         return [
             pltpu.make_async_copy(made.at[:, rows, :, :], new.at[:, rows, :, :], written.at[0, part]),
             pltpu.make_async_copy(pulls.at[:, rows, :, :], gravity.at[:, rows, :, :], written.at[1, part]),
@@ -628,10 +628,10 @@
                 pulls[e, x, y : y + 8, :] = pull[e]
                 made[1 + e, x, y : y + 8, :] = moved[1 + e] + weight * pull[e]
             made[4, x, y : y + 8, :] = moved[4] + time_step * gain
-        if x % 4 == 3:
-            for copy in writes(x // 4):
+        if x % 2 == 1:
+            for copy in writes(x // 2):
                 copy.start()
-    for part in range(4):
+    for part in range(8):
         for copy in writes(part):
             copy.wait()
 
@@ -677,7 +677,7 @@
     block = pltpu.VMEM((5, ROWS, 128), F32)
     sent, x_one, x_two, y_one, y_two, own = call(
         moments_kernel, [128 * SENT, LONG, LONG, 240, 240, 8],
-        [block, pltpu.SemaphoreType.DMA((4,))], far(state.reshape(5, ROWS, 128)), sources=[FAR],
+        [block, pltpu.SemaphoreType.DMA((8,))], far(state.reshape(5, ROWS, 128)), sources=[FAR],
     )
     got = lax.all_to_all(sent.reshape(mortons * octs, 1, SENT * 128), AXES[::-1], 0, 0, tiled=True)
     x_one = swap(x_one, lambda m, o: (other(m), o) if 0 < m < mortons - 1 else (m, o ^ 1))
@@ -700,7 +700,7 @@
     )
     return call(
         update_kernel, [(5, NX, NY, NZ), (3, NX, NY, NZ)],
-        [160, 72, pltpu.VMEM((5, NX, NY, NZ), F32), pltpu.VMEM((3, NX, NY, NZ), F32), pltpu.SemaphoreType.DMA((2, 4))],
+        [160, 72, pltpu.VMEM((5, NX, NY, NZ), F32), pltpu.VMEM((3, NX, NY, NZ), F32), pltpu.SemaphoreType.DMA((2, 8))],
         rows, twice, uses_fine, uses_coarse, got.reshape(mortons * octs * SENT, 128), own, beside,
         far_outs=range(2),
     )

time: 30.6 us -> 30.8 us (level)
  no operation moved by 1% of the time
where the time goes in v8:
time: 30.8 us; the launch traced here: 30.6 us
  starting transfers between devices  15.9 us (52%)
  Pallas kernels  12.9 us (42%)
  waiting for transfers between devices  1.16 us (4%)
  between operations  0.7 us (2%)
    pallas_call x4, Pallas kernels, call(): pl.pallas_call(kernel, out_shape=[pltpu.HBM(s, F32) if n in far_outs else...  12.9 us
    all_to_all x1, starting transfers between devices, local(): lax.all_to_all(sent.reshape(mortons * octs, 1, SENT * 128), AXES[::-1], 0...  10.5 us
    ppermute x4, starting transfers between devices, swap(): lax.ppermute(values, AXES, [(index(p), index(pair(*p))) for p in pairs])  5.38 us
    all_to_all x1, waiting for transfers between devices, local(): lax.all_to_all(sent.reshape(mortons * octs, 1, SENT * 128), AXES[::-1], 0...  1.15 us
  transfers between devices with their start and end apart: 5, of which 1 were waited for; matrix products, arithmetic and copies ran while one was open for 0% of the time, Pallas kernels for 25%

profile of v8, /device:TPU:1, one launch (start us, length us, event | category | flops | bytes accessed | tf_op | source)
XLA Modules:
  0.0 30.6 jit_solution(47306259567535313)
XLA Ops:
  0.6 0.0 copy-start
  0.6 2.8 %shard_map.59 = (f32[384,128]{1,0:T(8,128)}, f32[488,128]{1,0:T(8,128)S(1)}, f32[488,128]{1,0:T(8,128)S(1)}, f32[240,128]{1,0:T(8,128)S(1)}, f32[240,128]{1,0:T(8,128)S(1)}, /*index=5*/f32[8,128]{1,0:T(8,128)S(1)}) custom-call(f32[5,512,128]{2,1,0:T(8,128)} %bitcast.7), custom_call_target="tpu_custom_call" | custom-call | flops 1000 | bytes 1000 | tf_op jit(solution)/shard_map/pallas_call | solution.py:651
  3.4 1.5 %collective-permute-start = (f32[488,128]{1,0:T(8,128)S(1)}, f32[488,128]{1,0:T(8,128)S(1)}, u32[]{:S(2)}, u32[]{:S(2)}) collective-permute-start(f32[488,128]{1,0:T(8,128)S(1)} %get-tuple-element.17), channel_id=1, source_target_pairs={{0,1},{1,0},{2,3},{3,2},{4,8},{5,9},{6,10},{7,11},{8,4},{9,5},{10,... | collective-permute-start | bytes 749576 | tf_op jit(solution)/shard_map/ppermute | solution.py:672
  4.9 2.0 %collective-permute-start.1 = (f32[488,128]{1,0:T(8,128)S(1)}, f32[488,128]{1,0:T(8,128)S(1)}, u32[]{:S(2)}, u32[]{:S(2)}) collective-permute-start(f32[488,128]{1,0:T(8,128)S(1)} %get-tuple-element.18), channel_id=1, source_target_pairs={{0,4},{1,5},{2,6},{3,7},{4,0},{5,1},{6,2},{7,3},{8,12},{9,13},{10,... | collective-permute-start | bytes 749576 | tf_op jit(solution)/shard_map/ppermute | solution.py:672
  6.9 10.5 %all-to-all-start = ((f32[128,1,384]{2,1,0:T(1,128)}), f32[128,1,384]{2,1,0:T(1,128)S(1)}, u32[]{:S(2)}, u32[]{:S(2)}) async-start(f32[128,1,384]{2,1,0:T(1,128)} %bitcast.5), calls=%async_computation | async-start | bytes 393216 | tf_op jit(solution)/shard_map/all_to_all | solution.py:682
  17.4 1.1 %collective-permute-start.2 = (f32[240,128]{1,0:T(8,128)S(1)}, f32[240,128]{1,0:T(8,128)S(1)}, u32[]{:S(2)}, u32[]{:S(2)}) collective-permute-start(f32[240,128]{1,0:T(8,128)S(1)} %get-tuple-element.19), channel_id=1, source_target_pairs={{0,1},{1,0},{2,3},{3,2},{4,5},{5,4},{6,7},{7,6},{8,9},{9,8},{10,11... | collective-permute-start | bytes 368648 | tf_op jit(solution)/shard_map/ppermute | solution.py:672
  18.6 0.7 %collective-permute-start.3 = (f32[240,128]{1,0:T(8,128)S(1)}, f32[240,128]{1,0:T(8,128)S(1)}, u32[]{:S(2)}, u32[]{:S(2)}) collective-permute-start(f32[240,128]{1,0:T(8,128)S(1)} %get-tuple-element.20), channel_id=1, source_target_pairs={{0,3},{1,2},{2,1},{3,0},{4,7},{5,6},{6,5},{7,4},{8,11},{9,10},{10,... | collective-permute-start | bytes 368648 | tf_op jit(solution)/shard_map/ppermute | solution.py:672
  19.3 0.0 copy-done
  19.3 5.9 %shard_map.60 = (f32[2560,128]{1,0:T(8,128)S(1)}, s32[32,128]{1,0:T(8,128)S(1)}, s32[64,128]{1,0:T(8,128)S(1)}) custom-call(f32[2560,128]{1,0:T(8,128)S(1)} %bitcast.8, s32[128,32]{1,0:T(8,128)} %bitcast.12, s32[8,16]{1,0:T(8,128)} %bitcast.14, s32[16,32]{1,0:T(8,128)} %bitcast.13), custom_call_target="tpu_custom_call" | custom-call | flops 1000 | bytes 1000 | tf_op jit(solution)/shard_map/pallas_call | solution.py:651
  25.1 0.0 collective-permute-done.2.y_one
  25.2 0.0 collective-permute-done.3.y_two
  25.2 0.0 collective-permute-done.x_one
  25.2 0.0 collective-permute-done.1.x_two
  25.2 1.7 %shard_map.61 = (f32[2560,128]{1,0:T(8,128)S(1)}, f32[16,128]{1,0:T(8,128)S(1)}) custom-call(f32[2560,128]{1,0:T(8,128)S(1)} %bitcast.9, f32[2560,128]{1,0:T(8,128)S(1)} %get-tuple-element.16.inner, f32[488,128]{1,0:T(8,128)S(1)} %collective-permute-done.x_one, f32[488,128]{1,0:T(8,128)S(1)} %collective-permute-done.1.x_two, ...), custom_call_target="tpu_custom_call" | custom-call | flops 1000 | bytes 1000 | tf_op jit(solution)/shard_map/pallas_call | solution.py:651
  26.9 1.1 %all-to-all-done = f32[128,1,384]{2,1,0:T(1,128)S(1)} async-done(((f32[128,1,384]{2,1,0:T(1,128)}), f32[128,1,384]{2,1,0:T(1,128)S(1)}, u32[]{:S(2)}, u32[]{:S(2)}) %all-to-all-start) | async-done | bytes 196640 | tf_op jit(solution)/shard_map/all_to_all | solution.py:682
  28.1 2.6 %shard_map.62 = (f32[5,16,32,128]{3,2,1,0:T(8,128)}, f32[3,16,32,128]{3,2,1,0:T(8,128)}) custom-call(f32[2560,128]{1,0:T(8,128)S(1)} %bitcast.10, f32[2560,128]{1,0:T(8,128)S(1)} %get-tuple-element.21.twice, s32[32,128]{1,0:T(8,128)S(1)} %get-tuple-element.22.uses_fine, s32[64,128]{1,0:T(8,128)S(1)} %get-tuple-element.23.uses_coarse, ...), custom_call_target="tpu_custom_call" | custom-call | flops 1000 | bytes 1000 | tf_op jit(solution)/shard_map/pallas_call | solution.py:651
Async XLA Ops:
  0.6 18.7 %copy-start = (f32[5,16,32,128]{3,2,1,0:T(8,128)S(1)}, f32[5,16,32,128]{3,2,1,0:T(8,128)}, u32[]{:S(2)}) copy-start(f32[5,16,32,128]{3,2,1,0:T(8,128)} %param.4) | copy-start | bytes 3932164
  3.4 21.8 %collective-permute-start = (f32[488,128]{1,0:T(8,128)S(1)}, f32[488,128]{1,0:T(8,128)S(1)}, u32[]{:S(2)}, u32[]{:S(2)}) collective-permute-start(f32[488,128]{1,0:T(8,128)S(1)} %get-tuple-element.17), channel_id=1, source_target_pairs={{0,1},{1,0},{2,3},{3,2},{4,8},{5,9},{6,10},{7,11},{8,4},{9,5},{10,... | collective-permute-start | bytes 749576 | tf_op jit(solution)/shard_map/ppermute | solution.py:672
  4.9 20.3 %collective-permute-start.1 = (f32[488,128]{1,0:T(8,128)S(1)}, f32[488,128]{1,0:T(8,128)S(1)}, u32[]{:S(2)}, u32[]{:S(2)}) collective-permute-start(f32[488,128]{1,0:T(8,128)S(1)} %get-tuple-element.18), channel_id=1, source_target_pairs={{0,4},{1,5},{2,6},{3,7},{4,0},{5,1},{6,2},{7,3},{8,12},{9,13},{10,... | collective-permute-start | bytes 749576 | tf_op jit(solution)/shard_map/ppermute | solution.py:672
  6.9 21.2 %all-to-all-start = ((f32[128,1,384]{2,1,0:T(1,128)}), f32[128,1,384]{2,1,0:T(1,128)S(1)}, u32[]{:S(2)}, u32[]{:S(2)}) async-start(f32[128,1,384]{2,1,0:T(1,128)} %bitcast.5), calls=%async_computation | async-start | bytes 393216 | tf_op jit(solution)/shard_map/all_to_all | solution.py:682
  17.4 7.7 %collective-permute-start.2 = (f32[240,128]{1,0:T(8,128)S(1)}, f32[240,128]{1,0:T(8,128)S(1)}, u32[]{:S(2)}, u32[]{:S(2)}) collective-permute-start(f32[240,128]{1,0:T(8,128)S(1)} %get-tuple-element.19), channel_id=1, source_target_pairs={{0,1},{1,0},{2,3},{3,2},{4,5},{5,4},{6,7},{7,6},{8,9},{9,8},{10,11... | collective-permute-start | bytes 368648 | tf_op jit(solution)/shard_map/ppermute | solution.py:672
  18.6 6.6 %collective-permute-start.3 = (f32[240,128]{1,0:T(8,128)S(1)}, f32[240,128]{1,0:T(8,128)S(1)}, u32[]{:S(2)}, u32[]{:S(2)}) collective-permute-start(f32[240,128]{1,0:T(8,128)S(1)} %get-tuple-element.20), channel_id=1, source_target_pairs={{0,3},{1,2},{2,1},{3,0},{4,7},{5,6},{6,5},{7,4},{8,11},{9,10},{10,... | collective-permute-start | bytes 368648 | tf_op jit(solution)/shard_map/ppermute | solution.py:672
